TPU v7x, 512 devices: a whole 4x8x8 slice. The times are simulated.
512 devices in a mesh: dp: 128 (over y_lo, x, z, core), tensor: 4 (over y_hi).
Axes of the slice: x: 4, y: 8 (y_hi: 4, y_lo: 2; y = y_hi * 2 + y_lo), z: 8, core: 2. Of those that a mesh axis runs over, the one named last changes fastest.
Arguments:
- image_pooled: bfloat16 [8192, 1152], P('dp'), may hold values from -64 to 64
- text_pooled: bfloat16 [8192, 1152], P('dp'), may hold values from -64 to 64
- image_norm_gain: float32 [1152], replicated, may hold values from 0.5 to 1.5
- image_norm_bias: float32 [1152], replicated, may hold values from -3 to 3
- image_up: bfloat16 [1152, 4304], P('dp', 'tensor'), may hold values from -0.1875 to 0.1875
- image_up_bias: float32 [4304], P('tensor'), may hold values from -3 to 3
- image_down: bfloat16 [4304, 1152], P('tensor', 'dp'), may hold values from -0.09375 to 0.09375
- image_down_bias: float32 [1152], replicated, may hold values from -2 to 2
- text_norm_gain: float32 [1152], replicated, may hold values from 0.5 to 1.5
- text_norm_bias: float32 [1152], replicated, may hold values from -2 to 2
- text_head: bfloat16 [1152, 1152], P('tensor'), may hold values from -0.25 to 1.25
- text_head_bias: float32 [1152], replicated, may hold values from -2 to 2
- log_scale: float32 [1], replicated, may hold values from 3.7 to 4.8
- logit_shift: float32 [1], replicated, may hold values from -14 to -8
- loss_scale: float32 [1], replicated, may hold values from 128 to 1024
Outputs:
- image_grad: float32 [8192, 1152], P('dp')
- text_grad: float32 [8192, 1152], P('dp')
All inputs are finite; a program needn't handle non-finite values.
Results may differ from a plain program's by a relative error of at most 0.019.
Values may be sent and summed in bfloat16 or wider, within the bound.
No kernel may reach another device: no remote copies, remote signals or barrier semaphores. Data moves between devices by JAX's collectives and lax.ppermute only.
A program may use at most 64 MiB of HBM per device.

v0:
```python
import jax
import jax.numpy as jnp
from jax import lax
from jax.sharding import PartitionSpec as P

epsilon = 1e-06
tanh_coef = 0.7978845608028654
cubic_coef = 0.044715


def gelu_parts(preact):
    inside = tanh_coef * (preact + cubic_coef * preact * preact * preact)
    tangent = jnp.tanh(inside)
    activated = 0.5 * preact * (1.0 + tangent)
    derivative = 0.5 * (1.0 + tangent) + 0.5 * preact * (1.0 - tangent * tangent) * tanh_coef * (
        1.0 + 3.0 * cubic_coef * preact * preact
    )
    return (activated, derivative)


def norm_forward(source, gain_vec, bias_vec):
    centre = source - jnp.mean(source, axis=1, keepdims=True)
    inverse = lax.rsqrt(jnp.mean(centre * centre, axis=1, keepdims=True) + epsilon)
    normed = centre * inverse
    return (normed * gain_vec + bias_vec, normed, inverse)


def norm_backward(upstream, normed, inverse, gain_vec):
    scaled = upstream * gain_vec
    return inverse * (
        scaled
        - jnp.mean(scaled, axis=1, keepdims=True)
        - normed * jnp.mean(scaled * normed, axis=1, keepdims=True)
    )


def unit_rows(partial_value, addend):
    row_count = partial_value.shape[0]
    quarter = row_count // lax.axis_size("tensor")
    first_row = lax.axis_index("tensor") * quarter
    row_whole = lax.psum(partial_value, "tensor") + addend
    inverse_whole = lax.rsqrt(jnp.sum(row_whole * row_whole, axis=1, keepdims=True) + epsilon)
    unit_whole = row_whole * inverse_whole
    travel_rows = lax.dynamic_slice_in_dim(unit_whole, first_row, quarter, 0).astype(jnp.bfloat16)
    return (unit_whole, inverse_whole, travel_rows)


def per_device(
    image_pooled,
    text_pooled,
    image_norm_gain,
    image_norm_bias,
    image_up,
    image_up_bias,
    image_down,
    image_down_bias,
    text_norm_gain,
    text_norm_bias,
    text_head,
    text_head_bias,
    log_scale,
    logit_shift,
    loss_scale,
):
    local_rows = image_pooled.shape[0]
    quarter = local_rows // lax.axis_size("tensor")
    tensor_rank = lax.axis_index("tensor")
    data_rank = lax.axis_index("dp")
    pairs_total = local_rows * lax.axis_size("dp")
    up_whole, down_whole = (
        lax.all_gather(image_up, "dp", axis=0, tiled=True),
        lax.all_gather(image_down, "dp", axis=1, tiled=True),
    )
    image_float = image_pooled.astype(jnp.float32)
    image_ready, image_normed, image_inverse = norm_forward(
        image_float, image_norm_gain, image_norm_bias
    )
    hidden_pre = (
        jnp.dot(image_ready.astype(jnp.bfloat16), up_whole, preferred_element_type=jnp.float32)
        + image_up_bias
    )
    hidden_act, hidden_slope = gelu_parts(hidden_pre)
    image_partial = jnp.dot(
        hidden_act.astype(jnp.bfloat16), down_whole, preferred_element_type=jnp.float32
    )
    image_unit, image_invnorm, image_travel = unit_rows(
        image_partial, image_float + image_down_bias
    )
    text_float = text_pooled.astype(jnp.float32)
    text_ready, text_normed, text_inverse = norm_forward(text_float, text_norm_gain, text_norm_bias)
    head_rows = text_head.shape[0]
    text_columns = lax.dynamic_slice_in_dim(
        text_ready.astype(jnp.bfloat16), tensor_rank * head_rows, head_rows, 1
    )
    text_partial = jnp.dot(text_columns, text_head, preferred_element_type=jnp.float32)
    text_unit, text_invnorm, text_travel = unit_rows(
        text_partial, jnp.broadcast_to(text_head_bias, text_partial.shape)
    )
    image_emb = image_unit.astype(jnp.bfloat16)
    text_emb = text_unit.astype(jnp.bfloat16)
    scale_value = jnp.exp(log_scale[0])
    factor = loss_scale[0] * scale_value / pairs_total
    own_ids = data_rank * local_rows + jnp.arange(local_rows, dtype=jnp.int32)

    def visitor_ids(piece_rows):
        position = jnp.arange(piece_rows, dtype=jnp.int32)
        return position // quarter * local_rows + tensor_rank * quarter + position % quarter

    def fold_toward(own_table, visiting):
        scores = lax.dot_general(
            own_table, visiting, (((1,), (1,)), ((), ())), preferred_element_type=jnp.float32
        )
        matches = (own_ids[:, None] == visitor_ids(visiting.shape[0])[None, :]).astype(jnp.float32)
        weights = (
            factor * (jax.nn.sigmoid(scale_value * scores + logit_shift[0]) - matches)
        ).astype(jnp.bfloat16)
        return jnp.dot(weights, visiting, preferred_element_type=jnp.float32)

    image_part = fold_toward(image_emb, lax.all_gather(text_travel, "dp", axis=0, tiled=True))
    text_part = fold_toward(text_emb, lax.all_gather(image_travel, "dp", axis=0, tiled=True))
    image_unit_back, text_unit_back = (
        lax.psum(image_part.astype(jnp.bfloat16), "tensor").astype(jnp.float32),
        lax.psum(text_part.astype(jnp.bfloat16), "tensor").astype(jnp.float32),
    )
    image_back = (
        image_unit_back - image_unit * jnp.sum(image_unit * image_unit_back, axis=1, keepdims=True)
    ) * image_invnorm
    hidden_back = lax.dot_general(
        image_back.astype(jnp.bfloat16),
        down_whole,
        (((1,), (1,)), ((), ())),
        preferred_element_type=jnp.float32,
    )
    pre_back = (hidden_back * hidden_slope).astype(jnp.bfloat16)
    ready_part = lax.dot_general(
        pre_back, up_whole, (((1,), (1,)), ((), ())), preferred_element_type=jnp.float32
    )
    ready_back = lax.psum(ready_part.astype(jnp.bfloat16), "tensor").astype(jnp.float32)
    image_grad = image_back + norm_backward(
        ready_back, image_normed, image_inverse, image_norm_gain
    )
    text_back = (
        text_unit_back - text_unit * jnp.sum(text_unit * text_unit_back, axis=1, keepdims=True)
    ) * text_invnorm
    column_part = lax.dot_general(
        text_back.astype(jnp.bfloat16),
        text_head,
        (((1,), (1,)), ((), ())),
        preferred_element_type=jnp.float32,
    )
    column_back = lax.all_gather(
        column_part.astype(jnp.bfloat16), "tensor", axis=1, tiled=True
    ).astype(column_part.dtype)
    text_grad = norm_backward(column_back, text_normed, text_inverse, text_norm_gain)
    return (image_grad, text_grad)


def solution(mesh):
    return jax.shard_map(
        per_device,
        mesh=mesh,
        in_specs=(
            P("dp", None),
            P("dp", None),
            P(),
            P(),
            P("dp", "tensor"),
            P("tensor"),
            P("tensor", "dp"),
            P(),
            P(),
            P(),
            P("tensor", None),
            P(),
            P(),
            P(),
            P(),
        ),
        out_specs=(P("dp", None), P("dp", None)),
        check_vma=False,
    )
```

profile of v0, /device:TPU:6, one launch (start us, length us, event | category | flops | bytes accessed | tf_op | source)
XLA Modules:
  0.0 1116.6 jit_solution(7299025797681230598)
XLA Ops:
  7.2 0.7 all-gather.12.cloned.1.call-update
  7.9 0.0 all-gather.14.cloned.1.call-start
  8.0 0.7 all-gather.14.cloned.1.call-update
  8.7 0.0 all-reduce.8.cloned.1.call-start
  8.7 0.8 dynamic-slice.1
  9.5 0.8 dynamic-slice
  10.3 1.1 convert_reduce_fusion
  11.4 1.0 convert_reduce_fusion.1
  12.4 1.1 fusion.35
  13.6 1.1 fusion.36
  14.7 1.0 fusion.22
  15.7 1.0 fusion.105
  16.8 216.8 %all-gather.12.cloned.1.call-done = bf16[128,9,1076]{2,1,0:T(8,128)(2,1)} async-done(((bf16[1,9,1076]{2,1,0:T(8,128)(2,1)}), bf16[128,9,1076]{2,1,0:T(8,128)(2,1)}) %all-gather.12.cloned.1.call-update) | async-done | bytes 2479120 | tf_op jit(solution)/shard_map/all_gather | solution.py:71
  233.5 4.6 reshape.93
  238.2 1.4 convolution_add_fusion
  239.6 215.4 %all-gather.14.cloned.1.call-done = bf16[128,9,1076]{2,1,0:T(8,128)(2,1)} async-done(((bf16[1,9,1076]{2,1,0:T(8,128)(2,1)}), bf16[128,9,1076]{2,1,0:T(8,128)(2,1)}) %all-gather.14.cloned.1.call-update) | async-done | bytes 2479120 | tf_op jit(solution)/shard_map/all_gather | solution.py:72
  455.0 6.0 reshape.95
  460.9 3.5 fusion.77
  464.5 0.0 all-gather.8.cloned.1.call-start
  464.5 61.1 %all-reduce.8.cloned.1.call-done = (f32[64,1152]{1,0:T(8,128)}, f32[64,1152]{1,0:T(8,128)}) async-done(((f32[64,1152]{1,0:T(8,128)}, f32[64,1152]{1,0:T(8,128)}), (f32[64,1152]{1,0:T(8,128)}, f32[64,1152]{1,0:T(8,128)})) %all-reduce.8.cloned.1.call-update) | async-done | bytes 589840 | tf_op jit(solution)/shard_map/psum | solution.py:41
  525.6 1.1 multiply_reduce_fusion
  526.7 1.1 add_multiply_fusion
  527.8 0.7 copy-done.4
  528.5 0.6 dynamic-slice_convert_fusion.1
  529.1 0.0 all-gather.10.cloned.1.call-start
  529.2 1.1 multiply_reduce_fusion.1
  530.3 1.1 fusion.73
  531.4 0.7 copy-done.1
  532.1 0.6 dynamic-slice_convert_fusion
  532.7 0.0 all-reduce.6.cloned.1.call-start
  534.8 212.4 %all-gather.8.cloned.1.call-done = bf16[2048,1152]{1,0:T(8,128)(2,1)} async-done(((bf16[16,1152]{1,0:T(8,128)(2,1)}), bf16[2048,1152]{1,0:T(8,128)(2,1)}) %all-gather.8.cloned.1.call-update) | async-done | bytes 4718608 | tf_op jit(solution)/shard_map/all_gather | solution.py:119
  747.2 6.9 convolution_convert_fusion.2
  754.2 0.0 all-reduce.10.cloned.1.call-start
  754.2 214.4 %all-gather.10.cloned.1.call-done = bf16[2048,1152]{1,0:T(8,128)(2,1)} async-done(((bf16[16,1152]{1,0:T(8,128)(2,1)}), bf16[2048,1152]{1,0:T(8,128)(2,1)}) %all-gather.10.cloned.1.call-update) | async-done | bytes 4718608 | tf_op jit(solution)/shard_map/all_gather | solution.py:120
  968.6 6.9 convolution_convert_fusion.1
  975.6 51.4 %all-reduce.6.cloned.1.call-done = bf16[64,1152]{1,0:T(8,128)(2,1)} async-done(((bf16[64,1152]{1,0:T(8,128)(2,1)}), bf16[64,1152]{1,0:T(8,128)(2,1)}) %all-reduce.6.cloned.1.call-update) | async-done | bytes 147472 | tf_op jit(solution)/shard_map/psum | solution.py:122
  1026.9 1.1 fusion.37
  1028.1 3.9 convolution_convert_fusion
  1032.0 55.7 %all-reduce.10.cloned.1.call-done = (bf16[64,1152]{1,0:T(8,128)(2,1)}, bf16[64,1152]{1,0:T(8,128)(2,1)}) async-done(((bf16[64,1152]{1,0:T(8,128)(2,1)}, bf16[64,1152]{1,0:T(8,128)(2,1)}), (bf16[64,1152]{1,0:T(8,128)(2,1)}, bf16[64,1152]{1,0:T(8,128)(2,1)})) %all-reduce.10.cloned.1.call-update) | async-done | bytes 294928 | tf_op jit(solution)/shard_map/psum | solution.py:138
  1087.8 1.5 fusion.52
  1089.2 1.4 fusion.17
  1090.7 14.7 %all-gather.2 = bf16[4,288,64]{1,2,0:T(8,128)(2,1)S(1)} all-gather(bf16[1,288,64]{1,2,0:T(8,128)(2,1)S(1)} %fusion.17), channel_id=1, replica_groups=mesh['dp'=128,'tensor'=4] {'tensor'}, dimensions={0}, use_global_device_ids=true | all-gather | bytes 184320 | tf_op jit(solution)/shard_map/all_gather | solution.py:151
  1105.4 0.2 copy.18
  1105.5 0.2 reshape.98
  1105.8 1.1 fusion.49
  1106.9 0.1 multiply_reduce_fusion.2
  1107.1 1.8 fusion.51
  1108.8 0.9 fusion.34
  (42 shorter events, 0.2 us)
Async XLA Ops:
  7.2 8.6 copy-start
  7.2 226.4 %all-gather.12.cloned.1.call-start = ((), (), s32[]{:S(2)}) async-start(), calls=%async_computation.3 | async-start | bytes 4755456 | tf_op jit(solution)/shard_map/all_gather | solution.py:71
  7.9 447.1 %all-gather.14.cloned.1.call-start = ((), (), s32[]{:S(2)}) async-start(), calls=%async_computation.4 | async-start | bytes 4755456 | tf_op jit(solution)/shard_map/all_gather | solution.py:72
  8.7 516.9 %all-reduce.8.cloned.1.call-start = ((), (), s32[]{:S(2)}) async-start(), calls=%async_computation.5 | async-start | bytes 1179648 | tf_op jit(solution)/shard_map/psum | solution.py:41
  10.3 227.9 %copy-start.3 = (bf16[64,1152]{1,0:T(8,128)(2,1)S(1)}, bf16[64,1152]{1,0:T(8,128)(2,1)}, u32[]{:S(2)}) copy-start(bf16[64,1152]{1,0:T(8,128)(2,1)} %param.15) | copy-start | bytes 442372
  10.3 227.9 %copy-start.8 = (f32[1152]{0:T(1024)S(1)}, f32[1152]{0:T(1024)}, u32[]{:S(2)}) copy-start(f32[1152]{0:T(1024)} %param.17) | copy-start | bytes 13828
  10.3 227.9 %copy-start.11 = (f32[1076]{0:T(1024)S(1)}, f32[1076]{0:T(1024)}, u32[]{:S(2)}) copy-start(f32[1076]{0:T(1024)} %param.20) | copy-start | bytes 12916
  10.3 228.0 %copy-start.12 = (f32[1152]{0:T(1024)S(1)}, f32[1152]{0:T(1024)}, u32[]{:S(2)}) copy-start(f32[1152]{0:T(1024)} %param.18) | copy-start | bytes 13828
  239.6 286.0 %copy-start.9 = (f32[1152]{0:T(1024)S(1)}, f32[1152]{0:T(1024)}, u32[]{:S(2)}) copy-start(f32[1152]{0:T(1024)} %param.26) | copy-start | bytes 13828
  239.6 289.6 %copy-start.10 = (f32[1152]{0:T(1024)S(1)}, f32[1152]{0:T(1024)}, u32[]{:S(2)}) copy-start(f32[1152]{0:T(1024)} %param.22) | copy-start | bytes 13828
  464.5 282.8 %all-gather.8.cloned.1.call-start = ((), (), s32[]{:S(2)}) async-start(), calls=%async_computation | async-start | bytes 4755456 | tf_op jit(solution)/shard_map/all_gather | solution.py:119
  527.8 0.7 copy-start.4
  529.1 439.5 %all-gather.10.cloned.1.call-start = ((), (), s32[]{:S(2)}) async-start(), calls=%async_computation.2 | async-start | bytes 4755456 | tf_op jit(solution)/shard_map/all_gather | solution.py:120
  531.4 0.7 copy-start.1
  532.7 494.2 %all-reduce.6.cloned.1.call-start = ((), (), s32[]{:S(2)}) async-start(), calls=%async_computation.1 | async-start | bytes 294912 | tf_op jit(solution)/shard_map/psum | solution.py:122
  754.2 333.6 %all-reduce.10.cloned.1.call-start = ((), (), s32[]{:S(2)}) async-start(), calls=%async_computation.6 | async-start | bytes 589824 | tf_op jit(solution)/shard_map/psum | solution.py:138
  1028.1 77.7 %copy-start.7 = (f32[1152]{0:T(1024)S(1)}, f32[1152]{0:T(1024)}, u32[]{:S(2)}) copy-start(f32[1152]{0:T(1024)} %param.23) | copy-start | bytes 13828
  1032.0 76.8 %copy-start.2 = (f32[64,1152]{1,0:T(8,128)S(1)}, f32[64,1152]{1,0:T(8,128)}, u32[]{:S(2)}) copy-start(f32[64,1152]{1,0:T(8,128)} %copy-done.1) | copy-start | bytes 884740
  1032.0 76.8 %copy-start.5 = (bf16[64,1152]{1,0:T(8,128)(2,1)S(1)}, bf16[64,1152]{1,0:T(8,128)(2,1)}, u32[]{:S(2)}) copy-start(bf16[64,1152]{1,0:T(8,128)(2,1)} %all-reduce.6.cloned.1.call-done) | copy-start | bytes 442372
  1087.8 21.1 %copy-start.6 = (bf16[64,1152]{1,0:T(8,128)(2,1)S(1)}, bf16[64,1152]{1,0:T(8,128)(2,1)}, u32[]{:S(2)}) copy-start(bf16[64,1152]{1,0:T(8,128)(2,1)} %get-tuple-element.6) | copy-start | bytes 442372
Sparse Core Ops, SparseCore 0:
  10.2 223.3 all-gather.11
  235.7 219.2 all-gather.13
  464.6 60.9 all-reduce.7
  529.2 217.9 all-gather.7
  749.3 219.3 all-gather.9
  971.4 55.4 all-reduce.5
  1032.2 55.5 all-reduce.9
where the time goes:
time: 1120 us
  waiting for transfers between devices  1030 us (92%)
  matrix products  25.1 us (2%)
  between operations  16.4 us (1%)
  other arithmetic  16.3 us (1%)
  local copies, waits for them, and re-layouts  15.2 us (1%)
  blocking collectives  14.7 us (1%)
    all_gather x1, waiting for transfers between devices, per_device(): lax.all_gather(image_up, 'dp', axis=0, tiled=True)  217 us
    all_gather x1, waiting for transfers between devices, per_device(): lax.all_gather(image_down, 'dp', axis=1, tiled=True)  215 us
    all_gather x1, waiting for transfers between devices, per_device(): lax.all_gather(image_travel, 'dp', axis=0, tiled=True)  214 us
    all_gather x1, waiting for transfers between devices, per_device(): lax.all_gather(text_travel, 'dp', axis=0, tiled=True)  212 us
    psum x1, waiting for transfers between devices, unit_rows(): row_whole = lax.psum(partial_value, 'tensor') + addend  61.1 us
    psum x1, waiting for transfers between devices, per_device(): lax.psum(ready_part.astype(jnp.bfloat16), 'tensor').astype(jnp.float32)  55.7 us
    psum x1, waiting for transfers between devices, per_device(): lax.psum(image_part.astype(jnp.bfloat16), 'tensor').astype(jnp.float32)  51.4 us
  transfers between devices with their start and end apart: 7, of which 7 were waited for; matrix products, arithmetic and copies ran while one was open for 3% of the time, Pallas kernels for 0%

commit v1 on v0

v1 whole, which is shorter than its diff:
```python
import jax
import jax.numpy as jnp
from jax import lax
from jax.sharding import Mesh, PartitionSpec as P

epsilon = 1e-06
tanh_coef = 0.7978845608028654
cubic_coef = 0.044715
low = jnp.bfloat16
DP = ("ylo", "x", "z", "core")
GROUP = ("ylo", "x", "core")


def gelu_parts(preact):
    inside = tanh_coef * (preact + cubic_coef * preact * preact * preact)
    tangent = jnp.tanh(inside)
    activated = 0.5 * preact * (1.0 + tangent)
    derivative = 0.5 * (1.0 + tangent) + 0.5 * preact * (1.0 - tangent * tangent) * tanh_coef * (
        1.0 + 3.0 * cubic_coef * preact * preact
    )
    return (activated, derivative)


def norm_stats(source):
    centre = source - jnp.mean(source, axis=1, keepdims=True)
    inverse = lax.rsqrt(jnp.mean(centre * centre, axis=1, keepdims=True) + epsilon)
    return (centre * inverse, inverse)


def norm_backward(upstream, normed, inverse, gain_vec):
    scaled = upstream * gain_vec
    return inverse * (
        scaled
        - jnp.mean(scaled, axis=1, keepdims=True)
        - normed * jnp.mean(scaled * normed, axis=1, keepdims=True)
    )


def unit_rows(total):
    inverse = lax.rsqrt(jnp.sum(total * total, axis=1, keepdims=True) + epsilon)
    return (total * inverse, inverse)


def unit_backward(upstream, unit, inverse):
    return (upstream - unit * jnp.sum(unit * upstream, axis=1, keepdims=True)) * inverse


def mm(a, b):
    return jnp.dot(a, b, preferred_element_type=jnp.float32)


def mm_nt(a, b):
    return lax.dot_general(a, b, (((1,), (1,)), ((), ())), preferred_element_type=jnp.float32)


def mm_tn(a, b):
    return lax.dot_general(a, b, (((0,), (0,)), ((), ())), preferred_element_type=jnp.float32)


def spread(block, axes):
    count = lax.axis_size(axes)
    slots = jnp.broadcast_to(block[None], (count,) + block.shape)
    return lax.all_to_all(slots, axes, 0, 0, tiled=True)


def sum_slots(partial, axes):
    count = lax.axis_size(axes)
    slots = partial.astype(low).reshape(count, partial.shape[0] // count, partial.shape[1])
    return jnp.sum(lax.all_to_all(slots, axes, 0, 0, tiled=True).astype(jnp.float32), axis=0)


def tensor_total(partial):
    count = lax.axis_size("tensor")
    sent = partial.astype(low)
    total = sent.astype(jnp.float32)
    for step in range(1, count):
        turn = [(i, (i + step) % count) for i in range(count)]
        total = total + lax.ppermute(sent, "tensor", turn).astype(jnp.float32)
    return total


def per_device(
    image_pooled,
    text_pooled,
    image_norm_gain,
    image_norm_bias,
    image_up,
    image_up_bias,
    image_down,
    image_down_bias,
    text_norm_gain,
    text_norm_bias,
    text_head,
    text_head_bias,
    log_scale,
    logit_shift,
    loss_scale,
):
    ylo_count, x_count, z_count, core_count = (lax.axis_size(a) for a in DP)
    tensor_count = lax.axis_size("tensor")
    group_count = lax.axis_size(GROUP)
    tensor_rank = lax.axis_index("tensor")
    z_rank = lax.axis_index("z")
    group_rank = lax.axis_index(GROUP)
    block_rows, width = image_pooled.shape
    own_rows = block_rows // tensor_count
    pairs_total = block_rows * lax.axis_size(DP)
    slab, hidden_local = image_up.shape
    chunk = -(-hidden_local // (group_count * 4)) * 4
    hidden_mine = chunk * tensor_count

    def turned(vec):
        return (
            vec.reshape(ylo_count, x_count, z_count, core_count * slab).transpose(0, 2, 1, 3).reshape(width)
        )

    source_of = turned(jnp.arange(width, dtype=jnp.int32))
    turn = (jnp.arange(width, dtype=jnp.int32)[:, None] == source_of[None, :]).astype(low)

    def cut(arr):
        padded = jnp.pad(arr, ((0, 0), (0, chunk * group_count - hidden_local)))
        return padded.reshape(arr.shape[0], group_count, chunk)

    bias_high = image_up_bias.astype(low)
    bias_low = (image_up_bias - bias_high.astype(jnp.float32)).astype(low)
    rows = jnp.concatenate([image_up, image_down.T, bias_high[None], bias_low[None]], axis=0)
    slots = cut(rows).transpose(1, 0, 2)
    slots = jnp.broadcast_to(slots[:, None], (group_count, tensor_count) + slots.shape[1:])
    slots = slots.reshape((group_count * tensor_count,) + slots.shape[2:])
    got = lax.all_to_all(slots, GROUP + ("tensor",), 0, 0, tiled=True)
    got = got.reshape(ylo_count, x_count * core_count, tensor_count, 2 * slab + 2, chunk)
    up_bias = (
        got[0, 0, :, 2 * slab].astype(jnp.float32) + got[0, 0, :, 2 * slab + 1].astype(jnp.float32)
    ).reshape(hidden_mine)
    both = got[:, :, :, : 2 * slab].reshape(ylo_count, x_count * core_count, tensor_count, 2, slab, chunk)
    both = both.transpose(0, 1, 4, 3, 2, 5).reshape(
        ylo_count, x_count * core_count * slab, 2 * hidden_mine
    )
    first = spread(both[0], "z").reshape(-1, 2 * hidden_mine)
    second = lax.all_gather(both[1], "z", axis=0, tiled=True)
    weights = jnp.concatenate([first, second], axis=0)
    up_mine = weights[:, :hidden_mine]
    down_mine = weights[:, hidden_mine:]

    gain_turned = turned(image_norm_gain)
    image_own = lax.dynamic_slice_in_dim(image_pooled, tensor_rank * own_rows, own_rows, 0)
    image_own = mm(image_own, turn)
    image_normed, image_inverse = norm_stats(image_own)
    ready = (image_normed * gain_turned + turned(image_norm_bias)).astype(low)
    ready_all = lax.all_gather(ready, GROUP, axis=0, tiled=True)

    text_normed, text_inverse = norm_stats(text_pooled.astype(jnp.float32))
    text_ready = (text_normed * text_norm_gain + text_norm_bias).astype(low)
    head_rows = text_head.shape[0]
    text_columns = lax.dynamic_slice_in_dim(text_ready, tensor_rank * head_rows, head_rows, 1)
    head_turned = mm(text_head, turn).astype(low)
    text_sum = tensor_total(mm(text_columns, head_turned)) + turned(text_head_bias)
    text_unit, text_invnorm = unit_rows(text_sum)
    text_all = lax.all_gather(text_unit.astype(low), "z", axis=0, tiled=True)

    hidden_pre = mm(ready_all, up_mine) + up_bias
    hidden_act, hidden_slope = gelu_parts(hidden_pre)
    image_sum = sum_slots(mm_nt(hidden_act.astype(low), down_mine), GROUP)
    image_sum = image_sum + image_own + turned(image_down_bias)
    image_unit, image_invnorm = unit_rows(image_sum)
    image_all = spread(image_unit.astype(low), GROUP).reshape(-1, width)

    scale_value = jnp.exp(log_scale[0])
    factor = loss_scale[0] * scale_value / pairs_total
    scores = mm_nt(image_all, text_all)
    image_at = lax.broadcasted_iota(jnp.int32, scores.shape, 0) - group_rank * own_rows
    text_at = lax.broadcasted_iota(jnp.int32, scores.shape, 1) - (
        z_rank * block_rows + tensor_rank * own_rows
    )
    same = (image_at == text_at) & (image_at >= 0) & (image_at < own_rows)
    pair_coef = (
        factor * (jax.nn.sigmoid(scale_value * scores + logit_shift[0]) - same.astype(jnp.float32))
    ).astype(low)
    image_unit_back = sum_slots(mm(pair_coef, text_all), GROUP)
    text_part = mm_tn(pair_coef, image_all).astype(low)
    text_unit_back = tensor_total(lax.psum_scatter(text_part, "z", scatter_dimension=0, tiled=True))

    image_back = unit_backward(image_unit_back, image_unit, image_invnorm)
    back_all = spread(image_back.astype(low), GROUP).reshape(-1, width)
    pre_back = (mm(back_all, down_mine) * hidden_slope).astype(low)
    ready_back = sum_slots(mm_nt(pre_back, up_mine), GROUP)
    image_grad = image_back + norm_backward(ready_back, image_normed, image_inverse, gain_turned)
    image_grad = mm_nt(image_grad.astype(low), turn).astype(low)
    image_grad = spread(image_grad, "tensor").reshape(block_rows, width).astype(jnp.float32)

    text_back = unit_backward(text_unit_back, text_unit, text_invnorm)
    column_part = mm_nt(text_back.astype(low), head_turned).astype(low)
    column_back = spread(column_part, "tensor").transpose(1, 0, 2).reshape(block_rows, width)
    text_grad = norm_backward(column_back.astype(jnp.float32), text_normed, text_inverse, text_norm_gain)
    return (image_grad, text_grad)


def solution(mesh):
    grid = Mesh(mesh.devices.reshape(2, 4, 8, 2, 4), DP + ("tensor",))
    return jax.shard_map(
        per_device,
        mesh=grid,
        in_specs=(
            P(DP, None),
            P(DP, None),
            P(),
            P(),
            P(DP, "tensor"),
            P("tensor"),
            P("tensor", DP),
            P(),
            P(),
            P(),
            P("tensor", None),
            P(),
            P(),
            P(),
            P(),
        ),
        out_specs=(P(DP, None), P(DP, None)),
        check_vma=False,
    )
```

time: 1120 us -> 306 us (0.27)
  waiting for transfers between devices: 1030 us -> 99.4 us
  starting transfers between devices: 0.28 us -> 93.3 us
  blocking collectives: 14.7 us -> 57.5 us
    all_gather x4 -> x1, waiting for transfers between devices: 859 us -> 31.6 us  [per_device(): text_all = lax.all_gather(text_unit.astype(low), 'z', axis=0, tiled=True)]
    psum x3 -> x0, waiting for transfers between devices: 168 us -> none  [the longest x1 61.1 us: unit_rows(): row_whole = lax.psum(partial_value, 'tensor') + addend]
    all_to_all x0 -> x9, starting transfers between devices: none -> 66.1 us  [the longest x5 34.3 us: spread(): return lax.all_to_all(slots, axes, 0, 0, tiled=True)]
    all_gather x1 -> x2, blocking collectives: 14.7 us -> 57.5 us  [the longest x1 39.2 us: per_device(): second = lax.all_gather(both[1], 'z', axis=0, tiled=True)]
    all_to_all x0 -> x9, waiting for transfers between devices: none -> 29.5 us  [the longest x3 16.2 us: sum_slots(): lax.all_to_all(slots, axes, 0, 0, tiled=True).astype(jnp.float32)]
    ppermute x0 -> x6, starting transfers between devices: none -> 27.1 us  [tensor_total(): total = total + lax.ppermute(sent, 'tensor', turn).astype(jnp.float32)]
    reduce_scatter x0 -> x1, waiting for transfers between devices: none -> 26.3 us  [per_device(): lax.psum_scatter(text_part, 'z', scatter_dimension=0, tiled=True)]
    ppermute x0 -> x6, waiting for transfers between devices: none -> 12 us  [tensor_total(): total = total + lax.ppermute(sent, 'tensor', turn).astype(jnp.float32)]
  transfers between devices with their start and end apart: 7 -> 17, of which waited for: 7 -> 10; matrix products, arithmetic and copies ran while one was open for 3% -> 7% of each run, Pallas kernels for 0% -> 0%
where the time goes in v1:
time: 306 us; the launch traced here: 303 us
  waiting for transfers between devices  99.4 us (32%)
  starting transfers between devices  93.3 us (30%)
  blocking collectives  57.5 us (19%)
  matrix products  18.8 us (6%)
  between operations  16.7 us (5%)
  local copies, waits for them, and re-layouts  9.62 us (3%)
  other arithmetic  8.1 us (3%)
    all_gather x1, blocking collectives, per_device(): second = lax.all_gather(both[1], 'z', axis=0, tiled=True)  39.2 us
    all_to_all x5, starting transfers between devices, spread(): return lax.all_to_all(slots, axes, 0, 0, tiled=True)  34.3 us
    all_gather x1, waiting for transfers between devices, per_device(): text_all = lax.all_gather(text_unit.astype(low), 'z', axis=0, tiled=True)  31.6 us
    ppermute x6, starting transfers between devices, tensor_total(): total = total + lax.ppermute(sent, 'tensor', turn).astype(jnp.float32)  27.1 us
    reduce_scatter x1, waiting for transfers between devices, per_device(): lax.psum_scatter(text_part, 'z', scatter_dimension=0, tiled=True)  26.3 us
    all_to_all x3, starting transfers between devices, sum_slots(): lax.all_to_all(slots, axes, 0, 0, tiled=True).astype(jnp.float32)  21.1 us
    all_gather x1, blocking collectives, per_device(): ready_all = lax.all_gather(ready, GROUP, axis=0, tiled=True)  18.3 us
    all_to_all x3, waiting for transfers between devices, sum_slots(): lax.all_to_all(slots, axes, 0, 0, tiled=True).astype(jnp.float32)  16.2 us
  transfers between devices with their start and end apart: 17, of which 10 were waited for; matrix products, arithmetic and copies ran while one was open for 7% of the time, Pallas kernels for 0%

profile of v1, /device:TPU:6, one launch (start us, length us, event | category | flops | bytes accessed | tf_op | source)
XLA Modules:
  0.0 303.4 jit_solution(5570157508930131080)
XLA Ops:
  7.2 0.8 subtract_convert_fusion
  8.0 0.8 fusion.55
  9.1 1.3 reshape.264
  10.4 10.6 %all-to-all-start = ((bf16[64,2,680]{2,1,0:T(2,128)(2,1)}), bf16[64,2,680]{2,1,0:T(2,128)(2,1)S(1)}, u32[]{:S(2)}, u32[]{:S(2)}) async-start(bf16[64,2,680]{2,1,0:T(2,128)(2,1)} %reshape.264), calls=%async_computation | async-start | bytes 393216 | tf_op jit(solution)/shard_map/all_to_all | solution.py:130
  21.8 1.9 fusion.85
  23.9 1.3 fusion.6
  25.3 0.8 dynamic-slice.1
  26.5 18.3 %all_gather.9 = bf16[256,1152]{1,0:T(8,128)(2,1)} all-gather(bf16[16,1152]{1,0:T(8,128)(2,1)S(1)} %add_convert_fusion.1), channel_id=1, replica_groups=mesh['ylo'=2,'x'=4,'z'=8,'core'=2,'tensor'=4] {'ylo','x','core'}, dimensions={0}, use_global_device_ids=true | all-gather | bytes 626688 | tf_op jit(solution)/shard_map/all_gather | solution.py:150
  45.9 0.9 broadcast_in_dim.22
  46.8 10.3 %all-to-all-start.1 = ((bf16[8,72,544]{2,1,0:T(8,128)(2,1)}), bf16[8,72,544]{2,1,0:T(8,128)(2,1)S(1)}, u32[]{:S(2)}, u32[]{:S(2)}) async-start(bf16[8,72,544]{2,1,0:T(8,128)(2,1)} %broadcast_in_dim.22), calls=%async_computation.1 | async-start | bytes 1474560 | tf_op jit(solution)/shard_map/all_to_all | solution.py:63
  57.1 0.8 fusion.19
  58.3 39.2 %all_gather.10 = bf16[576,544]{1,0:T(8,128)(2,1)S(1)} all-gather(bf16[72,544]{1,0:T(8,128)(2,1)S(1)} %squeeze.13), channel_id=1, replica_groups=mesh['ylo'=2,'x'=4,'z'=8,'core'=2,'tensor'=4] {'z'}, dimensions={0}, use_global_device_ids=true | all-gather | bytes 705024 | tf_op jit(solution)/shard_map/all_gather | solution.py:140
  97.5 2.0 convolution_add_fusion
  99.5 1.6 convolution_convert_fusion.3
  101.1 8.5 %all-to-all-start.2 = ((bf16[16,16,1152]{2,1,0:T(8,128)(2,1)}), bf16[16,16,1152]{2,1,0:T(8,128)(2,1)S(1)}, u32[]{:S(2)}, u32[]{:S(2)}) async-start(bf16[16,16,1152]{2,1,0:T(8,128)(2,1)} %bitcast.49), calls=%async_computation.2 | async-start | bytes 1179648 | tf_op jit(solution)/shard_map/all_to_all | solution.py:69
  109.6 1.2 convolution_convert_fusion.4
  110.9 4.6 %collective-permute-start.2 = (bf16[64,1152]{1,0:T(8,128)(2,1)S(1)}, bf16[64,1152]{1,0:T(8,128)(2,1)S(1)}, u32[]{:S(2)}, u32[]{:S(2)}) collective-permute-start(bf16[64,1152]{1,0:T(8,128)(2,1)S(1)} %convolution_convert_fusion.4), channel_id=1, source_target_pairs={{0,3},{1,0},{2,1},{3,2},{4,7},{5,4},{6,5},{7,6},{8,11},{9,8},{10,9... | collective-permute-start | bytes 442376 | tf_op jit(solution)/shard_map/ppermute | solution.py:78
  115.5 5.2 %collective-permute-start.1 = (bf16[64,1152]{1,0:T(8,128)(2,1)S(1)}, bf16[64,1152]{1,0:T(8,128)(2,1)S(1)}, u32[]{:S(2)}, u32[]{:S(2)}) collective-permute-start(bf16[64,1152]{1,0:T(8,128)(2,1)S(1)} %convolution_convert_fusion.4), channel_id=1, source_target_pairs={{0,2},{1,3},{2,0},{3,1},{4,6},{5,7},{6,4},{7,5},{8,10},{9,11},{10,... | collective-permute-start | bytes 442376 | tf_op jit(solution)/shard_map/ppermute | solution.py:78
  120.6 3.4 %collective-permute-start = (bf16[64,1152]{1,0:T(8,128)(2,1)S(1)}, bf16[64,1152]{1,0:T(8,128)(2,1)S(1)}, u32[]{:S(2)}, u32[]{:S(2)}) collective-permute-start(bf16[64,1152]{1,0:T(8,128)(2,1)S(1)} %convolution_convert_fusion.4), channel_id=1, source_target_pairs={{0,1},{1,2},{2,3},{3,0},{4,5},{5,6},{6,7},{7,4},{8,9},{9,10},{10,1... | collective-permute-start | bytes 442376 | tf_op jit(solution)/shard_map/ppermute | solution.py:78
  124.6 6.7 %collective-permute-done.1 = bf16[64,1152]{1,0:T(8,128)(2,1)S(1)} collective-permute-done((bf16[64,1152]{1,0:T(8,128)(2,1)S(1)}, bf16[64,1152]{1,0:T(8,128)(2,1)S(1)}, u32[]{:S(2)}, u32[]{:S(2)}) %collective-permute-start.1) | collective-permute-done | bytes 147488 | tf_op jit(solution)/shard_map/ppermute | solution.py:78
  132.6 0.9 broadcast_in_dim.23
  133.5 8.8 %all-to-all-start.3 = ((bf16[16,16,1152]{2,1,0:T(8,128)(2,1)}), bf16[16,16,1152]{2,1,0:T(8,128)(2,1)S(1)}, u32[]{:S(2)}, u32[]{:S(2)}) async-start(bf16[16,16,1152]{2,1,0:T(8,128)(2,1)} %broadcast_in_dim.23), calls=%async_computation.3 | async-start | bytes 1179648 | tf_op jit(solution)/shard_map/all_to_all | solution.py:63
  144.3 31.6 %all-gather.2.cloned.1.call-done = bf16[512,1152]{1,0:T(8,128)(2,1)} async-done(((bf16[64,1152]{1,0:T(8,128)(2,1)}), bf16[512,1152]{1,0:T(8,128)(2,1)}) %all-gather.2.cloned.1.call-update) | async-done | bytes 1179664 | tf_op jit(solution)/shard_map/all_gather | solution.py:159
  175.9 2.0 fusion.15
  177.9 1.3 convolution_convert_fusion.1
  179.3 5.7 %all-to-all-start.4 = ((bf16[16,16,1152]{2,1,0:T(8,128)(2,1)}), bf16[16,16,1152]{2,1,0:T(8,128)(2,1)S(1)}, u32[]{:S(2)}, u32[]{:S(2)}) async-start(bf16[16,16,1152]{2,1,0:T(8,128)(2,1)} %bitcast.17), calls=%async_computation.4 | async-start | bytes 1179648 | tf_op jit(solution)/shard_map/all_to_all | solution.py:69
  185.0 1.6 convolution_convert_fusion
  186.6 7.8 %all-to-all-done.4 = bf16[16,16,1152]{2,1,0:T(8,128)(2,1)S(1)} async-done(((bf16[16,16,1152]{2,1,0:T(8,128)(2,1)}), bf16[16,16,1152]{2,1,0:T(8,128)(2,1)S(1)}, u32[]{:S(2)}, u32[]{:S(2)}) %all-to-all-start.4) | async-done | bytes 589856 | tf_op jit(solution)/shard_map/all_to_all | solution.py:69
  194.8 0.9 broadcast_in_dim.24
  195.6 6.5 %all-to-all-start.5 = ((bf16[16,16,1152]{2,1,0:T(8,128)(2,1)}), bf16[16,16,1152]{2,1,0:T(8,128)(2,1)}, u32[]{:S(2)}, u32[]{:S(2)}) async-start(bf16[16,16,1152]{2,1,0:T(8,128)(2,1)} %broadcast_in_dim.24), calls=%async_computation.5 | async-start | bytes 1179648 | tf_op jit(solution)/shard_map/all_to_all | solution.py:63
  202.1 26.3 %reduce-scatter.2.cloned.1.call-done = bf16[64,1152]{1,0:T(8,128)(2,1)} async-done(((bf16[512,1152]{1,0:T(8,128)(2,1)}), bf16[64,1152]{1,0:T(8,128)(2,1)}) %reduce-scatter.2.cloned.1.call-update) | async-done | bytes 147472 | tf_op jit(solution)/shard_map/reduce_scatter | solution.py:181
  228.4 5.5 %collective-permute-start.5 = (bf16[64,1152]{1,0:T(8,128)(2,1)}, bf16[64,1152]{1,0:T(8,128)(2,1)S(1)}, u32[]{:S(2)}, u32[]{:S(2)}) collective-permute-start(bf16[64,1152]{1,0:T(8,128)(2,1)} %reduce-scatter.2.cloned.1.call-done), channel_id=1, source_target_pairs={{0,3},{1,0},{2,1},{3,2},{4,7},{5,4},{6,5},{7,6},{8,11},{9,8},{10,9... | collective-permute-start | bytes 442376 | tf_op jit(solution)/shard_map/ppermute | solution.py:78
  233.9 4.1 %collective-permute-start.4 = (bf16[64,1152]{1,0:T(8,128)(2,1)}, bf16[64,1152]{1,0:T(8,128)(2,1)S(1)}, u32[]{:S(2)}, u32[]{:S(2)}) collective-permute-start(bf16[64,1152]{1,0:T(8,128)(2,1)} %reduce-scatter.2.cloned.1.call-done), channel_id=1, source_target_pairs={{0,2},{1,3},{2,0},{3,1},{4,6},{5,7},{6,4},{7,5},{8,10},{9,11},{10,... | collective-permute-start | bytes 442376 | tf_op jit(solution)/shard_map/ppermute | solution.py:78
  238.1 4.3 %collective-permute-start.3 = (bf16[64,1152]{1,0:T(8,128)(2,1)}, bf16[64,1152]{1,0:T(8,128)(2,1)S(1)}, u32[]{:S(2)}, u32[]{:S(2)}) collective-permute-start(bf16[64,1152]{1,0:T(8,128)(2,1)} %reduce-scatter.2.cloned.1.call-done), channel_id=1, source_target_pairs={{0,1},{1,2},{2,3},{3,0},{4,5},{5,6},{6,7},{7,4},{8,9},{9,10},{10,1... | collective-permute-start | bytes 442376 | tf_op jit(solution)/shard_map/ppermute | solution.py:78
  242.4 2.3 collective-permute-done.5
  244.7 1.1 collective-permute-done.4
  245.8 1.9 collective-permute-done.3
  247.8 1.1 multiply_reduce_fusion.1
  248.9 1.4 convolution_convert_fusion.5
  251.0 5.4 %all-to-all-start.8 = ((bf16[4,64,288]{2,1,0:T(8,128)(2,1)}), bf16[4,64,288]{2,1,0:T(8,128)(2,1)S(1)}, u32[]{:S(2)}, u32[]{:S(2)}) async-start(bf16[4,64,288]{2,1,0:T(8,128)(2,1)} %broadcast_in_dim.26), calls=%async_computation.9 | async-start | bytes 393216 | tf_op jit(solution)/shard_map/all_to_all | solution.py:63
  256.4 3.5 %convolution_convert_fusion.2 = bf16[256,1152]{1,0:T(8,128)(2,1)} fusion(bf16[256,1152]{1,0:T(8,128)(2,1)} %bitcast.18, f32[256,272]{0,1:T(8,128)} %copy-done.18, bf16[576,544]{1,0:T(8,128)(2,1)S(1)} %copy-done.4, bf16[576,544]{1,0:T(8,128)(2,1)S(1)} %bitcast.48), kind=kOutput, calls=%fused_computation.10 | convolution fusion | flops 324988928 | bytes 4407296 | tf_op jit(solution)/shard_map/dot_general | solution.py:53
  260.0 5.2 %all-to-all-done.8 = bf16[4,64,288]{2,1,0:T(8,128)(2,1)S(1)} async-done(((bf16[4,64,288]{2,1,0:T(8,128)(2,1)}), bf16[4,64,288]{2,1,0:T(8,128)(2,1)S(1)}, u32[]{:S(2)}, u32[]{:S(2)}) %all-to-all-start.8) | async-done | bytes 147488 | tf_op jit(solution)/shard_map/all_to_all | solution.py:63
  265.2 6.9 %all-to-all-start.6 = ((bf16[16,16,1152]{2,1,0:T(8,128)(2,1)}), bf16[16,16,1152]{2,1,0:T(8,128)(2,1)S(1)}, u32[]{:S(2)}, u32[]{:S(2)}) async-start(bf16[16,16,1152]{2,1,0:T(8,128)(2,1)} %bitcast.50), calls=%async_computation.6 | async-start | bytes 1179648 | tf_op jit(solution)/shard_map/all_to_all | solution.py:69
  273.0 8.4 %all-to-all-done.6 = bf16[16,16,1152]{2,1,0:T(8,128)(2,1)S(1)} async-done(((bf16[16,16,1152]{2,1,0:T(8,128)(2,1)}), bf16[16,16,1152]{2,1,0:T(8,128)(2,1)S(1)}, u32[]{:S(2)}, u32[]{:S(2)}) %all-to-all-start.6) | async-done | bytes 589856 | tf_op jit(solution)/shard_map/all_to_all | solution.py:69
  281.8 1.0 fusion.7
  283.5 3.3 %all-to-all-start.7 = ((bf16[4,16,1152]{2,1,0:T(8,128)(2,1)}), bf16[4,16,1152]{2,1,0:T(8,128)(2,1)S(1)}, u32[]{:S(2)}, u32[]{:S(2)}) async-start(bf16[4,16,1152]{2,1,0:T(8,128)(2,1)} %broadcast_in_dim.25), calls=%async_computation.7 | async-start | bytes 294912 | tf_op jit(solution)/shard_map/all_to_all | solution.py:63
  286.8 0.9 subtract_multiply_fusion
  287.7 8.2 %all-to-all-done.7 = bf16[4,16,1152]{2,1,0:T(8,128)(2,1)S(1)} async-done(((bf16[4,16,1152]{2,1,0:T(8,128)(2,1)}), bf16[4,16,1152]{2,1,0:T(8,128)(2,1)S(1)}, u32[]{:S(2)}, u32[]{:S(2)}) %all-to-all-start.7) | async-done | bytes 147488 | tf_op jit(solution)/shard_map/all_to_all | solution.py:63
  (116 shorter events, 8.7 us)
Async XLA Ops:
  7.2 16.7 %copy-start = (bf16[288,1152]{1,0:T(8,128)(2,1)S(1)}, bf16[288,1152]{1,0:T(8,128)(2,1)}, u32[]{:S(2)}) copy-start(bf16[288,1152]{1,0:T(8,128)(2,1)} %param.25) | copy-start | bytes 1990660
  7.2 14.0 %copy-start.8 = (f32[1152]{0:T(1024)S(1)}, f32[1152]{0:T(1024)}, u32[]{:S(2)}) copy-start(f32[1152]{0:T(1024)} %param.18) | copy-start | bytes 13828
  7.2 14.3 %copy-start.9 = (f32[1152]{0:T(1024)S(1)}, f32[1152]{0:T(1024)}, u32[]{:S(2)}) copy-start(f32[1152]{0:T(1024)} %param.17) | copy-start | bytes 13828
  10.4 34.4 %all-to-all-start = ((bf16[64,2,680]{2,1,0:T(2,128)(2,1)}), bf16[64,2,680]{2,1,0:T(2,128)(2,1)S(1)}, u32[]{:S(2)}, u32[]{:S(2)}) async-start(bf16[64,2,680]{2,1,0:T(2,128)(2,1)} %reshape.264), calls=%async_computation | async-start | bytes 393216 | tf_op jit(solution)/shard_map/all_to_all | solution.py:130
  23.9 2.3 copy-start.14
  23.9 1.3 copy-start.1
  23.9 2.2 copy-start.7
  46.8 50.7 %all-to-all-start.1 = ((bf16[8,72,544]{2,1,0:T(8,128)(2,1)}), bf16[8,72,544]{2,1,0:T(8,128)(2,1)S(1)}, u32[]{:S(2)}, u32[]{:S(2)}) async-start(bf16[8,72,544]{2,1,0:T(8,128)(2,1)} %broadcast_in_dim.22), calls=%async_computation.1 | async-start | bytes 1474560 | tf_op jit(solution)/shard_map/all_to_all | solution.py:63
  57.1 0.9 copy-start.12
  97.5 2.0 copy-start.3
  97.5 2.0 copy-start.5
  99.5 1.6 copy-start.18
  101.1 22.9 %copy-start.10 = (f32[1152]{0:T(1024)S(1)}, f32[1152]{0:T(1024)}, u32[]{:S(2)}) copy-start(f32[1152]{0:T(1024)} %param.22) | copy-start | bytes 13828
  101.1 23.2 %copy-start.11 = (f32[1152]{0:T(1024)S(1)}, f32[1152]{0:T(1024)}, u32[]{:S(2)}) copy-start(f32[1152]{0:T(1024)} %param.26) | copy-start | bytes 13828
  101.1 31.2 %all-to-all-start.2 = ((bf16[16,16,1152]{2,1,0:T(8,128)(2,1)}), bf16[16,16,1152]{2,1,0:T(8,128)(2,1)S(1)}, u32[]{:S(2)}, u32[]{:S(2)}) async-start(bf16[16,16,1152]{2,1,0:T(8,128)(2,1)} %bitcast.49), calls=%async_computation.2 | async-start | bytes 1179648 | tf_op jit(solution)/shard_map/all_to_all | solution.py:69
  109.6 66.3 %all-gather.2.cloned.1.call-start = ((), (), s32[]{:S(2)}) async-start(), calls=%async_computation.10 | async-start | bytes 1327104 | tf_op jit(solution)/shard_map/all_gather | solution.py:159
  110.9 13.8 %collective-permute-start.2 = (bf16[64,1152]{1,0:T(8,128)(2,1)S(1)}, bf16[64,1152]{1,0:T(8,128)(2,1)S(1)}, u32[]{:S(2)}, u32[]{:S(2)}) collective-permute-start(bf16[64,1152]{1,0:T(8,128)(2,1)S(1)} %convolution_convert_fusion.4), channel_id=1, source_target_pairs={{0,3},{1,0},{2,1},{3,2},{4,7},{5,4},{6,5},{7,6},{8,11},{9,8},{10,9... | collective-permute-start | bytes 442376 | tf_op jit(solution)/shard_map/ppermute | solution.py:78
  115.5 15.9 %collective-permute-start.1 = (bf16[64,1152]{1,0:T(8,128)(2,1)S(1)}, bf16[64,1152]{1,0:T(8,128)(2,1)S(1)}, u32[]{:S(2)}, u32[]{:S(2)}) collective-permute-start(bf16[64,1152]{1,0:T(8,128)(2,1)S(1)} %convolution_convert_fusion.4), channel_id=1, source_target_pairs={{0,2},{1,3},{2,0},{3,1},{4,6},{5,7},{6,4},{7,5},{8,10},{9,11},{10,... | collective-permute-start | bytes 442376 | tf_op jit(solution)/shard_map/ppermute | solution.py:78
  120.6 10.7 %collective-permute-start = (bf16[64,1152]{1,0:T(8,128)(2,1)S(1)}, bf16[64,1152]{1,0:T(8,128)(2,1)S(1)}, u32[]{:S(2)}, u32[]{:S(2)}) collective-permute-start(bf16[64,1152]{1,0:T(8,128)(2,1)S(1)} %convolution_convert_fusion.4), channel_id=1, source_target_pairs={{0,1},{1,2},{2,3},{3,0},{4,5},{5,6},{6,7},{7,4},{8,9},{9,10},{10,1... | collective-permute-start | bytes 442376 | tf_op jit(solution)/shard_map/ppermute | solution.py:78
  133.5 42.4 %all-to-all-start.3 = ((bf16[16,16,1152]{2,1,0:T(8,128)(2,1)}), bf16[16,16,1152]{2,1,0:T(8,128)(2,1)S(1)}, u32[]{:S(2)}, u32[]{:S(2)}) async-start(bf16[16,16,1152]{2,1,0:T(8,128)(2,1)} %broadcast_in_dim.23), calls=%async_computation.3 | async-start | bytes 1179648 | tf_op jit(solution)/shard_map/all_to_all | solution.py:63
  175.9 2.0 copy-start.2
  179.3 15.1 %all-to-all-start.4 = ((bf16[16,16,1152]{2,1,0:T(8,128)(2,1)}), bf16[16,16,1152]{2,1,0:T(8,128)(2,1)S(1)}, u32[]{:S(2)}, u32[]{:S(2)}) async-start(bf16[16,16,1152]{2,1,0:T(8,128)(2,1)} %bitcast.17), calls=%async_computation.4 | async-start | bytes 1179648 | tf_op jit(solution)/shard_map/all_to_all | solution.py:69
  185.0 43.4 %reduce-scatter.2.cloned.1.call-start = ((), (), s32[]{:S(2)}) async-start(), calls=%async_computation.11 | async-start | bytes 1327104 | tf_op jit(solution)/shard_map/reduce_scatter | solution.py:181
  194.7 53.1 %copy-start.16 = (f32[16]{0:T(128)}, f32[16]{0:T(128)S(1)}, u32[]{:S(2)}) copy-start(f32[16]{0:T(128)S(1)} %multiply_reduce_fusion.4) | copy-start | bytes 196
  195.6 54.7 %all-to-all-start.5 = ((bf16[16,16,1152]{2,1,0:T(8,128)(2,1)}), bf16[16,16,1152]{2,1,0:T(8,128)(2,1)}, u32[]{:S(2)}, u32[]{:S(2)}) async-start(bf16[16,16,1152]{2,1,0:T(8,128)(2,1)} %broadcast_in_dim.24), calls=%async_computation.5 | async-start | bytes 1179648 | tf_op jit(solution)/shard_map/all_to_all | solution.py:63
  228.4 16.3 %collective-permute-start.5 = (bf16[64,1152]{1,0:T(8,128)(2,1)}, bf16[64,1152]{1,0:T(8,128)(2,1)S(1)}, u32[]{:S(2)}, u32[]{:S(2)}) collective-permute-start(bf16[64,1152]{1,0:T(8,128)(2,1)} %reduce-scatter.2.cloned.1.call-done), channel_id=1, source_target_pairs={{0,3},{1,0},{2,1},{3,2},{4,7},{5,4},{6,5},{7,6},{8,11},{9,8},{10,9... | collective-permute-start | bytes 442376 | tf_op jit(solution)/shard_map/ppermute | solution.py:78
  233.9 11.9 %collective-permute-start.4 = (bf16[64,1152]{1,0:T(8,128)(2,1)}, bf16[64,1152]{1,0:T(8,128)(2,1)S(1)}, u32[]{:S(2)}, u32[]{:S(2)}) collective-permute-start(bf16[64,1152]{1,0:T(8,128)(2,1)} %reduce-scatter.2.cloned.1.call-done), channel_id=1, source_target_pairs={{0,2},{1,3},{2,0},{3,1},{4,6},{5,7},{6,4},{7,5},{8,10},{9,11},{10,... | collective-permute-start | bytes 442376 | tf_op jit(solution)/shard_map/ppermute | solution.py:78
  238.1 9.7 %collective-permute-start.3 = (bf16[64,1152]{1,0:T(8,128)(2,1)}, bf16[64,1152]{1,0:T(8,128)(2,1)S(1)}, u32[]{:S(2)}, u32[]{:S(2)}) collective-permute-start(bf16[64,1152]{1,0:T(8,128)(2,1)} %reduce-scatter.2.cloned.1.call-done), channel_id=1, source_target_pairs={{0,1},{1,2},{2,3},{3,0},{4,5},{5,6},{6,7},{7,4},{8,9},{9,10},{10,1... | collective-permute-start | bytes 442376 | tf_op jit(solution)/shard_map/ppermute | solution.py:78
  248.9 7.6 %copy-start.4 = (bf16[576,544]{1,0:T(8,128)(2,1)S(1)}, bf16[576,544]{1,0:T(8,128)(2,1)}, u32[]{:S(2)}) copy-start(bf16[576,544]{1,0:T(8,128)(2,1)} %copy-done.3) | copy-start | bytes 1880068
  248.9 7.6 %copy-start.6 = (bf16[8,72,544]{2,1,0:T(8,128)(2,1)S(1)}, bf16[8,72,544]{2,1,0:T(8,128)(2,1)}, u32[]{:S(2)}) copy-start(bf16[8,72,544]{2,1,0:T(8,128)(2,1)} %copy-done.5) | copy-start | bytes 1880068
  251.0 14.2 %all-to-all-start.8 = ((bf16[4,64,288]{2,1,0:T(8,128)(2,1)}), bf16[4,64,288]{2,1,0:T(8,128)(2,1)S(1)}, u32[]{:S(2)}, u32[]{:S(2)}) async-start(bf16[4,64,288]{2,1,0:T(8,128)(2,1)} %broadcast_in_dim.26), calls=%async_computation.9 | async-start | bytes 393216 | tf_op jit(solution)/shard_map/all_to_all | solution.py:63
  265.2 16.3 %all-to-all-start.6 = ((bf16[16,16,1152]{2,1,0:T(8,128)(2,1)}), bf16[16,16,1152]{2,1,0:T(8,128)(2,1)S(1)}, u32[]{:S(2)}, u32[]{:S(2)}) async-start(bf16[16,16,1152]{2,1,0:T(8,128)(2,1)} %bitcast.50), calls=%async_computation.6 | async-start | bytes 1179648 | tf_op jit(solution)/shard_map/all_to_all | solution.py:69
  272.0 0.8 copy-start.13
  272.4 9.1 %copy-start.15 = (f32[16]{0:T(128)S(1)}, f32[16]{0:T(128)}, u32[]{:S(2)}) copy-start(f32[16]{0:T(128)} %copy-done.14) | copy-start | bytes 196
  272.4 9.3 %copy-start.17 = (f32[16]{0:T(128)S(1)}, f32[16]{0:T(128)}, u32[]{:S(2)}) copy-start(f32[16]{0:T(128)} %copy-done.16) | copy-start | bytes 196
  283.5 12.4 %all-to-all-start.7 = ((bf16[4,16,1152]{2,1,0:T(8,128)(2,1)}), bf16[4,16,1152]{2,1,0:T(8,128)(2,1)S(1)}, u32[]{:S(2)}, u32[]{:S(2)}) async-start(bf16[4,16,1152]{2,1,0:T(8,128)(2,1)} %broadcast_in_dim.25), calls=%async_computation.7 | async-start | bytes 294912 | tf_op jit(solution)/shard_map/all_to_all | solution.py:63
Sparse Core Ops, SparseCore 0:
  132.4 43.3 all-gather.1
  188.7 39.6 reduce-scatter.1

commit v2 on v1

--- a/solution.py
+++ b/solution.py
@@ -8,7 +8,8 @@
 cubic_coef = 0.044715
 low = jnp.bfloat16
 DP = ("ylo", "x", "z", "core")
-GROUP = ("ylo", "x", "core")
+GROUP = ("x", "ylo", "core")
+IMAGES = ("z", "ylo")
 
 
 def gelu_parts(preact):
@@ -69,14 +70,22 @@
     return jnp.sum(lax.all_to_all(slots, axes, 0, 0, tiled=True).astype(jnp.float32), axis=0)
 
 
-def tensor_total(partial):
-    count = lax.axis_size("tensor")
-    sent = partial.astype(low)
+def passed(block, axis, step):
+    count = lax.axis_size(axis)
+    return lax.ppermute(block, axis, [(i, (i + step) % count) for i in range(count)])
+
+
+def together(*values):
+    return lax.optimization_barrier(values)
+
+
+def tensor_total(sent, earlier):
+    got = [passed(sent, "tensor", step) for step in range(1, lax.axis_size("tensor"))]
+    got, earlier = lax.optimization_barrier((got, earlier))
     total = sent.astype(jnp.float32)
-    for step in range(1, count):
-        turn = [(i, (i + step) % count) for i in range(count)]
-        total = total + lax.ppermute(sent, "tensor", turn).astype(jnp.float32)
-    return total
+    for part in got:
+        total = total + part.astype(jnp.float32)
+    return (total, earlier)
 
 
 def per_device(
@@ -100,8 +109,6 @@
     tensor_count = lax.axis_size("tensor")
     group_count = lax.axis_size(GROUP)
     tensor_rank = lax.axis_index("tensor")
-    z_rank = lax.axis_index("z")
-    group_rank = lax.axis_index(GROUP)
     block_rows, width = image_pooled.shape
     own_rows = block_rows // tensor_count
     pairs_total = block_rows * lax.axis_size(DP)
@@ -111,7 +118,7 @@
 
     def turned(vec):
         return (
-            vec.reshape(ylo_count, x_count, z_count, core_count * slab).transpose(0, 2, 1, 3).reshape(width)
+            vec.reshape(ylo_count, x_count, z_count, core_count * slab).transpose(2, 1, 0, 3).reshape(width)
         )
 
     source_of = turned(jnp.arange(width, dtype=jnp.int32))
@@ -128,69 +135,105 @@
     slots = jnp.broadcast_to(slots[:, None], (group_count, tensor_count) + slots.shape[1:])
     slots = slots.reshape((group_count * tensor_count,) + slots.shape[2:])
     got = lax.all_to_all(slots, GROUP + ("tensor",), 0, 0, tiled=True)
-    got = got.reshape(ylo_count, x_count * core_count, tensor_count, 2 * slab + 2, chunk)
-    up_bias = (
-        got[0, 0, :, 2 * slab].astype(jnp.float32) + got[0, 0, :, 2 * slab + 1].astype(jnp.float32)
-    ).reshape(hidden_mine)
-    both = got[:, :, :, : 2 * slab].reshape(ylo_count, x_count * core_count, tensor_count, 2, slab, chunk)
-    both = both.transpose(0, 1, 4, 3, 2, 5).reshape(
-        ylo_count, x_count * core_count * slab, 2 * hidden_mine
-    )
-    first = spread(both[0], "z").reshape(-1, 2 * hidden_mine)
-    second = lax.all_gather(both[1], "z", axis=0, tiled=True)
-    weights = jnp.concatenate([first, second], axis=0)
-    up_mine = weights[:, :hidden_mine]
-    down_mine = weights[:, hidden_mine:]
-
     gain_turned = turned(image_norm_gain)
     image_own = lax.dynamic_slice_in_dim(image_pooled, tensor_rank * own_rows, own_rows, 0)
     image_own = mm(image_own, turn)
     image_normed, image_inverse = norm_stats(image_own)
     ready = (image_normed * gain_turned + turned(image_norm_bias)).astype(low)
-    ready_all = lax.all_gather(ready, GROUP, axis=0, tiled=True)
-
-    text_normed, text_inverse = norm_stats(text_pooled.astype(jnp.float32))
+    ready_all = lax.all_gather(ready, ("ylo", "core"), axis=0, tiled=True)
+    ready_all, got = lax.optimization_barrier((ready_all, got))
+    ready_all = lax.all_gather(ready_all, "x", axis=0, tiled=True)
+
+    text_float, got = lax.optimization_barrier((text_pooled, got))
+    got = got.reshape(group_count, tensor_count, 2 * slab + 2, chunk)
+    up_bias = (
+        got[0, :, 2 * slab].astype(jnp.float32) + got[0, :, 2 * slab + 1].astype(jnp.float32)
+    ).reshape(hidden_mine)
+    both = got[:, :, : 2 * slab].reshape(group_count, tensor_count, 2, slab, chunk)
+    both = both.transpose(0, 3, 2, 1, 4).reshape(group_count * slab, 2 * hidden_mine)
+    weights = spread(both, "z").reshape(width, 2 * hidden_mine)
+
+    text_normed, text_inverse = norm_stats(text_float.astype(jnp.float32))
     text_ready = (text_normed * text_norm_gain + text_norm_bias).astype(low)
     head_rows = text_head.shape[0]
     text_columns = lax.dynamic_slice_in_dim(text_ready, tensor_rank * head_rows, head_rows, 1)
     head_turned = mm(text_head, turn).astype(low)
-    text_sum = tensor_total(mm(text_columns, head_turned)) + turned(text_head_bias)
-    text_unit, text_invnorm = unit_rows(text_sum)
-    text_all = lax.all_gather(text_unit.astype(low), "z", axis=0, tiled=True)
+    text_sent = mm(text_columns, head_turned).astype(low)
+    text_total, ready_all = tensor_total(text_sent, ready_all)
+    text_unit, text_invnorm = unit_rows(text_total + turned(text_head_bias))
+    text_emb = text_unit.astype(low)
+    ready_all, text_emb = together(ready_all, text_emb)
+    up_mine = weights[:, :hidden_mine]
+    down_mine = weights[:, hidden_mine:]
 
     hidden_pre = mm(ready_all, up_mine) + up_bias
     hidden_act, hidden_slope = gelu_parts(hidden_pre)
-    image_sum = sum_slots(mm_nt(hidden_act.astype(low), down_mine), GROUP)
+    image_part = mm_nt(hidden_act.astype(low), down_mine).astype(low)
+    image_part, text_emb = together(image_part, text_emb)
+    x_steps = range(1, lax.axis_size("x"))
+    image_sum, text_near = together(
+        sum_slots(image_part, GROUP),
+        [text_emb] + [passed(text_emb, "x", step) for step in x_steps],
+    )
+    text_near = jnp.concatenate(text_near, axis=0)
     image_sum = image_sum + image_own + turned(image_down_bias)
     image_unit, image_invnorm = unit_rows(image_sum)
-    image_all = spread(image_unit.astype(low), GROUP).reshape(-1, width)
+    image_all, text_far = together(
+        spread(image_unit.astype(low), IMAGES).reshape(-1, width), passed(text_near, "core", 1)
+    )
+    text_all = jnp.concatenate([text_near, text_far], axis=0)
 
     scale_value = jnp.exp(log_scale[0])
     factor = loss_scale[0] * scale_value / pairs_total
     scores = mm_nt(image_all, text_all)
-    image_at = lax.broadcasted_iota(jnp.int32, scores.shape, 0) - group_rank * own_rows
-    text_at = lax.broadcasted_iota(jnp.int32, scores.shape, 1) - (
-        z_rank * block_rows + tensor_rank * own_rows
-    )
+    image_at = lax.broadcasted_iota(jnp.int32, scores.shape, 0) - lax.axis_index(IMAGES) * own_rows
+    text_at = lax.broadcasted_iota(jnp.int32, scores.shape, 1) - tensor_rank * own_rows
     same = (image_at == text_at) & (image_at >= 0) & (image_at < own_rows)
     pair_coef = (
         factor * (jax.nn.sigmoid(scale_value * scores + logit_shift[0]) - same.astype(jnp.float32))
     ).astype(low)
-    image_unit_back = sum_slots(mm(pair_coef, text_all), GROUP)
     text_part = mm_tn(pair_coef, image_all).astype(low)
-    text_unit_back = tensor_total(lax.psum_scatter(text_part, "z", scatter_dimension=0, tiled=True))
+    pair_coef, text_part = together(pair_coef, text_part)
+    near_rows = text_near.shape[0]
+    text_part = text_part[:near_rows].astype(jnp.float32) + passed(
+        text_part[near_rows:], "core", 1
+    ).astype(jnp.float32)
+    text_part = text_part.astype(low).reshape(-1, block_rows, width)
+    image_unit_back, text_got = together(
+        sum_slots(mm(pair_coef, text_all), IMAGES),
+        [text_part[0]] + [passed(text_part[step], "x", -step) for step in x_steps],
+    )
+    text_unit_back = sum(part.astype(jnp.float32) for part in text_got).astype(low)
 
     image_back = unit_backward(image_unit_back, image_unit, image_invnorm)
     back_all = spread(image_back.astype(low), GROUP).reshape(-1, width)
     pre_back = (mm(back_all, down_mine) * hidden_slope).astype(low)
-    ready_back = sum_slots(mm_nt(pre_back, up_mine), GROUP)
+    ready_sent = mm_nt(pre_back, up_mine).astype(low)
+    text_unit_back, ready_sent = tensor_total(text_unit_back, ready_sent)
+    ready_back = sum_slots(ready_sent, GROUP)
     image_grad = image_back + norm_backward(ready_back, image_normed, image_inverse, gain_turned)
-    image_grad = mm_nt(image_grad.astype(low), turn).astype(low)
-    image_grad = spread(image_grad, "tensor").reshape(block_rows, width).astype(jnp.float32)
+    image_low = mm_nt(image_grad.astype(low), turn).astype(low)
 
     text_back = unit_backward(text_unit_back, text_unit, text_invnorm)
-    column_part = mm_nt(text_back.astype(low), head_turned).astype(low)
-    column_back = spread(column_part, "tensor").transpose(1, 0, 2).reshape(block_rows, width)
+    lanes = 128
+    head_tiles = -(-head_rows // lanes)
+    head_padded = jnp.pad(head_turned, ((0, head_tiles * lanes - head_rows), (0, 0)))
+    column_part = mm_nt(text_back.astype(low), head_padded).astype(low)
+
+    tiles = width // lanes
+    last = jnp.concatenate(
+        [
+            image_low.reshape(own_rows, tiles, lanes).transpose(1, 0, 2).reshape(-1, lanes),
+            column_part.reshape(block_rows, head_tiles, lanes).transpose(1, 0, 2).reshape(-1, lanes),
+        ],
+        axis=0,
+    )
+    last = spread(last, "tensor")
+    image_grad = last[:, : tiles * own_rows].reshape(tensor_count, tiles, own_rows, lanes)
+    image_grad = image_grad.transpose(0, 2, 1, 3).reshape(block_rows, width).astype(jnp.float32)
+    column_back = last[:, tiles * own_rows :].reshape(tensor_count, head_tiles, block_rows, lanes)
+    column_back = column_back.transpose(2, 0, 1, 3).reshape(block_rows, tensor_count, head_tiles * lanes)
+    column_back = column_back[:, :, :head_rows].reshape(block_rows, width)
     text_grad = norm_backward(column_back.astype(jnp.float32), text_normed, text_inverse, text_norm_gain)
     return (image_grad, text_grad)
 

time: 306 us -> 231 us (0.75)
  waiting for transfers between devices: 99.4 us -> 57 us
  blocking collectives: 57.5 us -> 19.2 us
  between operations: 16.7 us -> 3.62 us
  starting transfers between devices: 93.3 us -> 103 us
  local copies, waits for them, and re-layouts: 9.62 us -> 19.1 us
  matrix products: 18.8 us -> 15.6 us
    all_gather x2, blocking collectives: 57.5 us -> 19.2 us  [the longest x1 13.7 us: per_device(): ready_all = lax.all_gather(ready_all, 'x', axis=0, tiled=True)]
    all_gather x1 -> x0, waiting for transfers between devices: 31.6 us -> none  [per_device(): text_all = lax.all_gather(text_unit.astype(low), 'z', axis=0, tiled=True)]
    reduce_scatter x1 -> x0, waiting for transfers between devices: 26.3 us -> none  [per_device(): lax.psum_scatter(text_part, 'z', scatter_dimension=0, tiled=True)]
    ppermute x6 -> x14, starting transfers between devices: 27.1 us -> 52.9 us  [passed(): lax.ppermute(block, axis, [(i, (i + step) % count) for i in range(count)])]
    all_to_all x5 -> x4, waiting for transfers between devices: 13.4 us -> 31.6 us  [spread(): return lax.all_to_all(slots, axes, 0, 0, tiled=True)]
    all_to_all x5 -> x4, starting transfers between devices: 34.3 us -> 25.4 us  [spread(): return lax.all_to_all(slots, axes, 0, 0, tiled=True)]
    all_to_all x3, starting transfers between devices: 21.1 us -> 14.1 us  [sum_slots(): lax.all_to_all(slots, axes, 0, 0, tiled=True).astype(jnp.float32)]
    unnamed x40 -> x86, local copies, waits for them, and re-layouts: 1.9 us -> 8.83 us
  transfers between devices with their start and end apart: 17 -> 22, of which waited for: 10 -> 8; matrix products, arithmetic and copies ran while one was open for 7% -> 9% of each run, Pallas kernels for 0% -> 0%
where the time goes in v2:
time: 231 us; the launch traced here: 227 us
  starting transfers between devices  103 us (45%)
  waiting for transfers between devices  57 us (25%)
  blocking collectives  19.2 us (8%)
  local copies, waits for them, and re-layouts  19.1 us (8%)
  matrix products  15.6 us (7%)
  other arithmetic  9.18 us (4%)
  between operations  3.62 us (2%)
    ppermute x14, starting transfers between devices, passed(): lax.ppermute(block, axis, [(i, (i + step) % count) for i in range(count)])  52.9 us
    all_to_all x4, waiting for transfers between devices, spread(): return lax.all_to_all(slots, axes, 0, 0, tiled=True)  31.6 us
    all_to_all x4, starting transfers between devices, spread(): return lax.all_to_all(slots, axes, 0, 0, tiled=True)  25.4 us
    all_to_all x3, waiting for transfers between devices, sum_slots(): lax.all_to_all(slots, axes, 0, 0, tiled=True).astype(jnp.float32)  15.8 us
    all_to_all x3, starting transfers between devices, sum_slots(): lax.all_to_all(slots, axes, 0, 0, tiled=True).astype(jnp.float32)  14.1 us
    all_gather x1, blocking collectives, per_device(): ready_all = lax.all_gather(ready_all, 'x', axis=0, tiled=True)  13.7 us
    all_to_all x1, starting transfers between devices, per_device(): got = lax.all_to_all(slots, GROUP + ('tensor',), 0, 0, tiled=True)  10.9 us
    ppermute x14, waiting for transfers between devices, passed(): lax.ppermute(block, axis, [(i, (i + step) % count) for i in range(count)])  9.6 us
  transfers between devices with their start and end apart: 22, of which 8 were waited for; matrix products, arithmetic and copies ran while one was open for 9% of the time, Pallas kernels for 0%

profile of v2, /device:TPU:6, one launch (start us, length us, event | category | flops | bytes accessed | tf_op | source)
XLA Modules:
  0.0 226.9 jit_solution(6501181715128598283)
XLA Ops:
  2.6 1.3 reshape.296
  3.8 10.9 %all-to-all-start = ((bf16[64,2,680]{2,1,0:T(2,128)(2,1)}), bf16[64,2,680]{2,1,0:T(2,128)(2,1)S(1)}, u32[]{:S(2)}, u32[]{:S(2)}) async-start(bf16[64,2,680]{2,1,0:T(2,128)(2,1)} %reshape.296), calls=%async_computation | async-start | bytes 393216 | tf_op jit(solution)/shard_map/all_to_all | solution.py:137
  15.0 1.9 fusion.85
  19.0 5.5 %all_gather.6 = bf16[64,1152]{1,0:T(8,128)(2,1)S(1)} all-gather(bf16[16,1152]{1,0:T(8,128)(2,1)S(1)} %add_convert_fusion.3), channel_id=1, replica_groups=mesh['ylo'=2,'x'=4,'z'=8,'core'=2,'tensor'=4] {'ylo','core'}, dimensions={0}, use_global_device_ids=true | all-gather | bytes 184320 | tf_op jit(solution)/shard_map/all_gather | solution.py:143
  24.4 1.3 fusion.6
  27.3 1.2 broadcast_in_dim.20
  28.5 10.3 %all-to-all-start.1 = ((bf16[8,144,544]{2,1,0:T(8,128)(2,1)}), bf16[8,144,544]{2,1,0:T(8,128)(2,1)}, u32[]{:S(2)}, u32[]{:S(2)}) async-start(bf16[8,144,544]{2,1,0:T(8,128)(2,1)} %broadcast_in_dim.20), calls=%async_computation.1 | async-start | bytes 2949120 | tf_op jit(solution)/shard_map/all_to_all | solution.py:64
  39.9 4.4 %collective-permute-start = (bf16[64,1152]{1,0:T(8,128)(2,1)S(1)}, bf16[64,1152]{1,0:T(8,128)(2,1)S(1)}, u32[]{:S(2)}, u32[]{:S(2)}) collective-permute-start(bf16[64,1152]{1,0:T(8,128)(2,1)S(1)} %convolution_convert_fusion.4), channel_id=1, source_target_pairs={{0,1},{1,2},{2,3},{3,0},{4,5},{5,6},{6,7},{7,4},{8,9},{9,10},{10,1... | collective-permute-start | bytes 442376 | tf_op jit(solution)/shard_map/ppermute | solution.py:75
  44.3 5.4 %collective-permute-start.1 = (bf16[64,1152]{1,0:T(8,128)(2,1)S(1)}, bf16[64,1152]{1,0:T(8,128)(2,1)S(1)}, u32[]{:S(2)}, u32[]{:S(2)}) collective-permute-start(bf16[64,1152]{1,0:T(8,128)(2,1)S(1)} %convolution_convert_fusion.4), channel_id=1, source_target_pairs={{0,2},{1,3},{2,0},{3,1},{4,6},{5,7},{6,4},{7,5},{8,10},{9,11},{10,... | collective-permute-start | bytes 442376 | tf_op jit(solution)/shard_map/ppermute | solution.py:75
  49.7 5.5 %collective-permute-start.2 = (bf16[64,1152]{1,0:T(8,128)(2,1)S(1)}, bf16[64,1152]{1,0:T(8,128)(2,1)S(1)}, u32[]{:S(2)}, u32[]{:S(2)}) collective-permute-start(bf16[64,1152]{1,0:T(8,128)(2,1)S(1)} %convolution_convert_fusion.4), channel_id=1, source_target_pairs={{0,3},{1,0},{2,1},{3,2},{4,7},{5,4},{6,5},{7,6},{8,11},{9,8},{10,9... | collective-permute-start | bytes 442376 | tf_op jit(solution)/shard_map/ppermute | solution.py:75
  55.2 13.7 %all_gather.7 = bf16[256,1152]{1,0:T(8,128)(2,1)S(1)} all-gather(bf16[64,1152]{1,0:T(8,128)(2,1)S(1)} %all_gather.6), channel_id=1, replica_groups=mesh['ylo'=2,'x'=4,'z'=8,'core'=2,'tensor'=4] {'x'}, dimensions={0}, use_global_device_ids=true | all-gather | bytes 737280 | tf_op jit(solution)/shard_map/all_gather | solution.py:145
  69.3 8.1 %all-to-all-done.1 = bf16[8,144,544]{2,1,0:T(8,128)(2,1)} async-done(((bf16[8,144,544]{2,1,0:T(8,128)(2,1)}), bf16[8,144,544]{2,1,0:T(8,128)(2,1)}, u32[]{:S(2)}, u32[]{:S(2)}) %all-to-all-start.1) | async-done | bytes 1253408 | tf_op jit(solution)/shard_map/all_to_all | solution.py:64
  77.3 1.6 convolution_add_fusion
  79.7 2.8 %convolution_convert_fusion.3 = bf16[256,1152]{1,0:T(8,128)(2,1)} fusion(bf16[1152,544]{1,0:T(8,128)(2,1)} %bitcast.11, f32[256,272]{0,1:T(8,128)S(1)} %convolution_add_fusion), kind=kOutput, calls=%fused_computation.11 | convolution fusion | flops 161353728 | bytes 1753088 | tf_op jit(solution)/shard_map/dot_general | solution.py:54
  82.5 5.7 %all-to-all-start.2 = ((bf16[16,16,1152]{2,1,0:T(8,128)(2,1)}), bf16[16,16,1152]{2,1,0:T(8,128)(2,1)S(1)}, u32[]{:S(2)}, u32[]{:S(2)}) async-start(bf16[16,16,1152]{2,1,0:T(8,128)(2,1)} %bitcast.12), calls=%async_computation.2 | async-start | bytes 1179648 | tf_op jit(solution)/shard_map/all_to_all | solution.py:70
  89.3 2.0 collective-permute-start.3
  91.3 4.7 %collective-permute-start.4 = (bf16[64,1152]{1,0:T(8,128)(2,1)S(1)}, bf16[64,1152]{1,0:T(8,128)(2,1)S(1)}, u32[]{:S(2)}, u32[]{:S(2)}) collective-permute-start(bf16[64,1152]{1,0:T(8,128)(2,1)S(1)} %multiply_convert_fusion.2), channel_id=1, source_target_pairs={{0,128},{64,192},{128,0},{192,64},{1,129},{65,193},{129,1},{193,65... | collective-permute-start | bytes 442376 | tf_op jit(solution)/shard_map/ppermute | solution.py:75
  96.1 1.9 collective-permute-start.5
  101.0 3.5 %collective-permute-done.5 = bf16[64,1152]{1,0:T(8,128)(2,1)S(1)} collective-permute-done((bf16[64,1152]{1,0:T(8,128)(2,1)S(1)}, bf16[64,1152]{1,0:T(8,128)(2,1)S(1)}, u32[]{:S(2)}, u32[]{:S(2)}) %collective-permute-start.5) | collective-permute-done | bytes 147488 | tf_op jit(solution)/shard_map/ppermute | solution.py:75
  105.6 3.6 %all-to-all-start.3 = ((bf16[16,16,1152]{2,1,0:T(8,128)(2,1)}), bf16[16,16,1152]{2,1,0:T(8,128)(2,1)S(1)}, u32[]{:S(2)}, u32[]{:S(2)}) async-start(bf16[16,16,1152]{2,1,0:T(8,128)(2,1)} %broadcast_in_dim.21), calls=%async_computation.3 | async-start | bytes 1179648 | tf_op jit(solution)/shard_map/all_to_all | solution.py:64
  109.3 1.9 collective-permute-start.6
  112.2 0.9 constant_dynamic-update-slice_fusion.3
  113.1 0.9 constant_dynamic-update-slice_fusion.2
  114.0 0.9 constant_dynamic-update-slice_fusion.1
  115.0 11.7 %all-to-all-done.3 = bf16[16,16,1152]{2,1,0:T(8,128)(2,1)S(1)} async-done(((bf16[16,16,1152]{2,1,0:T(8,128)(2,1)}), bf16[16,16,1152]{2,1,0:T(8,128)(2,1)S(1)}, u32[]{:S(2)}, u32[]{:S(2)}) %all-to-all-start.3) | async-done | bytes 589856 | tf_op jit(solution)/shard_map/all_to_all | solution.py:64
  126.7 1.1 constant_dynamic-update-slice_fusion
  127.8 1.0 copy-done.2
  131.0 2.1 collective-permute-start.7
  133.1 1.3 convolution_convert_fusion.1
  134.4 3.6 %all-to-all-start.4 = ((bf16[16,16,1152]{2,1,0:T(8,128)(2,1)}), bf16[16,16,1152]{2,1,0:T(8,128)(2,1)S(1)}, u32[]{:S(2)}, u32[]{:S(2)}) async-start(bf16[16,16,1152]{2,1,0:T(8,128)(2,1)} %bitcast.58), calls=%async_computation.4 | async-start | bytes 1179648 | tf_op jit(solution)/shard_map/all_to_all | solution.py:70
  138.0 1.2 add_convert_fusion
  139.3 3.9 %collective-permute-start.10 = (bf16[64,1152]{1,0:T(8,128)(2,1)S(1)}, bf16[64,1152]{1,0:T(8,128)(2,1)S(1)}, u32[]{:S(2)}, u32[]{:S(2)}) collective-permute-start(bf16[64,1152]{1,0:T(8,128)(2,1)S(1)} %get-tuple-element.70), channel_id=1, source_target_pairs={{0,64},{64,128},{128,192},{192,0},{1,65},{65,129},{129,193},{193,1... | collective-permute-start | bytes 442376 | tf_op jit(solution)/shard_map/ppermute | solution.py:75
  143.2 2.0 collective-permute-start.8
  145.1 4.9 %collective-permute-start.9 = (bf16[64,1152]{1,0:T(8,128)(2,1)S(1)}, bf16[64,1152]{1,0:T(8,128)(2,1)}, u32[]{:S(2)}, u32[]{:S(2)}) collective-permute-start(bf16[64,1152]{1,0:T(8,128)(2,1)S(1)} %get-tuple-element.71), channel_id=1, source_target_pairs={{0,128},{64,192},{128,0},{192,64},{1,129},{65,193},{129,1},{193,65... | collective-permute-start | bytes 442376 | tf_op jit(solution)/shard_map/ppermute | solution.py:75
  150.0 7.2 %all-to-all-done.4 = bf16[16,16,1152]{2,1,0:T(8,128)(2,1)S(1)} async-done(((bf16[16,16,1152]{2,1,0:T(8,128)(2,1)}), bf16[16,16,1152]{2,1,0:T(8,128)(2,1)S(1)}, u32[]{:S(2)}, u32[]{:S(2)}) %all-to-all-start.4) | async-done | bytes 589856 | tf_op jit(solution)/shard_map/all_to_all | solution.py:70
  158.9 5.7 %all-to-all-start.5 = ((bf16[16,16,1152]{2,1,0:T(8,128)(2,1)}), bf16[16,16,1152]{2,1,0:T(8,128)(2,1)S(1)}, u32[]{:S(2)}, u32[]{:S(2)}) async-start(bf16[16,16,1152]{2,1,0:T(8,128)(2,1)} %broadcast_in_dim.22), calls=%async_computation.5 | async-start | bytes 1179648 | tf_op jit(solution)/shard_map/all_to_all | solution.py:64
  164.7 1.1 add_convert_fusion.1
  165.7 4.3 %collective-permute-start.11 = (bf16[64,1152]{1,0:T(8,128)(2,1)S(1)}, bf16[64,1152]{1,0:T(8,128)(2,1)S(1)}, u32[]{:S(2)}, u32[]{:S(2)}) collective-permute-start(bf16[64,1152]{1,0:T(8,128)(2,1)S(1)} %add_convert_fusion.1), channel_id=1, source_target_pairs={{0,1},{1,2},{2,3},{3,0},{4,5},{5,6},{6,7},{7,4},{8,9},{9,10},{10,1... | collective-permute-start | bytes 442376 | tf_op jit(solution)/shard_map/ppermute | solution.py:75
  170.0 4.6 %collective-permute-start.12 = (bf16[64,1152]{1,0:T(8,128)(2,1)S(1)}, bf16[64,1152]{1,0:T(8,128)(2,1)S(1)}, u32[]{:S(2)}, u32[]{:S(2)}) collective-permute-start(bf16[64,1152]{1,0:T(8,128)(2,1)S(1)} %add_convert_fusion.1), channel_id=1, source_target_pairs={{0,2},{1,3},{2,0},{3,1},{4,6},{5,7},{6,4},{7,5},{8,10},{9,11},{10,... | collective-permute-start | bytes 442376 | tf_op jit(solution)/shard_map/ppermute | solution.py:75
  174.6 5.5 %collective-permute-start.13 = (bf16[64,1152]{1,0:T(8,128)(2,1)S(1)}, bf16[64,1152]{1,0:T(8,128)(2,1)S(1)}, u32[]{:S(2)}, u32[]{:S(2)}) collective-permute-start(bf16[64,1152]{1,0:T(8,128)(2,1)S(1)} %add_convert_fusion.1), channel_id=1, source_target_pairs={{0,3},{1,0},{2,1},{3,2},{4,7},{5,4},{6,5},{7,6},{8,11},{9,8},{10,9... | collective-permute-start | bytes 442376 | tf_op jit(solution)/shard_map/ppermute | solution.py:75
  180.1 3.8 %convolution_convert_fusion.2 = bf16[256,1152]{1,0:T(8,128)(2,1)} fusion(bf16[256,1152]{1,0:T(8,128)(2,1)S(1)} %bitcast.68, bf16[1152,544]{1,0:T(8,128)(2,1)} %bitcast.11, f32[256,272]{0,1:T(8,128)S(1)} %copy-done.13), kind=kOutput, calls=%fused_computation.10 | convolution fusion | flops 322482176 | bytes 3227648 | tf_op jit(solution)/shard_map/dot_general | solution.py:54
  184.0 3.7 %collective-permute-done.12 = bf16[64,1152]{1,0:T(8,128)(2,1)S(1)} collective-permute-done((bf16[64,1152]{1,0:T(8,128)(2,1)S(1)}, bf16[64,1152]{1,0:T(8,128)(2,1)S(1)}, u32[]{:S(2)}, u32[]{:S(2)}) %collective-permute-start.12) | collective-permute-done | bytes 147488 | tf_op jit(solution)/shard_map/ppermute | solution.py:75
  187.6 2.4 %collective-permute-done.13 = bf16[64,1152]{1,0:T(8,128)(2,1)S(1)} collective-permute-done((bf16[64,1152]{1,0:T(8,128)(2,1)S(1)}, bf16[64,1152]{1,0:T(8,128)(2,1)S(1)}, u32[]{:S(2)}, u32[]{:S(2)}) %collective-permute-start.13) | collective-permute-done | bytes 147488 | tf_op jit(solution)/shard_map/ppermute | solution.py:75
  190.1 4.8 %all-to-all-start.6 = ((bf16[16,16,1152]{2,1,0:T(8,128)(2,1)}), bf16[16,16,1152]{2,1,0:T(8,128)(2,1)S(1)}, u32[]{:S(2)}, u32[]{:S(2)}) async-start(bf16[16,16,1152]{2,1,0:T(8,128)(2,1)} %bitcast.18), calls=%async_computation.6 | async-start | bytes 1179648 | tf_op jit(solution)/shard_map/all_to_all | solution.py:70
  195.5 8.6 %all-to-all-done.6 = bf16[16,16,1152]{2,1,0:T(8,128)(2,1)S(1)} async-done(((bf16[16,16,1152]{2,1,0:T(8,128)(2,1)}), bf16[16,16,1152]{2,1,0:T(8,128)(2,1)S(1)}, u32[]{:S(2)}, u32[]{:S(2)}) %all-to-all-start.6) | async-done | bytes 589856 | tf_op jit(solution)/shard_map/all_to_all | solution.py:70
  204.5 1.0 fusion.7
  206.4 5.8 %all-to-all-start.7 = ((bf16[4,336,128]{2,1,0:T(8,128)(2,1)}), bf16[4,336,128]{2,1,0:T(8,128)(2,1)S(1)}, u32[]{:S(2)}, u32[]{:S(2)}) async-start(bf16[4,336,128]{2,1,0:T(8,128)(2,1)} %broadcast_in_dim.23), calls=%async_computation.7 | async-start | bytes 688128 | tf_op jit(solution)/shard_map/all_to_all | solution.py:64
  212.2 11.8 %all-to-all-done.7 = bf16[4,336,128]{2,1,0:T(8,128)(2,1)S(1)} async-done(((bf16[4,336,128]{2,1,0:T(8,128)(2,1)}), bf16[4,336,128]{2,1,0:T(8,128)(2,1)S(1)}, u32[]{:S(2)}, u32[]{:S(2)}) %all-to-all-start.7) | async-done | bytes 344096 | tf_op jit(solution)/shard_map/all_to_all | solution.py:64
  (182 shorter events, 20.5 us)
Async XLA Ops:
  0.6 23.8 %copy-start = (bf16[288,1152]{1,0:T(8,128)(2,1)S(1)}, bf16[288,1152]{1,0:T(8,128)(2,1)}, u32[]{:S(2)}) copy-start(bf16[288,1152]{1,0:T(8,128)(2,1)} %param.25) | copy-start | bytes 1990660
  2.5 14.5 %copy-start.18 = (f32[1152]{0:T(1024)S(1)}, f32[1152]{0:T(1024)}, u32[]{:S(2)}) copy-start(f32[1152]{0:T(1024)} %param.17) | copy-start | bytes 13828
  3.8 13.6 %copy-start.19 = (f32[1152]{0:T(1024)S(1)}, f32[1152]{0:T(1024)}, u32[]{:S(2)}) copy-start(f32[1152]{0:T(1024)} %param.18) | copy-start | bytes 13828
  3.8 14.0 %copy-start.17 = (f32[1152]{0:T(1024)S(1)}, f32[1152]{0:T(1024)}, u32[]{:S(2)}) copy-start(f32[1152]{0:T(1024)} %param.23) | copy-start | bytes 13828
  3.8 14.8 %copy-start.20 = (f32[1152]{0:T(1024)S(1)}, f32[1152]{0:T(1024)}, u32[]{:S(2)}) copy-start(f32[1152]{0:T(1024)} %param.26) | copy-start | bytes 13828
  3.8 21.9 %all-to-all-start = ((bf16[64,2,680]{2,1,0:T(2,128)(2,1)}), bf16[64,2,680]{2,1,0:T(2,128)(2,1)S(1)}, u32[]{:S(2)}, u32[]{:S(2)}) async-start(bf16[64,2,680]{2,1,0:T(2,128)(2,1)} %reshape.296), calls=%async_computation | async-start | bytes 393216 | tf_op jit(solution)/shard_map/all_to_all | solution.py:137
  14.9 10.8 %copy-start.22 = (s32[1152]{0:T(1024)}, s32[1152]{0:T(1024)S(1)}, u32[]{:S(2)}) copy-start(s32[1152]{0:T(1024)S(1)} %reshape.263) | copy-start | bytes 13828
  16.8 87.7 %copy-start.5 = (f32[16,1152]{1,0:T(8,128)}, f32[16,1152]{1,0:T(8,128)S(1)}, u32[]{:S(2)}) copy-start(f32[16,1152]{1,0:T(8,128)S(1)} %get-tuple-element.75) | copy-start | bytes 221188
  26.4 12.4 %copy-start.24 = (f32[64]{0:T(128)}, f32[64]{0:T(128)S(1)}, u32[]{:S(2)}) copy-start(f32[64]{0:T(128)S(1)} %broadcast_multiply_fusion.2) | copy-start | bytes 772
  28.5 48.8 %all-to-all-start.1 = ((bf16[8,144,544]{2,1,0:T(8,128)(2,1)}), bf16[8,144,544]{2,1,0:T(8,128)(2,1)}, u32[]{:S(2)}, u32[]{:S(2)}) async-start(bf16[8,144,544]{2,1,0:T(8,128)(2,1)} %broadcast_in_dim.20), calls=%async_computation.1 | async-start | bytes 2949120 | tf_op jit(solution)/shard_map/all_to_all | solution.py:64
  39.9 29.1 %collective-permute-start = (bf16[64,1152]{1,0:T(8,128)(2,1)S(1)}, bf16[64,1152]{1,0:T(8,128)(2,1)S(1)}, u32[]{:S(2)}, u32[]{:S(2)}) collective-permute-start(bf16[64,1152]{1,0:T(8,128)(2,1)S(1)} %convolution_convert_fusion.4), channel_id=1, source_target_pairs={{0,1},{1,2},{2,3},{3,0},{4,5},{5,6},{6,7},{7,4},{8,9},{9,10},{10,1... | collective-permute-start | bytes 442376 | tf_op jit(solution)/shard_map/ppermute | solution.py:75
  44.3 24.7 %collective-permute-start.1 = (bf16[64,1152]{1,0:T(8,128)(2,1)S(1)}, bf16[64,1152]{1,0:T(8,128)(2,1)S(1)}, u32[]{:S(2)}, u32[]{:S(2)}) collective-permute-start(bf16[64,1152]{1,0:T(8,128)(2,1)S(1)} %convolution_convert_fusion.4), channel_id=1, source_target_pairs={{0,2},{1,3},{2,0},{3,1},{4,6},{5,7},{6,4},{7,5},{8,10},{9,11},{10,... | collective-permute-start | bytes 442376 | tf_op jit(solution)/shard_map/ppermute | solution.py:75
  49.7 19.3 %collective-permute-start.2 = (bf16[64,1152]{1,0:T(8,128)(2,1)S(1)}, bf16[64,1152]{1,0:T(8,128)(2,1)S(1)}, u32[]{:S(2)}, u32[]{:S(2)}) collective-permute-start(bf16[64,1152]{1,0:T(8,128)(2,1)S(1)} %convolution_convert_fusion.4), channel_id=1, source_target_pairs={{0,3},{1,0},{2,1},{3,2},{4,7},{5,4},{6,5},{7,6},{8,11},{9,8},{10,9... | collective-permute-start | bytes 442376 | tf_op jit(solution)/shard_map/ppermute | solution.py:75
  69.1 13.3 %copy-start.30 = (f32[64]{0:T(128)}, f32[64]{0:T(128)S(1)}, u32[]{:S(2)}) copy-start(f32[64]{0:T(128)S(1)} %add_rsqrt_fusion.1) | copy-start | bytes 772
  69.2 40.0 %copy-start.4 = (bf16[64,1152]{1,0:T(8,128)(2,1)}, bf16[64,1152]{1,0:T(8,128)(2,1)S(1)}, u32[]{:S(2)}) copy-start(bf16[64,1152]{1,0:T(8,128)(2,1)S(1)} %multiply_convert_fusion.2) | copy-start | bytes 442372
  79.7 18.9 %copy-start.21 = (f32[1152]{0:T(1024)S(1)}, f32[1152]{0:T(1024)}, u32[]{:S(2)}) copy-start(f32[1152]{0:T(1024)} %param.22) | copy-start | bytes 13828
  82.5 18.4 %all-to-all-start.2 = ((bf16[16,16,1152]{2,1,0:T(8,128)(2,1)}), bf16[16,16,1152]{2,1,0:T(8,128)(2,1)S(1)}, u32[]{:S(2)}, u32[]{:S(2)}) async-start(bf16[16,16,1152]{2,1,0:T(8,128)(2,1)} %bitcast.12), calls=%async_computation.2 | async-start | bytes 1179648 | tf_op jit(solution)/shard_map/all_to_all | solution.py:70
  89.3 11.7 %collective-permute-start.3 = (bf16[64,1152]{1,0:T(8,128)(2,1)S(1)}, bf16[64,1152]{1,0:T(8,128)(2,1)S(1)}, u32[]{:S(2)}, u32[]{:S(2)}) collective-permute-start(bf16[64,1152]{1,0:T(8,128)(2,1)S(1)} %multiply_convert_fusion.2), channel_id=1, source_target_pairs={{0,64},{64,128},{128,192},{192,0},{1,65},{65,129},{129,193},{193,1... | collective-permute-start | bytes 442376 | tf_op jit(solution)/shard_map/ppermute | solution.py:75
  91.3 9.7 %collective-permute-start.4 = (bf16[64,1152]{1,0:T(8,128)(2,1)S(1)}, bf16[64,1152]{1,0:T(8,128)(2,1)S(1)}, u32[]{:S(2)}, u32[]{:S(2)}) collective-permute-start(bf16[64,1152]{1,0:T(8,128)(2,1)S(1)} %multiply_convert_fusion.2), channel_id=1, source_target_pairs={{0,128},{64,192},{128,0},{192,64},{1,129},{65,193},{129,1},{193,65... | collective-permute-start | bytes 442376 | tf_op jit(solution)/shard_map/ppermute | solution.py:75
  96.1 8.4 %collective-permute-start.5 = (bf16[64,1152]{1,0:T(8,128)(2,1)S(1)}, bf16[64,1152]{1,0:T(8,128)(2,1)S(1)}, u32[]{:S(2)}, u32[]{:S(2)}) collective-permute-start(bf16[64,1152]{1,0:T(8,128)(2,1)S(1)} %multiply_convert_fusion.2), channel_id=1, source_target_pairs={{0,192},{64,0},{128,64},{192,128},{1,193},{65,1},{129,65},{193,129... | collective-permute-start | bytes 442376 | tf_op jit(solution)/shard_map/ppermute | solution.py:75
  101.0 8.3 %copy-start.9 = (bf16[64,1152]{1,0:T(8,128)(2,1)}, bf16[64,1152]{1,0:T(8,128)(2,1)S(1)}, u32[]{:S(2)}) copy-start(bf16[64,1152]{1,0:T(8,128)(2,1)S(1)} %collective-permute-done.3) | copy-start | bytes 442372
  101.0 8.3 %copy-start.10 = (bf16[64,1152]{1,0:T(8,128)(2,1)}, bf16[64,1152]{1,0:T(8,128)(2,1)S(1)}, u32[]{:S(2)}) copy-start(bf16[64,1152]{1,0:T(8,128)(2,1)S(1)} %collective-permute-done.4) | copy-start | bytes 442372
  104.5 4.8 %copy-start.11 = (bf16[64,1152]{1,0:T(8,128)(2,1)}, bf16[64,1152]{1,0:T(8,128)(2,1)S(1)}, u32[]{:S(2)}) copy-start(bf16[64,1152]{1,0:T(8,128)(2,1)S(1)} %collective-permute-done.5) | copy-start | bytes 442372
  104.7 4.6 %copy-start.28 = (f32[16]{0:T(128)}, f32[16]{0:T(128)S(1)}, u32[]{:S(2)}) copy-start(f32[16]{0:T(128)S(1)} %add_rsqrt_fusion) | copy-start | bytes 196
  105.6 21.1 %all-to-all-start.3 = ((bf16[16,16,1152]{2,1,0:T(8,128)(2,1)}), bf16[16,16,1152]{2,1,0:T(8,128)(2,1)S(1)}, u32[]{:S(2)}, u32[]{:S(2)}) async-start(bf16[16,16,1152]{2,1,0:T(8,128)(2,1)} %broadcast_in_dim.21), calls=%async_computation.3 | async-start | bytes 1179648 | tf_op jit(solution)/shard_map/all_to_all | solution.py:64
  109.3 5.6 %collective-permute-start.6 = (bf16[256,1152]{1,0:T(8,128)(2,1)S(1)}, bf16[256,1152]{1,0:T(8,128)(2,1)}, u32[]{:S(2)}, u32[]{:S(2)}) collective-permute-start(bf16[256,1152]{1,0:T(8,128)(2,1)S(1)} %pad_maximum_fusion), channel_id=1, source_target_pairs={{0,4},{4,0},{1,5},{5,1},{2,6},{6,2},{3,7},{7,3},{8,12},{12,8},{9,1... | collective-permute-start | bytes 1769480 | tf_op jit(solution)/shard_map/ppermute | solution.py:75
  126.7 2.2 copy-start.39
  129.6 3.5 %copy-start.3 = (bf16[512,1152]{1,0:T(8,128)(2,1)S(1)}, bf16[512,1152]{1,0:T(8,128)(2,1)}, u32[]{:S(2)}) copy-start(bf16[512,1152]{1,0:T(8,128)(2,1)} %copy-done.2) | copy-start | bytes 3538948
  131.0 7.0 %collective-permute-start.7 = (bf16[256,1152]{1,0:T(8,128)(2,1)}, bf16[256,1152]{1,0:T(8,128)(2,1)}, u32[]{:S(2)}, u32[]{:S(2)}) collective-permute-start(bf16[256,1152]{1,0:T(8,128)(2,1)} %slice.52), channel_id=1, source_target_pairs={{0,4},{4,0},{1,5},{5,1},{2,6},{6,2},{3,7},{7,3},{8,12},{12,8},{9,1... | collective-permute-start | bytes 1769480 | tf_op jit(solution)/shard_map/ppermute | solution.py:75
  134.4 22.8 %all-to-all-start.4 = ((bf16[16,16,1152]{2,1,0:T(8,128)(2,1)}), bf16[16,16,1152]{2,1,0:T(8,128)(2,1)S(1)}, u32[]{:S(2)}, u32[]{:S(2)}) async-start(bf16[16,16,1152]{2,1,0:T(8,128)(2,1)} %bitcast.58), calls=%async_computation.4 | async-start | bytes 1179648 | tf_op jit(solution)/shard_map/all_to_all | solution.py:70
  139.2 18.1 %copy-start.8 = (f32[16,1152]{1,0:T(8,128)S(1)}, f32[16,1152]{1,0:T(8,128)}, u32[]{:S(2)}) copy-start(f32[16,1152]{1,0:T(8,128)} %copy-done.7) | copy-start | bytes 221188
  139.2 18.1 %copy-start.29 = (f32[16]{0:T(128)S(1)}, f32[16]{0:T(128)}, u32[]{:S(2)}) copy-start(f32[16]{0:T(128)} %copy-done.28) | copy-start | bytes 196
  139.3 18.0 %collective-permute-start.10 = (bf16[64,1152]{1,0:T(8,128)(2,1)S(1)}, bf16[64,1152]{1,0:T(8,128)(2,1)S(1)}, u32[]{:S(2)}, u32[]{:S(2)}) collective-permute-start(bf16[64,1152]{1,0:T(8,128)(2,1)S(1)} %get-tuple-element.70), channel_id=1, source_target_pairs={{0,64},{64,128},{128,192},{192,0},{1,65},{65,129},{129,193},{193,1... | collective-permute-start | bytes 442376 | tf_op jit(solution)/shard_map/ppermute | solution.py:75
  143.2 14.1 %collective-permute-start.8 = (bf16[64,1152]{1,0:T(8,128)(2,1)S(1)}, bf16[64,1152]{1,0:T(8,128)(2,1)S(1)}, u32[]{:S(2)}, u32[]{:S(2)}) collective-permute-start(bf16[64,1152]{1,0:T(8,128)(2,1)S(1)} %get-tuple-element.72), channel_id=1, source_target_pairs={{0,192},{64,0},{128,64},{192,128},{1,193},{65,1},{129,65},{193,129... | collective-permute-start | bytes 442376 | tf_op jit(solution)/shard_map/ppermute | solution.py:75
  145.1 12.2 %collective-permute-start.9 = (bf16[64,1152]{1,0:T(8,128)(2,1)S(1)}, bf16[64,1152]{1,0:T(8,128)(2,1)}, u32[]{:S(2)}, u32[]{:S(2)}) collective-permute-start(bf16[64,1152]{1,0:T(8,128)(2,1)S(1)} %get-tuple-element.71), channel_id=1, source_target_pairs={{0,128},{64,192},{128,0},{192,64},{1,129},{65,193},{129,1},{193,65... | collective-permute-start | bytes 442376 | tf_op jit(solution)/shard_map/ppermute | solution.py:75
  158.1 6.6 %copy-start.15 = (bf16[64,1152]{1,0:T(8,128)(2,1)S(1)}, bf16[64,1152]{1,0:T(8,128)(2,1)}, u32[]{:S(2)}) copy-start(bf16[64,1152]{1,0:T(8,128)(2,1)} %copy-done.14) | copy-start | bytes 442372
  158.1 22.0 %copy-start.13 = (f32[256,272]{0,1:T(8,128)S(1)}, f32[256,272]{0,1:T(8,128)}, u32[]{:S(2)}) copy-start(f32[256,272]{0,1:T(8,128)} %copy-done.12) | copy-start | bytes 835588
  158.9 21.2 %all-to-all-start.5 = ((bf16[16,16,1152]{2,1,0:T(8,128)(2,1)}), bf16[16,16,1152]{2,1,0:T(8,128)(2,1)S(1)}, u32[]{:S(2)}, u32[]{:S(2)}) async-start(bf16[16,16,1152]{2,1,0:T(8,128)(2,1)} %broadcast_in_dim.22), calls=%async_computation.5 | async-start | bytes 1179648 | tf_op jit(solution)/shard_map/all_to_all | solution.py:64
  165.7 18.2 %collective-permute-start.11 = (bf16[64,1152]{1,0:T(8,128)(2,1)S(1)}, bf16[64,1152]{1,0:T(8,128)(2,1)S(1)}, u32[]{:S(2)}, u32[]{:S(2)}) collective-permute-start(bf16[64,1152]{1,0:T(8,128)(2,1)S(1)} %add_convert_fusion.1), channel_id=1, source_target_pairs={{0,1},{1,2},{2,3},{3,0},{4,5},{5,6},{6,7},{7,4},{8,9},{9,10},{10,1... | collective-permute-start | bytes 442376 | tf_op jit(solution)/shard_map/ppermute | solution.py:75
  170.0 17.6 %collective-permute-start.12 = (bf16[64,1152]{1,0:T(8,128)(2,1)S(1)}, bf16[64,1152]{1,0:T(8,128)(2,1)S(1)}, u32[]{:S(2)}, u32[]{:S(2)}) collective-permute-start(bf16[64,1152]{1,0:T(8,128)(2,1)S(1)} %add_convert_fusion.1), channel_id=1, source_target_pairs={{0,2},{1,3},{2,0},{3,1},{4,6},{5,7},{6,4},{7,5},{8,10},{9,11},{10,... | collective-permute-start | bytes 442376 | tf_op jit(solution)/shard_map/ppermute | solution.py:75
  174.6 15.4 %collective-permute-start.13 = (bf16[64,1152]{1,0:T(8,128)(2,1)S(1)}, bf16[64,1152]{1,0:T(8,128)(2,1)S(1)}, u32[]{:S(2)}, u32[]{:S(2)}) collective-permute-start(bf16[64,1152]{1,0:T(8,128)(2,1)S(1)} %add_convert_fusion.1), channel_id=1, source_target_pairs={{0,3},{1,0},{2,1},{3,2},{4,7},{5,4},{6,5},{7,6},{8,11},{9,8},{10,9... | collective-permute-start | bytes 442376 | tf_op jit(solution)/shard_map/ppermute | solution.py:75
  184.0 10.9 %copy-start.31 = (f32[64]{0:T(128)S(1)}, f32[64]{0:T(128)}, u32[]{:S(2)}) copy-start(f32[64]{0:T(128)} %copy-done.30) | copy-start | bytes 772
  190.1 14.1 %all-to-all-start.6 = ((bf16[16,16,1152]{2,1,0:T(8,128)(2,1)}), bf16[16,16,1152]{2,1,0:T(8,128)(2,1)S(1)}, u32[]{:S(2)}, u32[]{:S(2)}) async-start(bf16[16,16,1152]{2,1,0:T(8,128)(2,1)} %bitcast.18), calls=%async_computation.6 | async-start | bytes 1179648 | tf_op jit(solution)/shard_map/all_to_all | solution.py:70
  195.1 9.2 %copy-start.6 = (f32[16,1152]{1,0:T(8,128)S(1)}, f32[16,1152]{1,0:T(8,128)}, u32[]{:S(2)}) copy-start(f32[16,1152]{1,0:T(8,128)} %copy-done.5) | copy-start | bytes 221188
  195.1 9.2 %copy-start.27 = (f32[16]{0:T(128)S(1)}, f32[16]{0:T(128)}, u32[]{:S(2)}) copy-start(f32[16]{0:T(128)} %copy-done.26) | copy-start | bytes 196
  195.1 9.2 %copy-start.35 = (f32[16]{0:T(128)S(1)}, f32[16]{0:T(128)}, u32[]{:S(2)}) copy-start(f32[16]{0:T(128)} %copy-done.34) | copy-start | bytes 196
  195.1 9.4 %copy-start.23 = (s32[1152]{0:T(1024)S(1)}, s32[1152]{0:T(1024)}, u32[]{:S(2)}) copy-start(s32[1152]{0:T(1024)} %copy-done.22) | copy-start | bytes 13828
  206.4 17.6 %all-to-all-start.7 = ((bf16[4,336,128]{2,1,0:T(8,128)(2,1)}), bf16[4,336,128]{2,1,0:T(8,128)(2,1)S(1)}, u32[]{:S(2)}, u32[]{:S(2)}) async-start(bf16[4,336,128]{2,1,0:T(8,128)(2,1)} %broadcast_in_dim.23), calls=%async_computation.7 | async-start | bytes 688128 | tf_op jit(solution)/shard_map/all_to_all | solution.py:64
  (14 other events, 16.3 us)

commit v3 on v2

--- a/solution.py
+++ b/solution.py
@@ -1,6 +1,8 @@
 import jax
 import jax.numpy as jnp
 from jax import lax
+from jax.experimental import pallas as pl
+from jax.experimental.pallas import tpu as pltpu
 from jax.sharding import Mesh, PartitionSpec as P
 
 epsilon = 1e-06
@@ -64,10 +66,14 @@
     return lax.all_to_all(slots, axes, 0, 0, tiled=True)
 
 
-def sum_slots(partial, axes):
+def swap_slots(partial, axes):
     count = lax.axis_size(axes)
     slots = partial.astype(low).reshape(count, partial.shape[0] // count, partial.shape[1])
-    return jnp.sum(lax.all_to_all(slots, axes, 0, 0, tiled=True).astype(jnp.float32), axis=0)
+    return lax.all_to_all(slots, axes, 0, 0, tiled=True)
+
+
+def sum_slots(partial, axes):
+    return jnp.sum(swap_slots(partial, axes).astype(jnp.float32), axis=0)
 
 
 def passed(block, axis, step):
@@ -86,6 +92,61 @@
     for part in got:
         total = total + part.astype(jnp.float32)
     return (total, earlier)
+
+
+def pair_kernel(number_ref, place_ref, image_ref, near_ref, far_ref, near_coef_ref, far_coef_ref, part_ref):
+    scale_value, shift, factor = (number_ref[i] for i in range(3))
+    image = image_ref[...]
+    near = near_ref[...]
+    far = far_ref[...]
+    chance = jax.nn.sigmoid(scale_value * mm_nt(image, near) + shift)
+    image_at = lax.broadcasted_iota(jnp.int32, chance.shape, 0) - place_ref[0]
+    text_at = lax.broadcasted_iota(jnp.int32, chance.shape, 1) - place_ref[1]
+    same = (image_at == text_at) & (image_at >= 0) & (image_at < place_ref[2])
+    near_coef = (factor * (chance - same.astype(jnp.float32))).astype(low)
+    far_coef = (factor * jax.nn.sigmoid(scale_value * mm_nt(image, far) + shift)).astype(low)
+    near_coef_ref[...] = near_coef
+    far_coef_ref[...] = far_coef
+    part_ref[...] = (mm(near_coef, near) + mm(far_coef, far)).astype(low)
+
+
+def back_kernel(got_ref, unit_ref, inverse_ref, back_ref, slots_ref):
+    upstream = jnp.sum(got_ref[...].astype(jnp.float32), axis=0)
+    back = unit_backward(upstream, unit_ref[...], inverse_ref[...])
+    back_ref[...] = back
+    sent = back.astype(low)
+    for slot in range(slots_ref.shape[0]):
+        slots_ref[slot] = sent
+
+
+def back_slots(got, unit, inverse, count):
+    vmem = pl.BlockSpec(memory_space=pltpu.VMEM)
+    return pl.pallas_call(
+        back_kernel,
+        out_shape=(
+            jax.ShapeDtypeStruct(unit.shape, jnp.float32),
+            jax.ShapeDtypeStruct((count,) + unit.shape, low),
+        ),
+        in_specs=[vmem, vmem, vmem],
+        out_specs=(vmem, vmem),
+        compiler_params=pltpu.CompilerParams(vmem_limit_bytes=10 * 1024 * 1024),
+    )(got, unit, inverse)
+
+
+def pairs(numbers, places, image, near, far):
+    rows, width = image.shape
+    vmem, smem = pl.BlockSpec(memory_space=pltpu.VMEM), pl.BlockSpec(memory_space=pltpu.SMEM)
+    return pl.pallas_call(
+        pair_kernel,
+        out_shape=(
+            jax.ShapeDtypeStruct((rows, near.shape[0]), low),
+            jax.ShapeDtypeStruct((rows, far.shape[0]), low),
+            jax.ShapeDtypeStruct((rows, width), low),
+        ),
+        in_specs=[smem, smem, vmem, vmem, vmem],
+        out_specs=(vmem, vmem, vmem),
+        compiler_params=pltpu.CompilerParams(vmem_limit_bytes=10 * 1024 * 1024),
+    )(numbers, places, image, near, far)
 
 
 def per_device(
@@ -169,11 +230,11 @@
     hidden_pre = mm(ready_all, up_mine) + up_bias
     hidden_act, hidden_slope = gelu_parts(hidden_pre)
     image_part = mm_nt(hidden_act.astype(low), down_mine).astype(low)
-    image_part, text_emb = together(image_part, text_emb)
     x_steps = range(1, lax.axis_size("x"))
+    image_part, text_emb, text_got = together(image_part, text_emb, passed(text_emb, "x", 2))
     image_sum, text_near = together(
         sum_slots(image_part, GROUP),
-        [text_emb] + [passed(text_emb, "x", step) for step in x_steps],
+        [text_emb, passed(text_emb, "x", 1), text_got, passed(text_emb, "x", 3)],
     )
     text_near = jnp.concatenate(text_near, axis=0)
     image_sum = image_sum + image_own + turned(image_down_bias)
@@ -181,36 +242,30 @@
     image_all, text_far = together(
         spread(image_unit.astype(low), IMAGES).reshape(-1, width), passed(text_near, "core", 1)
     )
-    text_all = jnp.concatenate([text_near, text_far], axis=0)
 
     scale_value = jnp.exp(log_scale[0])
-    factor = loss_scale[0] * scale_value / pairs_total
-    scores = mm_nt(image_all, text_all)
-    image_at = lax.broadcasted_iota(jnp.int32, scores.shape, 0) - lax.axis_index(IMAGES) * own_rows
-    text_at = lax.broadcasted_iota(jnp.int32, scores.shape, 1) - tensor_rank * own_rows
-    same = (image_at == text_at) & (image_at >= 0) & (image_at < own_rows)
-    pair_coef = (
-        factor * (jax.nn.sigmoid(scale_value * scores + logit_shift[0]) - same.astype(jnp.float32))
-    ).astype(low)
-    text_part = mm_tn(pair_coef, image_all).astype(low)
-    pair_coef, text_part = together(pair_coef, text_part)
-    near_rows = text_near.shape[0]
-    text_part = text_part[:near_rows].astype(jnp.float32) + passed(
-        text_part[near_rows:], "core", 1
-    ).astype(jnp.float32)
+    numbers = jnp.stack([scale_value, logit_shift[0], loss_scale[0] * scale_value / pairs_total])
+    places = jnp.stack(
+        [lax.axis_index(IMAGES) * own_rows, tensor_rank * own_rows, jnp.int32(own_rows)]
+    ).astype(jnp.int32)
+    near_coef, far_coef, image_part = pairs(numbers, places, image_all, text_near, text_far)
+    far_part = mm_tn(far_coef, image_all).astype(low)
+    text_part = mm_tn(near_coef, image_all) + passed(far_part, "core", 1).astype(jnp.float32)
     text_part = text_part.astype(low).reshape(-1, block_rows, width)
-    image_unit_back, text_got = together(
-        sum_slots(mm(pair_coef, text_all), IMAGES),
+    image_got, text_got = together(
+        swap_slots(image_part, IMAGES),
         [text_part[0]] + [passed(text_part[step], "x", -step) for step in x_steps],
     )
     text_unit_back = sum(part.astype(jnp.float32) for part in text_got).astype(low)
 
-    image_back = unit_backward(image_unit_back, image_unit, image_invnorm)
-    back_all = spread(image_back.astype(low), GROUP).reshape(-1, width)
+    image_back, slots = back_slots(image_got, image_unit, image_invnorm, group_count)
+    back_all = lax.all_to_all(slots, GROUP, 0, 0, tiled=True).reshape(-1, width)
     pre_back = (mm(back_all, down_mine) * hidden_slope).astype(low)
     ready_sent = mm_nt(pre_back, up_mine).astype(low)
-    text_unit_back, ready_sent = tensor_total(text_unit_back, ready_sent)
-    ready_back = sum_slots(ready_sent, GROUP)
+    text_got = [text_unit_back] + [passed(text_unit_back, "tensor", step) for step in (1, 2, 3)]
+    ready_sent, text_got[1], text_got[3] = together(ready_sent, text_got[1], text_got[3])
+    ready_back, text_got[2] = together(sum_slots(ready_sent, GROUP), text_got[2])
+    text_unit_back = sum(part.astype(jnp.float32) for part in text_got)
     image_grad = image_back + norm_backward(ready_back, image_normed, image_inverse, gain_turned)
     image_low = mm_nt(image_grad.astype(low), turn).astype(low)
 

time: 231 us -> 220 us (0.952); the launches traced: 227 us -> 219 us
  local copies, waits for them, and re-layouts: 19.1 us -> 11.6 us
  Pallas kernels: 0 us -> 3.44 us
  starting transfers between devices: 103 us -> 106 us
  other arithmetic: 9.18 us -> 6.67 us
  matrix products: 15.6 us -> 13.2 us
    all_to_all x3 -> x4, starting transfers between devices: 14.1 us -> 21.2 us  [the longest x3 15.5 us: swap_slots(): return lax.all_to_all(slots, axes, 0, 0, tiled=True)]
    unnamed x86 -> x59, local copies, waits for them, and re-layouts: 8.83 us -> 3.43 us
    pallas_call x0 -> x2, Pallas kernels: none -> 3.44 us  [the longest x1 2.41 us: pairs(): pl.pallas_call(pair_kernel, out_shape=(jax.ShapeDtypeStruct((rows, near.s...]
    ppermute x14, starting transfers between devices: 52.9 us -> 49.7 us  [passed(): lax.ppermute(block, axis, [(i, (i + step) % count) for i in range(count)])]
    ppermute x14, waiting for transfers between devices: 9.6 us -> 12.8 us  [passed(): lax.ppermute(block, axis, [(i, (i + step) % count) for i in range(count)])]
    all_to_all x4 -> x3, waiting for transfers between devices: 31.6 us -> 28.6 us  [spread(): return lax.all_to_all(slots, axes, 0, 0, tiled=True)]
    all_to_all x3 -> x4, waiting for transfers between devices: 15.8 us -> 13.5 us  [the longest x3 10.7 us: swap_slots(): return lax.all_to_all(slots, axes, 0, 0, tiled=True)]
    dot_general x5 -> x4, matrix products: 6.41 us -> 4.59 us  [mm(): return jnp.dot(a, b, preferred_element_type=jnp.float32)]
  transfers between devices with their start and end apart: 22 -> 22, of which waited for: 8 -> 11; matrix products, arithmetic and copies ran while one was open for 9% -> 8% of each run, Pallas kernels for 0% -> 0%
where the time goes in v3:
time: 220 us; the launch traced here: 219 us
  starting transfers between devices  106 us (48%)
  waiting for transfers between devices  54.9 us (25%)
  blocking collectives  19.4 us (9%)
  matrix products  13.2 us (6%)
  local copies, waits for them, and re-layouts  11.6 us (5%)
  other arithmetic  6.67 us (3%)
  Pallas kernels  3.44 us (2%)
  between operations  3.42 us (2%)
    ppermute x14, starting transfers between devices, passed(): lax.ppermute(block, axis, [(i, (i + step) % count) for i in range(count)])  49.7 us
    all_to_all x3, waiting for transfers between devices, spread(): return lax.all_to_all(slots, axes, 0, 0, tiled=True)  28.6 us
    all_to_all x3, starting transfers between devices, spread(): return lax.all_to_all(slots, axes, 0, 0, tiled=True)  24.3 us
    all_to_all x3, starting transfers between devices, swap_slots(): return lax.all_to_all(slots, axes, 0, 0, tiled=True)  15.5 us
    all_gather x1, blocking collectives, per_device(): ready_all = lax.all_gather(ready_all, 'x', axis=0, tiled=True)  13.5 us
    ppermute x14, waiting for transfers between devices, passed(): lax.ppermute(block, axis, [(i, (i + step) % count) for i in range(count)])  12.8 us
    all_to_all x1, starting transfers between devices, per_device(): got = lax.all_to_all(slots, GROUP + ('tensor',), 0, 0, tiled=True)  10.8 us
    all_to_all x3, waiting for transfers between devices, swap_slots(): return lax.all_to_all(slots, axes, 0, 0, tiled=True)  10.7 us
  transfers between devices with their start and end apart: 22, of which 11 were waited for; matrix products, arithmetic and copies ran while one was open for 8% of the time, Pallas kernels for 0%

profile of v3, /device:TPU:6, one launch (start us, length us, event | category | flops | bytes accessed | tf_op | source)
XLA Modules:
  0.0 218.6 jit_solution(16271878233837007749)
XLA Ops:
  2.6 1.3 reshape.308
  3.9 10.8 %all-to-all-start = ((bf16[64,2,680]{2,1,0:T(2,128)(2,1)}), bf16[64,2,680]{2,1,0:T(2,128)(2,1)S(1)}, u32[]{:S(2)}, u32[]{:S(2)}) async-start(bf16[64,2,680]{2,1,0:T(2,128)(2,1)} %reshape.308), calls=%async_computation | async-start | bytes 393216 | tf_op jit(solution)/shard_map/all_to_all | solution.py:198
  14.9 1.9 fusion.77
  18.9 5.9 %all_gather.6 = bf16[64,1152]{1,0:T(8,128)(2,1)} all-gather(bf16[16,1152]{1,0:T(8,128)(2,1)S(1)} %add_convert_fusion.2), channel_id=1, replica_groups=mesh['ylo'=2,'x'=4,'z'=8,'core'=2,'tensor'=4] {'ylo','core'}, dimensions={0}, use_global_device_ids=true | all-gather | bytes 184320 | tf_op jit(solution)/shard_map/all_gather | solution.py:204
  24.8 1.3 fusion.6
  27.6 1.3 broadcast_in_dim.18
  28.9 10.4 %all-to-all-start.1 = ((bf16[8,144,544]{2,1,0:T(8,128)(2,1)}), bf16[8,144,544]{2,1,0:T(8,128)(2,1)S(1)}, u32[]{:S(2)}, u32[]{:S(2)}) async-start(bf16[8,144,544]{2,1,0:T(8,128)(2,1)} %broadcast_in_dim.18), calls=%async_computation.1 | async-start | bytes 2949120 | tf_op jit(solution)/shard_map/all_to_all | solution.py:66
  39.8 4.4 %collective-permute-start = (bf16[64,1152]{1,0:T(8,128)(2,1)S(1)}, bf16[64,1152]{1,0:T(8,128)(2,1)}, u32[]{:S(2)}, u32[]{:S(2)}) collective-permute-start(bf16[64,1152]{1,0:T(8,128)(2,1)S(1)} %convolution_convert_fusion.3), channel_id=1, source_target_pairs={{0,1},{1,2},{2,3},{3,0},{4,5},{5,6},{6,7},{7,4},{8,9},{9,10},{10,1... | collective-permute-start | bytes 442376 | tf_op jit(solution)/shard_map/ppermute | solution.py:81
  44.2 5.4 %collective-permute-start.1 = (bf16[64,1152]{1,0:T(8,128)(2,1)S(1)}, bf16[64,1152]{1,0:T(8,128)(2,1)S(1)}, u32[]{:S(2)}, u32[]{:S(2)}) collective-permute-start(bf16[64,1152]{1,0:T(8,128)(2,1)S(1)} %convolution_convert_fusion.3), channel_id=1, source_target_pairs={{0,2},{1,3},{2,0},{3,1},{4,6},{5,7},{6,4},{7,5},{8,10},{9,11},{10,... | collective-permute-start | bytes 442376 | tf_op jit(solution)/shard_map/ppermute | solution.py:81
  49.6 5.5 %collective-permute-start.2 = (bf16[64,1152]{1,0:T(8,128)(2,1)S(1)}, bf16[64,1152]{1,0:T(8,128)(2,1)}, u32[]{:S(2)}, u32[]{:S(2)}) collective-permute-start(bf16[64,1152]{1,0:T(8,128)(2,1)S(1)} %convolution_convert_fusion.3), channel_id=1, source_target_pairs={{0,3},{1,0},{2,1},{3,2},{4,7},{5,4},{6,5},{7,6},{8,11},{9,8},{10,9... | collective-permute-start | bytes 442376 | tf_op jit(solution)/shard_map/ppermute | solution.py:81
  56.4 13.5 %all_gather.7 = bf16[256,1152]{1,0:T(8,128)(2,1)S(1)} all-gather(bf16[64,1152]{1,0:T(8,128)(2,1)S(1)} %copy-done.6), channel_id=1, replica_groups=mesh['ylo'=2,'x'=4,'z'=8,'core'=2,'tensor'=4] {'x'}, dimensions={0}, use_global_device_ids=true | all-gather | bytes 737280 | tf_op jit(solution)/shard_map/all_gather | solution.py:206
  70.6 1.3 multiply_reduce_fusion.3
  72.5 3.4 %collective-permute-start.3 = (bf16[64,1152]{1,0:T(8,128)(2,1)S(1)}, bf16[64,1152]{1,0:T(8,128)(2,1)S(1)}, u32[]{:S(2)}, u32[]{:S(2)}) collective-permute-start(bf16[64,1152]{1,0:T(8,128)(2,1)S(1)} %multiply_convert_fusion.2), channel_id=1, source_target_pairs={{0,128},{64,192},{128,0},{192,64},{1,129},{65,193},{129,1},{193,65... | collective-permute-start | bytes 442376 | tf_op jit(solution)/shard_map/ppermute | solution.py:81
  75.9 1.8 all-to-all-done.1
  77.7 1.1 convolution_add_fusion.1
  78.9 1.6 convolution_convert_fusion.2
  81.1 5.1 %all-to-all-start.2 = ((bf16[16,16,1152]{2,1,0:T(8,128)(2,1)}), bf16[16,16,1152]{2,1,0:T(8,128)(2,1)S(1)}, u32[]{:S(2)}, u32[]{:S(2)}) async-start(bf16[16,16,1152]{2,1,0:T(8,128)(2,1)} %bitcast.12), calls=%async_computation.2 | async-start | bytes 1179648 | tf_op jit(solution)/shard_map/all_to_all | solution.py:72
  86.2 2.0 collective-permute-start.4
  88.2 3.8 %collective-permute-start.5 = (bf16[64,1152]{1,0:T(8,128)(2,1)S(1)}, bf16[64,1152]{1,0:T(8,128)(2,1)S(1)}, u32[]{:S(2)}, u32[]{:S(2)}) collective-permute-start(bf16[64,1152]{1,0:T(8,128)(2,1)S(1)} %multiply_convert_fusion.2), channel_id=1, source_target_pairs={{0,192},{64,0},{128,64},{192,128},{1,193},{65,1},{129,65},{193,129... | collective-permute-start | bytes 442376 | tf_op jit(solution)/shard_map/ppermute | solution.py:81
  92.4 3.2 %all-to-all-done.2 = bf16[16,16,1152]{2,1,0:T(8,128)(2,1)S(1)} async-done(((bf16[16,16,1152]{2,1,0:T(8,128)(2,1)}), bf16[16,16,1152]{2,1,0:T(8,128)(2,1)S(1)}, u32[]{:S(2)}, u32[]{:S(2)}) %all-to-all-start.2) | async-done | bytes 589856 | tf_op jit(solution)/shard_map/all_to_all | solution.py:72
  95.7 2.1 collective-permute-done.4
  98.0 0.9 broadcast_in_dim.19
  98.8 7.7 %all-to-all-start.3 = ((bf16[16,16,1152]{2,1,0:T(8,128)(2,1)}), bf16[16,16,1152]{2,1,0:T(8,128)(2,1)S(1)}, u32[]{:S(2)}, u32[]{:S(2)}) async-start(bf16[16,16,1152]{2,1,0:T(8,128)(2,1)} %broadcast_in_dim.19), calls=%async_computation.3 | async-start | bytes 1179648 | tf_op jit(solution)/shard_map/all_to_all | solution.py:66
  106.7 1.9 collective-permute-start.6
  110.7 14.3 %all-to-all-done.3 = bf16[16,16,1152]{2,1,0:T(8,128)(2,1)S(1)} async-done(((bf16[16,16,1152]{2,1,0:T(8,128)(2,1)}), bf16[16,16,1152]{2,1,0:T(8,128)(2,1)S(1)}, u32[]{:S(2)}, u32[]{:S(2)}) %all-to-all-start.3) | async-done | bytes 589856 | tf_op jit(solution)/shard_map/all_to_all | solution.py:66
  125.1 2.4 %shard_map.158 = (bf16[256,256]{1,0:T(8,128)(2,1)S(1)}, bf16[256,256]{1,0:T(8,128)(2,1)S(1)}, bf16[256,1152]{1,0:T(8,128)(2,1)}) custom-call(f32[3]{0:T(128)S(1)} %pad_maximum_fusion.1.number_ref, s32[3]{0:T(128)S(1)} %pad_add_fusion.place_ref, bf16[256,1152]{1,0:T(8,128)(2,1)S(1)} %bitcast.52, ...), custom_call_target="tpu_custom_call" | custom-call | tf_op jit(solution)/shard_map/pallas_call | solution.py:139
  127.9 1.9 collective-permute-start.7
  129.8 3.8 %all-to-all-start.4 = ((bf16[16,16,1152]{2,1,0:T(8,128)(2,1)}), bf16[16,16,1152]{2,1,0:T(8,128)(2,1)S(1)}, u32[]{:S(2)}, u32[]{:S(2)}) async-start(bf16[16,16,1152]{2,1,0:T(8,128)(2,1)} %bitcast.15), calls=%async_computation.4 | async-start | bytes 1179648 | tf_op jit(solution)/shard_map/all_to_all | solution.py:72
  133.6 1.4 fusion.7
  135.1 4.4 %collective-permute-start.10 = (bf16[64,1152]{1,0:T(8,128)(2,1)S(1)}, bf16[64,1152]{1,0:T(8,128)(2,1)S(1)}, u32[]{:S(2)}, u32[]{:S(2)}) collective-permute-start(bf16[64,1152]{1,0:T(8,128)(2,1)S(1)} %get-tuple-element.80), channel_id=1, source_target_pairs={{0,64},{64,128},{128,192},{192,0},{1,65},{65,129},{129,193},{193,1... | collective-permute-start | bytes 442376 | tf_op jit(solution)/shard_map/ppermute | solution.py:81
  139.5 1.9 collective-permute-start.8
  141.4 3.7 %collective-permute-start.9 = (bf16[64,1152]{1,0:T(8,128)(2,1)S(1)}, bf16[64,1152]{1,0:T(8,128)(2,1)S(1)}, u32[]{:S(2)}, u32[]{:S(2)}) collective-permute-start(bf16[64,1152]{1,0:T(8,128)(2,1)S(1)} %get-tuple-element.81), channel_id=1, source_target_pairs={{0,128},{64,192},{128,0},{192,64},{1,129},{65,193},{129,1},{193,65... | collective-permute-start | bytes 442376 | tf_op jit(solution)/shard_map/ppermute | solution.py:81
  145.1 6.6 %collective-permute-done.8 = bf16[64,1152]{1,0:T(8,128)(2,1)S(1)} collective-permute-done((bf16[64,1152]{1,0:T(8,128)(2,1)S(1)}, bf16[64,1152]{1,0:T(8,128)(2,1)S(1)}, u32[]{:S(2)}, u32[]{:S(2)}) %collective-permute-start.8) | collective-permute-done | bytes 147488 | tf_op jit(solution)/shard_map/ppermute | solution.py:81
  151.7 0.9 all-to-all-done.4.got_ref
  152.6 1.0 shard_map.159
  153.6 5.7 %all-to-all-start.5 = ((bf16[16,16,1152]{2,1,0:T(8,128)(2,1)}), bf16[16,16,1152]{2,1,0:T(8,128)(2,1)S(1)}, u32[]{:S(2)}, u32[]{:S(2)}) async-start(bf16[16,16,1152]{2,1,0:T(8,128)(2,1)} %get-tuple-element.62), calls=%async_computation.5 | async-start | bytes 1179648 | tf_op jit(solution)/shard_map/all_to_all | solution.py:262
  159.4 1.9 collective-permute-start.11
  161.4 6.0 %collective-permute-start.12 = (bf16[64,1152]{1,0:T(8,128)(2,1)S(1)}, bf16[64,1152]{1,0:T(8,128)(2,1)S(1)}, u32[]{:S(2)}, u32[]{:S(2)}) collective-permute-start(bf16[64,1152]{1,0:T(8,128)(2,1)S(1)} %add_convert_fusion), channel_id=1, source_target_pairs={{0,3},{1,0},{2,1},{3,2},{4,7},{5,4},{6,5},{7,6},{8,11},{9,8},{10,9... | collective-permute-start | bytes 442376 | tf_op jit(solution)/shard_map/ppermute | solution.py:81
  167.4 2.8 %all-to-all-done.5 = bf16[16,16,1152]{2,1,0:T(8,128)(2,1)S(1)} async-done(((bf16[16,16,1152]{2,1,0:T(8,128)(2,1)}), bf16[16,16,1152]{2,1,0:T(8,128)(2,1)S(1)}, u32[]{:S(2)}, u32[]{:S(2)}) %all-to-all-start.5) | async-done | bytes 589856 | tf_op jit(solution)/shard_map/all_to_all | solution.py:262
  170.2 3.9 %convolution_convert_fusion.1 = bf16[256,1152]{1,0:T(8,128)(2,1)} fusion(bf16[256,1152]{1,0:T(8,128)(2,1)S(1)} %bitcast.68, bf16[1152,544]{1,0:T(8,128)(2,1)} %bitcast.57, f32[256,272]{0,1:T(8,128)S(1)} %copy-done.8), kind=kOutput, calls=%fused_computation.11 | convolution fusion | flops 322482176 | bytes 3227648 | tf_op jit(solution)/shard_map/dot_general | solution.py:56
  174.0 6.6 %all-to-all-start.6 = ((bf16[16,16,1152]{2,1,0:T(8,128)(2,1)}), bf16[16,16,1152]{2,1,0:T(8,128)(2,1)S(1)}, u32[]{:S(2)}, u32[]{:S(2)}) async-start(bf16[16,16,1152]{2,1,0:T(8,128)(2,1)} %bitcast.18), calls=%async_computation.6 | async-start | bytes 1179648 | tf_op jit(solution)/shard_map/all_to_all | solution.py:72
  180.7 3.5 %collective-permute-start.13 = (bf16[64,1152]{1,0:T(8,128)(2,1)S(1)}, bf16[64,1152]{1,0:T(8,128)(2,1)S(1)}, u32[]{:S(2)}, u32[]{:S(2)}) collective-permute-start(bf16[64,1152]{1,0:T(8,128)(2,1)S(1)} %add_convert_fusion), channel_id=1, source_target_pairs={{0,2},{1,3},{2,0},{3,1},{4,6},{5,7},{6,4},{7,5},{8,10},{9,11},{10,... | collective-permute-start | bytes 442376 | tf_op jit(solution)/shard_map/ppermute | solution.py:81
  184.1 6.6 %all-to-all-done.6 = bf16[16,16,1152]{2,1,0:T(8,128)(2,1)S(1)} async-done(((bf16[16,16,1152]{2,1,0:T(8,128)(2,1)}), bf16[16,16,1152]{2,1,0:T(8,128)(2,1)S(1)}, u32[]{:S(2)}, u32[]{:S(2)}) %all-to-all-start.6) | async-done | bytes 589856 | tf_op jit(solution)/shard_map/all_to_all | solution.py:72
  190.9 3.6 %collective-permute-done.13 = bf16[64,1152]{1,0:T(8,128)(2,1)S(1)} collective-permute-done((bf16[64,1152]{1,0:T(8,128)(2,1)S(1)}, bf16[64,1152]{1,0:T(8,128)(2,1)S(1)}, u32[]{:S(2)}, u32[]{:S(2)}) %collective-permute-start.13) | collective-permute-done | bytes 147488 | tf_op jit(solution)/shard_map/ppermute | solution.py:81
  194.6 1.0 fusion.8
  197.2 6.1 %all-to-all-start.7 = ((bf16[4,336,128]{2,1,0:T(8,128)(2,1)}), bf16[4,336,128]{2,1,0:T(8,128)(2,1)S(1)}, u32[]{:S(2)}, u32[]{:S(2)}) async-start(bf16[4,336,128]{2,1,0:T(8,128)(2,1)} %broadcast_in_dim.20), calls=%async_computation.7 | async-start | bytes 688128 | tf_op jit(solution)/shard_map/all_to_all | solution.py:66
  203.3 12.4 %all-to-all-done.7 = bf16[4,336,128]{2,1,0:T(8,128)(2,1)S(1)} async-done(((bf16[4,336,128]{2,1,0:T(8,128)(2,1)}), bf16[4,336,128]{2,1,0:T(8,128)(2,1)S(1)}, u32[]{:S(2)}, u32[]{:S(2)}) %all-to-all-start.7) | async-done | bytes 344096 | tf_op jit(solution)/shard_map/all_to_all | solution.py:66
  217.7 0.9 subtract_multiply_fusion
  (148 shorter events, 14.4 us)
Async XLA Ops:
  0.6 24.2 %copy-start = (bf16[288,1152]{1,0:T(8,128)(2,1)S(1)}, bf16[288,1152]{1,0:T(8,128)(2,1)}, u32[]{:S(2)}) copy-start(bf16[288,1152]{1,0:T(8,128)(2,1)} %param.25) | copy-start | bytes 1990660
  2.5 14.5 %copy-start.11 = (f32[1152]{0:T(1024)S(1)}, f32[1152]{0:T(1024)}, u32[]{:S(2)}) copy-start(f32[1152]{0:T(1024)} %param.17) | copy-start | bytes 13828
  2.6 14.7 %copy-start.12 = (f32[1152]{0:T(1024)S(1)}, f32[1152]{0:T(1024)}, u32[]{:S(2)}) copy-start(f32[1152]{0:T(1024)} %param.18) | copy-start | bytes 13828
  2.6 15.1 %copy-start.10 = (f32[1152]{0:T(1024)S(1)}, f32[1152]{0:T(1024)}, u32[]{:S(2)}) copy-start(f32[1152]{0:T(1024)} %param.23) | copy-start | bytes 13828
  2.6 16.0 %copy-start.13 = (f32[1152]{0:T(1024)S(1)}, f32[1152]{0:T(1024)}, u32[]{:S(2)}) copy-start(f32[1152]{0:T(1024)} %param.26) | copy-start | bytes 13828
  3.9 22.2 %all-to-all-start = ((bf16[64,2,680]{2,1,0:T(2,128)(2,1)}), bf16[64,2,680]{2,1,0:T(2,128)(2,1)S(1)}, u32[]{:S(2)}, u32[]{:S(2)}) async-start(bf16[64,2,680]{2,1,0:T(2,128)(2,1)} %reshape.308), calls=%async_computation | async-start | bytes 393216 | tf_op jit(solution)/shard_map/all_to_all | solution.py:198
  14.8 11.2 %copy-start.15 = (s32[1152]{0:T(1024)}, s32[1152]{0:T(1024)S(1)}, u32[]{:S(2)}) copy-start(s32[1152]{0:T(1024)S(1)} %reshape.275) | copy-start | bytes 13828
  16.7 1.0 copy-start.19
  16.9 0.8 copy-start.25
  24.8 1.9 copy-start.2
  26.1 13.4 %copy-start.3 = (bf16[1152,288]{0,1:T(8,128)(2,1)}, bf16[1152,288]{0,1:T(8,128)(2,1)S(1)}, u32[]{:S(2)}) copy-start(bf16[1152,288]{0,1:T(8,128)(2,1)S(1)} %fusion.6) | copy-start | bytes 1990660
  26.8 12.6 %copy-start.17 = (f32[64]{0:T(128)}, f32[64]{0:T(128)S(1)}, u32[]{:S(2)}) copy-start(f32[64]{0:T(128)S(1)} %broadcast_multiply_fusion.3) | copy-start | bytes 772
  27.1 1.8 copy-start.5
  28.9 27.5 %copy-start.6 = (bf16[64,1152]{1,0:T(8,128)(2,1)S(1)}, bf16[64,1152]{1,0:T(8,128)(2,1)}, u32[]{:S(2)}) copy-start(bf16[64,1152]{1,0:T(8,128)(2,1)} %all_gather.6) | copy-start | bytes 442372
  28.9 48.8 %all-to-all-start.1 = ((bf16[8,144,544]{2,1,0:T(8,128)(2,1)}), bf16[8,144,544]{2,1,0:T(8,128)(2,1)S(1)}, u32[]{:S(2)}, u32[]{:S(2)}) async-start(bf16[8,144,544]{2,1,0:T(8,128)(2,1)} %broadcast_in_dim.18), calls=%async_computation.1 | async-start | bytes 2949120 | tf_op jit(solution)/shard_map/all_to_all | solution.py:66
  39.4 32.5 %copy-start.23 = (f32[64]{0:T(128)}, f32[64]{0:T(128)S(1)}, u32[]{:S(2)}) copy-start(f32[64]{0:T(128)S(1)} %add_rsqrt_fusion.2) | copy-start | bytes 772
  39.8 30.1 %collective-permute-start = (bf16[64,1152]{1,0:T(8,128)(2,1)S(1)}, bf16[64,1152]{1,0:T(8,128)(2,1)}, u32[]{:S(2)}, u32[]{:S(2)}) collective-permute-start(bf16[64,1152]{1,0:T(8,128)(2,1)S(1)} %convolution_convert_fusion.3), channel_id=1, source_target_pairs={{0,1},{1,2},{2,3},{3,0},{4,5},{5,6},{6,7},{7,4},{8,9},{9,10},{10,1... | collective-permute-start | bytes 442376 | tf_op jit(solution)/shard_map/ppermute | solution.py:81
  44.2 25.8 %collective-permute-start.1 = (bf16[64,1152]{1,0:T(8,128)(2,1)S(1)}, bf16[64,1152]{1,0:T(8,128)(2,1)S(1)}, u32[]{:S(2)}, u32[]{:S(2)}) collective-permute-start(bf16[64,1152]{1,0:T(8,128)(2,1)S(1)} %convolution_convert_fusion.3), channel_id=1, source_target_pairs={{0,2},{1,3},{2,0},{3,1},{4,6},{5,7},{6,4},{7,5},{8,10},{9,11},{10,... | collective-permute-start | bytes 442376 | tf_op jit(solution)/shard_map/ppermute | solution.py:81
  49.6 21.0 %collective-permute-start.2 = (bf16[64,1152]{1,0:T(8,128)(2,1)S(1)}, bf16[64,1152]{1,0:T(8,128)(2,1)}, u32[]{:S(2)}, u32[]{:S(2)}) collective-permute-start(bf16[64,1152]{1,0:T(8,128)(2,1)S(1)} %convolution_convert_fusion.3), channel_id=1, source_target_pairs={{0,3},{1,0},{2,1},{3,2},{4,7},{5,4},{6,5},{7,6},{8,11},{9,8},{10,9... | collective-permute-start | bytes 442376 | tf_op jit(solution)/shard_map/ppermute | solution.py:81
  70.0 0.7 copy-start.9
  72.5 8.5 %collective-permute-start.3 = (bf16[64,1152]{1,0:T(8,128)(2,1)S(1)}, bf16[64,1152]{1,0:T(8,128)(2,1)S(1)}, u32[]{:S(2)}, u32[]{:S(2)}) collective-permute-start(bf16[64,1152]{1,0:T(8,128)(2,1)S(1)} %multiply_convert_fusion.2), channel_id=1, source_target_pairs={{0,128},{64,192},{128,0},{192,64},{1,129},{65,193},{129,1},{193,65... | collective-permute-start | bytes 442376 | tf_op jit(solution)/shard_map/ppermute | solution.py:81
  77.7 2.8 %copy-start.1 = (bf16[8,144,544]{2,1,0:T(8,128)(2,1)}, bf16[8,144,544]{2,1,0:T(8,128)(2,1)S(1)}, u32[]{:S(2)}) copy-start(bf16[8,144,544]{2,1,0:T(8,128)(2,1)S(1)} %all-to-all-done.1) | copy-start | bytes 3760132
  78.9 2.2 %copy-start.7 = (f32[256,272]{0,1:T(8,128)}, f32[256,272]{0,1:T(8,128)S(1)}, u32[]{:S(2)}) copy-start(f32[256,272]{0,1:T(8,128)S(1)} %convolution_add_fusion.1) | copy-start | bytes 835588
  78.9 13.2 %copy-start.14 = (f32[1152]{0:T(1024)S(1)}, f32[1152]{0:T(1024)}, u32[]{:S(2)}) copy-start(f32[1152]{0:T(1024)} %param.22) | copy-start | bytes 13828
  81.1 14.5 %all-to-all-start.2 = ((bf16[16,16,1152]{2,1,0:T(8,128)(2,1)}), bf16[16,16,1152]{2,1,0:T(8,128)(2,1)S(1)}, u32[]{:S(2)}, u32[]{:S(2)}) async-start(bf16[16,16,1152]{2,1,0:T(8,128)(2,1)} %bitcast.12), calls=%async_computation.2 | async-start | bytes 1179648 | tf_op jit(solution)/shard_map/all_to_all | solution.py:72
  86.2 11.5 %collective-permute-start.4 = (bf16[64,1152]{1,0:T(8,128)(2,1)S(1)}, bf16[64,1152]{1,0:T(8,128)(2,1)S(1)}, u32[]{:S(2)}, u32[]{:S(2)}) collective-permute-start(bf16[64,1152]{1,0:T(8,128)(2,1)S(1)} %multiply_convert_fusion.2), channel_id=1, source_target_pairs={{0,64},{64,128},{128,192},{192,0},{1,65},{65,129},{129,193},{193,1... | collective-permute-start | bytes 442376 | tf_op jit(solution)/shard_map/ppermute | solution.py:81
  88.2 9.5 %collective-permute-start.5 = (bf16[64,1152]{1,0:T(8,128)(2,1)S(1)}, bf16[64,1152]{1,0:T(8,128)(2,1)S(1)}, u32[]{:S(2)}, u32[]{:S(2)}) collective-permute-start(bf16[64,1152]{1,0:T(8,128)(2,1)S(1)} %multiply_convert_fusion.2), channel_id=1, source_target_pairs={{0,192},{64,0},{128,64},{192,128},{1,193},{65,1},{129,65},{193,129... | collective-permute-start | bytes 442376 | tf_op jit(solution)/shard_map/ppermute | solution.py:81
  98.8 26.2 %all-to-all-start.3 = ((bf16[16,16,1152]{2,1,0:T(8,128)(2,1)}), bf16[16,16,1152]{2,1,0:T(8,128)(2,1)S(1)}, u32[]{:S(2)}, u32[]{:S(2)}) async-start(bf16[16,16,1152]{2,1,0:T(8,128)(2,1)} %broadcast_in_dim.19), calls=%async_computation.3 | async-start | bytes 1179648 | tf_op jit(solution)/shard_map/all_to_all | solution.py:66
  106.7 4.1 %collective-permute-start.6 = (bf16[256,1152]{1,0:T(8,128)(2,1)S(1)}, bf16[256,1152]{1,0:T(8,128)(2,1)S(1)}, u32[]{:S(2)}, u32[]{:S(2)}) collective-permute-start(bf16[256,1152]{1,0:T(8,128)(2,1)S(1)} %constant_dynamic-update-slice_fusion.near_ref), channel_id=1, source_target_pairs={{0,4},{4,0},{1,5},{5,1},{2,6},{6,2},{3,7},{7,3},{8,12},{12,8},{9,1... | collective-permute-start | bytes 1769480 | tf_op jit(solution)/shard_map/ppermute | solution.py:81
  127.9 5.7 %collective-permute-start.7 = (bf16[256,1152]{1,0:T(8,128)(2,1)S(1)}, bf16[256,1152]{1,0:T(8,128)(2,1)}, u32[]{:S(2)}, u32[]{:S(2)}) collective-permute-start(bf16[256,1152]{1,0:T(8,128)(2,1)S(1)} %convolution_convert_fusion), channel_id=1, source_target_pairs={{0,4},{4,0},{1,5},{5,1},{2,6},{6,2},{3,7},{7,3},{8,12},{12,8},{9,1... | collective-permute-start | bytes 1769480 | tf_op jit(solution)/shard_map/ppermute | solution.py:81
  129.8 22.8 %all-to-all-start.4 = ((bf16[16,16,1152]{2,1,0:T(8,128)(2,1)}), bf16[16,16,1152]{2,1,0:T(8,128)(2,1)S(1)}, u32[]{:S(2)}, u32[]{:S(2)}) async-start(bf16[16,16,1152]{2,1,0:T(8,128)(2,1)} %bitcast.15), calls=%async_computation.4 | async-start | bytes 1179648 | tf_op jit(solution)/shard_map/all_to_all | solution.py:72
  135.1 35.1 %copy-start.8 = (f32[256,272]{0,1:T(8,128)S(1)}, f32[256,272]{0,1:T(8,128)}, u32[]{:S(2)}) copy-start(f32[256,272]{0,1:T(8,128)} %copy-done.7) | copy-start | bytes 835588
  135.1 10.1 %collective-permute-start.10 = (bf16[64,1152]{1,0:T(8,128)(2,1)S(1)}, bf16[64,1152]{1,0:T(8,128)(2,1)S(1)}, u32[]{:S(2)}, u32[]{:S(2)}) collective-permute-start(bf16[64,1152]{1,0:T(8,128)(2,1)S(1)} %get-tuple-element.80), channel_id=1, source_target_pairs={{0,64},{64,128},{128,192},{192,0},{1,65},{65,129},{129,193},{193,1... | collective-permute-start | bytes 442376 | tf_op jit(solution)/shard_map/ppermute | solution.py:81
  139.5 12.2 %collective-permute-start.8 = (bf16[64,1152]{1,0:T(8,128)(2,1)S(1)}, bf16[64,1152]{1,0:T(8,128)(2,1)S(1)}, u32[]{:S(2)}, u32[]{:S(2)}) collective-permute-start(bf16[64,1152]{1,0:T(8,128)(2,1)S(1)} %get-tuple-element.82), channel_id=1, source_target_pairs={{0,192},{64,0},{128,64},{192,128},{1,193},{65,1},{129,65},{193,129... | collective-permute-start | bytes 442376 | tf_op jit(solution)/shard_map/ppermute | solution.py:81
  141.4 10.3 %collective-permute-start.9 = (bf16[64,1152]{1,0:T(8,128)(2,1)S(1)}, bf16[64,1152]{1,0:T(8,128)(2,1)S(1)}, u32[]{:S(2)}, u32[]{:S(2)}) collective-permute-start(bf16[64,1152]{1,0:T(8,128)(2,1)S(1)} %get-tuple-element.81), channel_id=1, source_target_pairs={{0,128},{64,192},{128,0},{192,64},{1,129},{65,193},{129,1},{193,65... | collective-permute-start | bytes 442376 | tf_op jit(solution)/shard_map/ppermute | solution.py:81
  153.6 16.5 %all-to-all-start.5 = ((bf16[16,16,1152]{2,1,0:T(8,128)(2,1)}), bf16[16,16,1152]{2,1,0:T(8,128)(2,1)S(1)}, u32[]{:S(2)}, u32[]{:S(2)}) async-start(bf16[16,16,1152]{2,1,0:T(8,128)(2,1)} %get-tuple-element.62), calls=%async_computation.5 | async-start | bytes 1179648 | tf_op jit(solution)/shard_map/all_to_all | solution.py:262
  159.4 14.6 %collective-permute-start.11 = (bf16[64,1152]{1,0:T(8,128)(2,1)S(1)}, bf16[64,1152]{1,0:T(8,128)(2,1)S(1)}, u32[]{:S(2)}, u32[]{:S(2)}) collective-permute-start(bf16[64,1152]{1,0:T(8,128)(2,1)S(1)} %add_convert_fusion), channel_id=1, source_target_pairs={{0,1},{1,2},{2,3},{3,0},{4,5},{5,6},{6,7},{7,4},{8,9},{9,10},{10,1... | collective-permute-start | bytes 442376 | tf_op jit(solution)/shard_map/ppermute | solution.py:81
  161.4 12.7 %collective-permute-start.12 = (bf16[64,1152]{1,0:T(8,128)(2,1)S(1)}, bf16[64,1152]{1,0:T(8,128)(2,1)S(1)}, u32[]{:S(2)}, u32[]{:S(2)}) collective-permute-start(bf16[64,1152]{1,0:T(8,128)(2,1)S(1)} %add_convert_fusion), channel_id=1, source_target_pairs={{0,3},{1,0},{2,1},{3,2},{4,7},{5,4},{6,5},{7,6},{8,11},{9,8},{10,9... | collective-permute-start | bytes 442376 | tf_op jit(solution)/shard_map/ppermute | solution.py:81
  174.0 20.4 %copy-start.20 = (f32[16]{0:T(128)S(1)}, f32[16]{0:T(128)}, u32[]{:S(2)}) copy-start(f32[16]{0:T(128)} %copy-done.19) | copy-start | bytes 196
  174.0 20.4 %copy-start.26 = (f32[16]{0:T(128)S(1)}, f32[16]{0:T(128)}, u32[]{:S(2)}) copy-start(f32[16]{0:T(128)} %copy-done.25) | copy-start | bytes 196
  174.0 20.6 %copy-start.16 = (s32[1152]{0:T(1024)S(1)}, s32[1152]{0:T(1024)}, u32[]{:S(2)}) copy-start(s32[1152]{0:T(1024)} %copy-done.15) | copy-start | bytes 13828
  174.0 16.7 %all-to-all-start.6 = ((bf16[16,16,1152]{2,1,0:T(8,128)(2,1)}), bf16[16,16,1152]{2,1,0:T(8,128)(2,1)S(1)}, u32[]{:S(2)}, u32[]{:S(2)}) async-start(bf16[16,16,1152]{2,1,0:T(8,128)(2,1)} %bitcast.18), calls=%async_computation.6 | async-start | bytes 1179648 | tf_op jit(solution)/shard_map/all_to_all | solution.py:72
  180.7 15.1 %copy-start.22 = (f32[64]{0:T(128)S(1)}, f32[64]{0:T(128)}, u32[]{:S(2)}) copy-start(f32[64]{0:T(128)} %copy-done.21) | copy-start | bytes 772
  180.7 13.8 %collective-permute-start.13 = (bf16[64,1152]{1,0:T(8,128)(2,1)S(1)}, bf16[64,1152]{1,0:T(8,128)(2,1)S(1)}, u32[]{:S(2)}, u32[]{:S(2)}) collective-permute-start(bf16[64,1152]{1,0:T(8,128)(2,1)S(1)} %add_convert_fusion), channel_id=1, source_target_pairs={{0,2},{1,3},{2,0},{3,1},{4,6},{5,7},{6,4},{7,5},{8,10},{9,11},{10,... | collective-permute-start | bytes 442376 | tf_op jit(solution)/shard_map/ppermute | solution.py:81
  190.9 5.1 %copy-start.4 = (bf16[1152,288]{0,1:T(8,128)(2,1)S(1)}, bf16[1152,288]{0,1:T(8,128)(2,1)}, u32[]{:S(2)}) copy-start(bf16[1152,288]{0,1:T(8,128)(2,1)} %copy-done.3) | copy-start | bytes 1990660
  197.2 18.6 %all-to-all-start.7 = ((bf16[4,336,128]{2,1,0:T(8,128)(2,1)}), bf16[4,336,128]{2,1,0:T(8,128)(2,1)S(1)}, u32[]{:S(2)}, u32[]{:S(2)}) async-start(bf16[4,336,128]{2,1,0:T(8,128)(2,1)} %broadcast_in_dim.20), calls=%async_computation.7 | async-start | bytes 688128 | tf_op jit(solution)/shard_map/all_to_all | solution.py:66
  203.3 13.1 %copy-start.18 = (f32[64]{0:T(128)S(1)}, f32[64]{0:T(128)}, u32[]{:S(2)}) copy-start(f32[64]{0:T(128)} %copy-done.17) | copy-start | bytes 772
  203.3 13.1 %copy-start.24 = (f32[64]{0:T(128)S(1)}, f32[64]{0:T(128)}, u32[]{:S(2)}) copy-start(f32[64]{0:T(128)} %copy-done.23) | copy-start | bytes 772
  (1 other events, 0.5 us)

commit v4 on v3

--- a/solution.py
+++ b/solution.py
@@ -9,6 +9,7 @@
 tanh_coef = 0.7978845608028654
 cubic_coef = 0.044715
 low = jnp.bfloat16
+lanes = 128
 DP = ("ylo", "x", "z", "core")
 GROUP = ("x", "ylo", "core")
 IMAGES = ("z", "ylo")
@@ -79,6 +80,14 @@
 def passed(block, axis, step):
     count = lax.axis_size(axis)
     return lax.ppermute(block, axis, [(i, (i + step) % count) for i in range(count)])
+
+
+def crossed(block, axis, bits):
+    return lax.ppermute(block, axis, [(i, i ^ bits) for i in range(lax.axis_size(axis))])
+
+
+def add(one, other):
+    return (one.astype(jnp.float32) + other.astype(jnp.float32)).astype(low)
 
 
 def together(*values):
@@ -131,6 +140,37 @@
         out_specs=(vmem, vmem),
         compiler_params=pltpu.CompilerParams(vmem_limit_bytes=10 * 1024 * 1024),
     )(got, unit, inverse)
+
+
+def output_kernel(last_ref, normed_ref, inverse_ref, gain_ref, image_ref, text_ref):
+    count = last_ref.shape[0]
+    rows, width = image_ref.shape
+    own, tiles = rows // count, width // lanes
+    for slot in range(count):
+        for tile in range(tiles):
+            image_ref[slot * own : (slot + 1) * own, tile * lanes : (tile + 1) * lanes] = last_ref[
+                slot, tile * own : (tile + 1) * own
+            ].astype(jnp.float32)
+    pieces = []
+    for slot in range(count):
+        left = width // count
+        for at in range(tiles * own, last_ref.shape[1], rows):
+            piece = last_ref[slot, at : at + rows].astype(jnp.float32)
+            pieces.append(piece[:, : min(left, lanes)])
+            left -= lanes
+    column_back = jnp.concatenate(pieces, axis=1)
+    text_ref[...] = norm_backward(column_back, normed_ref[...], inverse_ref[...], gain_ref[...])
+
+
+def outputs(last, normed, inverse, gain):
+    vmem = pl.BlockSpec(memory_space=pltpu.VMEM)
+    return pl.pallas_call(
+        output_kernel,
+        out_shape=(jax.ShapeDtypeStruct(normed.shape, jnp.float32),) * 2,
+        in_specs=[vmem] * 4,
+        out_specs=(vmem, vmem),
+        compiler_params=pltpu.CompilerParams(vmem_limit_bytes=10 * 1024 * 1024),
+    )(last, normed, inverse, gain)
 
 
 def pairs(numbers, places, image, near, far):
@@ -262,15 +302,16 @@
     back_all = lax.all_to_all(slots, GROUP, 0, 0, tiled=True).reshape(-1, width)
     pre_back = (mm(back_all, down_mine) * hidden_slope).astype(low)
     ready_sent = mm_nt(pre_back, up_mine).astype(low)
-    text_got = [text_unit_back] + [passed(text_unit_back, "tensor", step) for step in (1, 2, 3)]
-    ready_sent, text_got[1], text_got[3] = together(ready_sent, text_got[1], text_got[3])
-    ready_back, text_got[2] = together(sum_slots(ready_sent, GROUP), text_got[2])
-    text_unit_back = sum(part.astype(jnp.float32) for part in text_got)
+    ready_sent, text_got = together(ready_sent, crossed(text_unit_back, "tensor", 2))
+    text_unit_back = add(text_unit_back, text_got)
+    ready_back, text_got = together(
+        sum_slots(ready_sent, GROUP), crossed(text_unit_back, "tensor", 1)
+    )
+    text_unit_back = text_unit_back.astype(jnp.float32) + text_got.astype(jnp.float32)
     image_grad = image_back + norm_backward(ready_back, image_normed, image_inverse, gain_turned)
     image_low = mm_nt(image_grad.astype(low), turn).astype(low)
 
     text_back = unit_backward(text_unit_back, text_unit, text_invnorm)
-    lanes = 128
     head_tiles = -(-head_rows // lanes)
     head_padded = jnp.pad(head_turned, ((0, head_tiles * lanes - head_rows), (0, 0)))
     column_part = mm_nt(text_back.astype(low), head_padded).astype(low)
@@ -284,13 +325,7 @@
         axis=0,
     )
     last = spread(last, "tensor")
-    image_grad = last[:, : tiles * own_rows].reshape(tensor_count, tiles, own_rows, lanes)
-    image_grad = image_grad.transpose(0, 2, 1, 3).reshape(block_rows, width).astype(jnp.float32)
-    column_back = last[:, tiles * own_rows :].reshape(tensor_count, head_tiles, block_rows, lanes)
-    column_back = column_back.transpose(2, 0, 1, 3).reshape(block_rows, tensor_count, head_tiles * lanes)
-    column_back = column_back[:, :, :head_rows].reshape(block_rows, width)
-    text_grad = norm_backward(column_back.astype(jnp.float32), text_normed, text_inverse, text_norm_gain)
-    return (image_grad, text_grad)
+    return outputs(last, text_normed, text_inverse, text_norm_gain[None])
 
 
 def solution(mesh):

time: 220 us -> 213 us (0.968)
  starting transfers between devices: 106 us -> 97.9 us
  waiting for transfers between devices: 54.9 us -> 60 us
  local copies, waits for them, and re-layouts: 11.6 us -> 8.32 us
  other arithmetic: 6.67 us -> 3.71 us
    ppermute x14 -> x11, starting transfers between devices: 49.7 us -> 38.3 us  [passed(): lax.ppermute(block, axis, [(i, (i + step) % count) for i in range(count)])]
    ppermute x0 -> x2, starting transfers between devices: none -> 8.45 us  [crossed(): lax.ppermute(block, axis, [(i, i ^ bits) for i in range(lax.axis_size(axi...]
    all_to_all x3, starting transfers between devices: 24.3 us -> 17.4 us  [spread(): return lax.all_to_all(slots, axes, 0, 0, tiled=True)]
    ppermute x14 -> x11, waiting for transfers between devices: 12.8 us -> 8.61 us  [passed(): lax.ppermute(block, axis, [(i, (i + step) % count) for i in range(count)])]
    ppermute x0 -> x2, waiting for transfers between devices: none -> 3.69 us  [crossed(): lax.ppermute(block, axis, [(i, i ^ bits) for i in range(lax.axis_size(axi...]
    all_to_all x3, waiting for transfers between devices: 10.7 us -> 13.5 us  [swap_slots(): return lax.all_to_all(slots, axes, 0, 0, tiled=True)]
    all_to_all x3, waiting for transfers between devices: 28.6 us -> 31.2 us  [spread(): return lax.all_to_all(slots, axes, 0, 0, tiled=True)]
  transfers between devices with their start and end apart: 22 -> 21, of which waited for: 11 -> 11; matrix products, arithmetic and copies ran while one was open for 8% -> 8% of each run, Pallas kernels for 0% -> 0%
where the time goes in v4:
time: 213 us; the launch traced here: 212 us
  starting transfers between devices  97.9 us (46%)
  waiting for transfers between devices  60 us (28%)
  blocking collectives  19.2 us (9%)
  matrix products  15 us (7%)
  local copies, waits for them, and re-layouts  8.32 us (4%)
  Pallas kernels  4.43 us (2%)
  other arithmetic  3.71 us (2%)
  between operations  3.25 us (2%)
    ppermute x11, starting transfers between devices, passed(): lax.ppermute(block, axis, [(i, (i + step) % count) for i in range(count)])  38.3 us
    all_to_all x3, waiting for transfers between devices, spread(): return lax.all_to_all(slots, axes, 0, 0, tiled=True)  31.2 us
    all_to_all x3, starting transfers between devices, spread(): return lax.all_to_all(slots, axes, 0, 0, tiled=True)  17.4 us
    all_to_all x3, starting transfers between devices, swap_slots(): return lax.all_to_all(slots, axes, 0, 0, tiled=True)  16.8 us
    all_gather x1, blocking collectives, per_device(): ready_all = lax.all_gather(ready_all, 'x', axis=0, tiled=True)  13.7 us
    all_to_all x3, waiting for transfers between devices, swap_slots(): return lax.all_to_all(slots, axes, 0, 0, tiled=True)  13.5 us
    all_to_all x1, starting transfers between devices, per_device(): got = lax.all_to_all(slots, GROUP + ('tensor',), 0, 0, tiled=True)  10.8 us
    ppermute x11, waiting for transfers between devices, passed(): lax.ppermute(block, axis, [(i, (i + step) % count) for i in range(count)])  8.61 us
  transfers between devices with their start and end apart: 21, of which 11 were waited for; matrix products, arithmetic and copies ran while one was open for 8% of the time, Pallas kernels for 0%

profile of v4, /device:TPU:6, one launch (start us, length us, event | category | flops | bytes accessed | tf_op | source)
XLA Modules:
  0.0 211.8 jit_solution(6603355491876179203)
XLA Ops:
  0.6 0.8 subtract_convert_fusion
  1.4 0.8 fusion.52
  2.6 1.3 reshape.289
  3.9 10.8 %all-to-all-start = ((bf16[64,2,680]{2,1,0:T(2,128)(2,1)}), bf16[64,2,680]{2,1,0:T(2,128)(2,1)S(1)}, u32[]{:S(2)}, u32[]{:S(2)}) async-start(bf16[64,2,680]{2,1,0:T(2,128)(2,1)} %reshape.289), calls=%async_computation | async-start | bytes 393216 | tf_op jit(solution)/shard_map/all_to_all | solution.py:238
  14.8 1.9 fusion.78
  18.8 5.5 %all_gather.6 = bf16[64,1152]{1,0:T(8,128)(2,1)S(1)} all-gather(bf16[16,1152]{1,0:T(8,128)(2,1)S(1)} %add_convert_fusion.3), channel_id=1, replica_groups=mesh['ylo'=2,'x'=4,'z'=8,'core'=2,'tensor'=4] {'ylo','core'}, dimensions={0}, use_global_device_ids=true | all-gather | bytes 184320 | tf_op jit(solution)/shard_map/all_gather | solution.py:244
  24.3 1.3 fusion.6
  27.1 1.2 broadcast_in_dim.20
  28.4 10.3 %all-to-all-start.1 = ((bf16[8,144,544]{2,1,0:T(8,128)(2,1)}), bf16[8,144,544]{2,1,0:T(8,128)(2,1)}, u32[]{:S(2)}, u32[]{:S(2)}) async-start(bf16[8,144,544]{2,1,0:T(8,128)(2,1)} %broadcast_in_dim.20), calls=%async_computation.1 | async-start | bytes 2949120 | tf_op jit(solution)/shard_map/all_to_all | solution.py:67
  39.2 4.4 %collective-permute-start = (bf16[64,1152]{1,0:T(8,128)(2,1)S(1)}, bf16[64,1152]{1,0:T(8,128)(2,1)S(1)}, u32[]{:S(2)}, u32[]{:S(2)}) collective-permute-start(bf16[64,1152]{1,0:T(8,128)(2,1)S(1)} %convolution_convert_fusion.3), channel_id=1, source_target_pairs={{0,1},{1,2},{2,3},{3,0},{4,5},{5,6},{6,7},{7,4},{8,9},{9,10},{10,1... | collective-permute-start | bytes 442376 | tf_op jit(solution)/shard_map/ppermute | solution.py:82
  43.6 5.4 %collective-permute-start.1 = (bf16[64,1152]{1,0:T(8,128)(2,1)S(1)}, bf16[64,1152]{1,0:T(8,128)(2,1)S(1)}, u32[]{:S(2)}, u32[]{:S(2)}) collective-permute-start(bf16[64,1152]{1,0:T(8,128)(2,1)S(1)} %convolution_convert_fusion.3), channel_id=1, source_target_pairs={{0,2},{1,3},{2,0},{3,1},{4,6},{5,7},{6,4},{7,5},{8,10},{9,11},{10,... | collective-permute-start | bytes 442376 | tf_op jit(solution)/shard_map/ppermute | solution.py:82
  49.0 5.5 %collective-permute-start.2 = (bf16[64,1152]{1,0:T(8,128)(2,1)S(1)}, bf16[64,1152]{1,0:T(8,128)(2,1)S(1)}, u32[]{:S(2)}, u32[]{:S(2)}) collective-permute-start(bf16[64,1152]{1,0:T(8,128)(2,1)S(1)} %convolution_convert_fusion.3), channel_id=1, source_target_pairs={{0,3},{1,0},{2,1},{3,2},{4,7},{5,4},{6,5},{7,6},{8,11},{9,8},{10,9... | collective-permute-start | bytes 442376 | tf_op jit(solution)/shard_map/ppermute | solution.py:82
  54.5 13.7 %all_gather.7 = bf16[256,1152]{1,0:T(8,128)(2,1)S(1)} all-gather(bf16[64,1152]{1,0:T(8,128)(2,1)S(1)} %all_gather.6), channel_id=1, replica_groups=mesh['ylo'=2,'x'=4,'z'=8,'core'=2,'tensor'=4] {'x'}, dimensions={0}, use_global_device_ids=true | all-gather | bytes 737280 | tf_op jit(solution)/shard_map/all_gather | solution.py:246
  68.5 3.4 %collective-permute-start.3 = (bf16[64,1152]{1,0:T(8,128)(2,1)S(1)}, bf16[64,1152]{1,0:T(8,128)(2,1)S(1)}, u32[]{:S(2)}, u32[]{:S(2)}) collective-permute-start(bf16[64,1152]{1,0:T(8,128)(2,1)S(1)} %multiply_convert_fusion.2), channel_id=1, source_target_pairs={{0,128},{64,192},{128,0},{192,64},{1,129},{65,193},{129,1},{193,65... | collective-permute-start | bytes 442376 | tf_op jit(solution)/shard_map/ppermute | solution.py:82
  71.9 5.3 %all-to-all-done.1 = bf16[8,144,544]{2,1,0:T(8,128)(2,1)} async-done(((bf16[8,144,544]{2,1,0:T(8,128)(2,1)}), bf16[8,144,544]{2,1,0:T(8,128)(2,1)}, u32[]{:S(2)}, u32[]{:S(2)}) %all-to-all-start.1) | async-done | bytes 1253408 | tf_op jit(solution)/shard_map/all_to_all | solution.py:67
  77.2 1.6 convolution_add_fusion.1
  78.9 2.9 %convolution_convert_fusion.2 = bf16[256,1152]{1,0:T(8,128)(2,1)} fusion(bf16[1152,544]{1,0:T(8,128)(2,1)} %bitcast.11, f32[256,272]{0,1:T(8,128)S(1)} %convolution_add_fusion.1), kind=kOutput, calls=%fused_computation.12 | convolution fusion | flops 161353728 | bytes 1753088 | tf_op jit(solution)/shard_map/dot_general | solution.py:57
  81.8 5.7 %all-to-all-start.2 = ((bf16[16,16,1152]{2,1,0:T(8,128)(2,1)}), bf16[16,16,1152]{2,1,0:T(8,128)(2,1)S(1)}, u32[]{:S(2)}, u32[]{:S(2)}) async-start(bf16[16,16,1152]{2,1,0:T(8,128)(2,1)} %bitcast.12), calls=%async_computation.2 | async-start | bytes 1179648 | tf_op jit(solution)/shard_map/all_to_all | solution.py:73
  87.5 2.0 collective-permute-start.4
  89.5 3.8 %collective-permute-start.5 = (bf16[64,1152]{1,0:T(8,128)(2,1)S(1)}, bf16[64,1152]{1,0:T(8,128)(2,1)S(1)}, u32[]{:S(2)}, u32[]{:S(2)}) collective-permute-start(bf16[64,1152]{1,0:T(8,128)(2,1)S(1)} %multiply_convert_fusion.2), channel_id=1, source_target_pairs={{0,192},{64,0},{128,64},{192,128},{1,193},{65,1},{129,65},{193,129... | collective-permute-start | bytes 442376 | tf_op jit(solution)/shard_map/ppermute | solution.py:82
  93.6 3.2 %all-to-all-done.2 = bf16[16,16,1152]{2,1,0:T(8,128)(2,1)S(1)} async-done(((bf16[16,16,1152]{2,1,0:T(8,128)(2,1)}), bf16[16,16,1152]{2,1,0:T(8,128)(2,1)S(1)}, u32[]{:S(2)}, u32[]{:S(2)}) %all-to-all-start.2) | async-done | bytes 589856 | tf_op jit(solution)/shard_map/all_to_all | solution.py:73
  96.9 2.1 collective-permute-done.4
  99.2 0.9 broadcast_in_dim.21
  100.1 3.6 %all-to-all-start.3 = ((bf16[16,16,1152]{2,1,0:T(8,128)(2,1)}), bf16[16,16,1152]{2,1,0:T(8,128)(2,1)S(1)}, u32[]{:S(2)}, u32[]{:S(2)}) async-start(bf16[16,16,1152]{2,1,0:T(8,128)(2,1)} %broadcast_in_dim.21), calls=%async_computation.3 | async-start | bytes 1179648 | tf_op jit(solution)/shard_map/all_to_all | solution.py:67
  103.8 1.9 collective-permute-start.6
  107.9 14.3 %all-to-all-done.3 = bf16[16,16,1152]{2,1,0:T(8,128)(2,1)S(1)} async-done(((bf16[16,16,1152]{2,1,0:T(8,128)(2,1)}), bf16[16,16,1152]{2,1,0:T(8,128)(2,1)S(1)}, u32[]{:S(2)}, u32[]{:S(2)}) %all-to-all-start.3) | async-done | bytes 589856 | tf_op jit(solution)/shard_map/all_to_all | solution.py:67
  122.1 2.4 %shard_map.158 = (bf16[256,256]{1,0:T(8,128)(2,1)S(1)}, bf16[256,256]{1,0:T(8,128)(2,1)S(1)}, bf16[256,1152]{1,0:T(8,128)(2,1)}) custom-call(f32[3]{0:T(128)S(1)} %pad_maximum_fusion.1.number_ref, s32[3]{0:T(128)S(1)} %pad_add_fusion.place_ref, bf16[256,1152]{1,0:T(8,128)(2,1)S(1)} %bitcast.38, ...), custom_call_target="tpu_custom_call" | custom-call | tf_op jit(solution)/shard_map/pallas_call | solution.py:179
  124.9 1.9 collective-permute-start.7
  126.9 3.8 %all-to-all-start.4 = ((bf16[16,16,1152]{2,1,0:T(8,128)(2,1)}), bf16[16,16,1152]{2,1,0:T(8,128)(2,1)S(1)}, u32[]{:S(2)}, u32[]{:S(2)}) async-start(bf16[16,16,1152]{2,1,0:T(8,128)(2,1)} %bitcast.15), calls=%async_computation.4 | async-start | bytes 1179648 | tf_op jit(solution)/shard_map/all_to_all | solution.py:73
  130.7 1.4 fusion.7
  132.2 4.4 %collective-permute-start.10 = (bf16[64,1152]{1,0:T(8,128)(2,1)S(1)}, bf16[64,1152]{1,0:T(8,128)(2,1)S(1)}, u32[]{:S(2)}, u32[]{:S(2)}) collective-permute-start(bf16[64,1152]{1,0:T(8,128)(2,1)S(1)} %get-tuple-element.78), channel_id=1, source_target_pairs={{0,64},{64,128},{128,192},{192,0},{1,65},{65,129},{129,193},{193,1... | collective-permute-start | bytes 442376 | tf_op jit(solution)/shard_map/ppermute | solution.py:82
  136.6 1.9 collective-permute-start.8
  138.5 3.7 %collective-permute-start.9 = (bf16[64,1152]{1,0:T(8,128)(2,1)S(1)}, bf16[64,1152]{1,0:T(8,128)(2,1)S(1)}, u32[]{:S(2)}, u32[]{:S(2)}) collective-permute-start(bf16[64,1152]{1,0:T(8,128)(2,1)S(1)} %get-tuple-element.79), channel_id=1, source_target_pairs={{0,128},{64,192},{128,0},{192,64},{1,129},{65,193},{129,1},{193,65... | collective-permute-start | bytes 442376 | tf_op jit(solution)/shard_map/ppermute | solution.py:82
  142.3 6.5 %collective-permute-done.8 = bf16[64,1152]{1,0:T(8,128)(2,1)S(1)} collective-permute-done((bf16[64,1152]{1,0:T(8,128)(2,1)S(1)}, bf16[64,1152]{1,0:T(8,128)(2,1)S(1)}, u32[]{:S(2)}, u32[]{:S(2)}) %collective-permute-start.8) | collective-permute-done | bytes 147488 | tf_op jit(solution)/shard_map/ppermute | solution.py:82
  149.6 1.1 shard_map.159
  150.6 6.1 %all-to-all-start.5 = ((bf16[16,16,1152]{2,1,0:T(8,128)(2,1)}), bf16[16,16,1152]{2,1,0:T(8,128)(2,1)S(1)}, u32[]{:S(2)}, u32[]{:S(2)}) async-start(bf16[16,16,1152]{2,1,0:T(8,128)(2,1)} %get-tuple-element.61), calls=%async_computation.5 | async-start | bytes 1179648 | tf_op jit(solution)/shard_map/all_to_all | solution.py:302
  156.8 6.4 %collective-permute-start.11 = (bf16[64,1152]{1,0:T(8,128)(2,1)S(1)}, bf16[64,1152]{1,0:T(8,128)(2,1)S(1)}, u32[]{:S(2)}, u32[]{:S(2)}) collective-permute-start(bf16[64,1152]{1,0:T(8,128)(2,1)S(1)} %add_convert_fusion.1), channel_id=1, source_target_pairs={{0,2},{1,3},{2,0},{3,1},{4,6},{5,7},{6,4},{7,5},{8,10},{9,11},{10,... | collective-permute-start | bytes 442376 | tf_op jit(solution)/shard_map/ppermute | solution.py:86
  163.3 3.1 %all-to-all-done.5 = bf16[16,16,1152]{2,1,0:T(8,128)(2,1)S(1)} async-done(((bf16[16,16,1152]{2,1,0:T(8,128)(2,1)}), bf16[16,16,1152]{2,1,0:T(8,128)(2,1)S(1)}, u32[]{:S(2)}, u32[]{:S(2)}) %all-to-all-start.5) | async-done | bytes 589856 | tf_op jit(solution)/shard_map/all_to_all | solution.py:302
  166.3 3.9 %convolution_convert_fusion.1 = bf16[256,1152]{1,0:T(8,128)(2,1)} fusion(bf16[256,1152]{1,0:T(8,128)(2,1)S(1)} %bitcast.46, bf16[1152,544]{1,0:T(8,128)(2,1)} %bitcast.11, f32[256,272]{0,1:T(8,128)S(1)} %copy-done.5), kind=kOutput, calls=%fused_computation.11 | convolution fusion | flops 322482176 | bytes 3227648 | tf_op jit(solution)/shard_map/dot_general | solution.py:57
  170.2 3.3 %collective-permute-done.11 = bf16[64,1152]{1,0:T(8,128)(2,1)S(1)} collective-permute-done((bf16[64,1152]{1,0:T(8,128)(2,1)S(1)}, bf16[64,1152]{1,0:T(8,128)(2,1)S(1)}, u32[]{:S(2)}, u32[]{:S(2)}) %collective-permute-start.11) | collective-permute-done | bytes 147488 | tf_op jit(solution)/shard_map/ppermute | solution.py:86
  173.4 7.4 %all-to-all-start.6 = ((bf16[16,16,1152]{2,1,0:T(8,128)(2,1)}), bf16[16,16,1152]{2,1,0:T(8,128)(2,1)S(1)}, u32[]{:S(2)}, u32[]{:S(2)}) async-start(bf16[16,16,1152]{2,1,0:T(8,128)(2,1)} %bitcast.47), calls=%async_computation.6 | async-start | bytes 1179648 | tf_op jit(solution)/shard_map/all_to_all | solution.py:73
  180.9 2.1 collective-permute-start.12
  182.9 9.6 %all-to-all-done.6 = bf16[16,16,1152]{2,1,0:T(8,128)(2,1)S(1)} async-done(((bf16[16,16,1152]{2,1,0:T(8,128)(2,1)}), bf16[16,16,1152]{2,1,0:T(8,128)(2,1)S(1)}, u32[]{:S(2)}, u32[]{:S(2)}) %all-to-all-start.6) | async-done | bytes 589856 | tf_op jit(solution)/shard_map/all_to_all | solution.py:73
  193.2 1.0 fusion.8
  194.9 0.8 broadcast_in_dim.22
  195.7 3.5 %all-to-all-start.7 = ((bf16[4,336,128]{2,1,0:T(8,128)(2,1)}), bf16[4,336,128]{2,1,0:T(8,128)(2,1)S(1)}, u32[]{:S(2)}, u32[]{:S(2)}) async-start(bf16[4,336,128]{2,1,0:T(8,128)(2,1)} %broadcast_in_dim.22), calls=%async_computation.7 | async-start | bytes 688128 | tf_op jit(solution)/shard_map/all_to_all | solution.py:67
  199.3 11.6 %all-to-all-done.7.last_ref = bf16[4,336,128]{2,1,0:T(8,128)(2,1)S(1)} async-done(((bf16[4,336,128]{2,1,0:T(8,128)(2,1)}), bf16[4,336,128]{2,1,0:T(8,128)(2,1)S(1)}, u32[]{:S(2)}, u32[]{:S(2)}) %all-to-all-start.7) | async-done | bytes 344096 | tf_op jit(solution)/shard_map/all_to_all | solution.py:67
  210.9 1.0 shard_map.160
  (103 shorter events, 8.5 us)
Async XLA Ops:
  0.6 23.7 %copy-start = (bf16[288,1152]{1,0:T(8,128)(2,1)S(1)}, bf16[288,1152]{1,0:T(8,128)(2,1)}, u32[]{:S(2)}) copy-start(bf16[288,1152]{1,0:T(8,128)(2,1)} %param.25) | copy-start | bytes 1990660
  2.5 14.4 %copy-start.7 = (f32[1152]{0:T(1024)S(1)}, f32[1152]{0:T(1024)}, u32[]{:S(2)}) copy-start(f32[1152]{0:T(1024)} %param.17) | copy-start | bytes 13828
  2.6 14.7 %copy-start.8 = (f32[1152]{0:T(1024)S(1)}, f32[1152]{0:T(1024)}, u32[]{:S(2)}) copy-start(f32[1152]{0:T(1024)} %param.18) | copy-start | bytes 13828
  2.6 15.1 %copy-start.6 = (f32[1152]{0:T(1024)S(1)}, f32[1152]{0:T(1024)}, u32[]{:S(2)}) copy-start(f32[1152]{0:T(1024)} %param.23) | copy-start | bytes 13828
  2.6 15.9 %copy-start.9 = (f32[1152]{0:T(1024)S(1)}, f32[1152]{0:T(1024)}, u32[]{:S(2)}) copy-start(f32[1152]{0:T(1024)} %param.26) | copy-start | bytes 13828
  3.9 21.7 %all-to-all-start = ((bf16[64,2,680]{2,1,0:T(2,128)(2,1)}), bf16[64,2,680]{2,1,0:T(2,128)(2,1)S(1)}, u32[]{:S(2)}, u32[]{:S(2)}) async-start(bf16[64,2,680]{2,1,0:T(2,128)(2,1)} %reshape.289), calls=%async_computation | async-start | bytes 393216 | tf_op jit(solution)/shard_map/all_to_all | solution.py:238
  24.3 1.8 copy-start.3
  25.6 13.2 %copy-start.1 = (bf16[1152,288]{0,1:T(8,128)(2,1)}, bf16[1152,288]{0,1:T(8,128)(2,1)S(1)}, u32[]{:S(2)}) copy-start(bf16[1152,288]{0,1:T(8,128)(2,1)S(1)} %fusion.6) | copy-start | bytes 1990660
  28.4 48.8 %all-to-all-start.1 = ((bf16[8,144,544]{2,1,0:T(8,128)(2,1)}), bf16[8,144,544]{2,1,0:T(8,128)(2,1)}, u32[]{:S(2)}, u32[]{:S(2)}) async-start(bf16[8,144,544]{2,1,0:T(8,128)(2,1)} %broadcast_in_dim.20), calls=%async_computation.1 | async-start | bytes 2949120 | tf_op jit(solution)/shard_map/all_to_all | solution.py:67
  39.2 29.1 %collective-permute-start = (bf16[64,1152]{1,0:T(8,128)(2,1)S(1)}, bf16[64,1152]{1,0:T(8,128)(2,1)S(1)}, u32[]{:S(2)}, u32[]{:S(2)}) collective-permute-start(bf16[64,1152]{1,0:T(8,128)(2,1)S(1)} %convolution_convert_fusion.3), channel_id=1, source_target_pairs={{0,1},{1,2},{2,3},{3,0},{4,5},{5,6},{6,7},{7,4},{8,9},{9,10},{10,1... | collective-permute-start | bytes 442376 | tf_op jit(solution)/shard_map/ppermute | solution.py:82
  43.6 24.6 %collective-permute-start.1 = (bf16[64,1152]{1,0:T(8,128)(2,1)S(1)}, bf16[64,1152]{1,0:T(8,128)(2,1)S(1)}, u32[]{:S(2)}, u32[]{:S(2)}) collective-permute-start(bf16[64,1152]{1,0:T(8,128)(2,1)S(1)} %convolution_convert_fusion.3), channel_id=1, source_target_pairs={{0,2},{1,3},{2,0},{3,1},{4,6},{5,7},{6,4},{7,5},{8,10},{9,11},{10,... | collective-permute-start | bytes 442376 | tf_op jit(solution)/shard_map/ppermute | solution.py:82
  49.0 19.3 %collective-permute-start.2 = (bf16[64,1152]{1,0:T(8,128)(2,1)S(1)}, bf16[64,1152]{1,0:T(8,128)(2,1)S(1)}, u32[]{:S(2)}, u32[]{:S(2)}) collective-permute-start(bf16[64,1152]{1,0:T(8,128)(2,1)S(1)} %convolution_convert_fusion.3), channel_id=1, source_target_pairs={{0,3},{1,0},{2,1},{3,2},{4,7},{5,4},{6,5},{7,6},{8,11},{9,8},{10,9... | collective-permute-start | bytes 442376 | tf_op jit(solution)/shard_map/ppermute | solution.py:82
  68.5 13.2 %collective-permute-start.3 = (bf16[64,1152]{1,0:T(8,128)(2,1)S(1)}, bf16[64,1152]{1,0:T(8,128)(2,1)S(1)}, u32[]{:S(2)}, u32[]{:S(2)}) collective-permute-start(bf16[64,1152]{1,0:T(8,128)(2,1)S(1)} %multiply_convert_fusion.2), channel_id=1, source_target_pairs={{0,128},{64,192},{128,0},{192,64},{1,129},{65,193},{129,1},{193,65... | collective-permute-start | bytes 442376 | tf_op jit(solution)/shard_map/ppermute | solution.py:82
  78.9 2.9 %copy-start.4 = (f32[256,272]{0,1:T(8,128)}, f32[256,272]{0,1:T(8,128)S(1)}, u32[]{:S(2)}) copy-start(f32[256,272]{0,1:T(8,128)S(1)} %convolution_add_fusion.1) | copy-start | bytes 835588
  78.9 14.4 %copy-start.10 = (f32[1152]{0:T(1024)S(1)}, f32[1152]{0:T(1024)}, u32[]{:S(2)}) copy-start(f32[1152]{0:T(1024)} %param.22) | copy-start | bytes 13828
  81.8 15.1 %all-to-all-start.2 = ((bf16[16,16,1152]{2,1,0:T(8,128)(2,1)}), bf16[16,16,1152]{2,1,0:T(8,128)(2,1)S(1)}, u32[]{:S(2)}, u32[]{:S(2)}) async-start(bf16[16,16,1152]{2,1,0:T(8,128)(2,1)} %bitcast.12), calls=%async_computation.2 | async-start | bytes 1179648 | tf_op jit(solution)/shard_map/all_to_all | solution.py:73
  87.5 11.5 %collective-permute-start.4 = (bf16[64,1152]{1,0:T(8,128)(2,1)S(1)}, bf16[64,1152]{1,0:T(8,128)(2,1)S(1)}, u32[]{:S(2)}, u32[]{:S(2)}) collective-permute-start(bf16[64,1152]{1,0:T(8,128)(2,1)S(1)} %multiply_convert_fusion.2), channel_id=1, source_target_pairs={{0,64},{64,128},{128,192},{192,0},{1,65},{65,129},{129,193},{193,1... | collective-permute-start | bytes 442376 | tf_op jit(solution)/shard_map/ppermute | solution.py:82
  89.5 9.5 %collective-permute-start.5 = (bf16[64,1152]{1,0:T(8,128)(2,1)S(1)}, bf16[64,1152]{1,0:T(8,128)(2,1)S(1)}, u32[]{:S(2)}, u32[]{:S(2)}) collective-permute-start(bf16[64,1152]{1,0:T(8,128)(2,1)S(1)} %multiply_convert_fusion.2), channel_id=1, source_target_pairs={{0,192},{64,0},{128,64},{192,128},{1,193},{65,1},{129,65},{193,129... | collective-permute-start | bytes 442376 | tf_op jit(solution)/shard_map/ppermute | solution.py:82
  100.1 22.0 %all-to-all-start.3 = ((bf16[16,16,1152]{2,1,0:T(8,128)(2,1)}), bf16[16,16,1152]{2,1,0:T(8,128)(2,1)S(1)}, u32[]{:S(2)}, u32[]{:S(2)}) async-start(bf16[16,16,1152]{2,1,0:T(8,128)(2,1)} %broadcast_in_dim.21), calls=%async_computation.3 | async-start | bytes 1179648 | tf_op jit(solution)/shard_map/all_to_all | solution.py:67
  103.8 4.1 %collective-permute-start.6 = (bf16[256,1152]{1,0:T(8,128)(2,1)S(1)}, bf16[256,1152]{1,0:T(8,128)(2,1)S(1)}, u32[]{:S(2)}, u32[]{:S(2)}) collective-permute-start(bf16[256,1152]{1,0:T(8,128)(2,1)S(1)} %constant_dynamic-update-slice_fusion.near_ref), channel_id=1, source_target_pairs={{0,4},{4,0},{1,5},{5,1},{2,6},{6,2},{3,7},{7,3},{8,12},{12,8},{9,1... | collective-permute-start | bytes 1769480 | tf_op jit(solution)/shard_map/ppermute | solution.py:82
  124.9 5.7 %collective-permute-start.7 = (bf16[256,1152]{1,0:T(8,128)(2,1)S(1)}, bf16[256,1152]{1,0:T(8,128)(2,1)}, u32[]{:S(2)}, u32[]{:S(2)}) collective-permute-start(bf16[256,1152]{1,0:T(8,128)(2,1)S(1)} %convolution_convert_fusion), channel_id=1, source_target_pairs={{0,4},{4,0},{1,5},{5,1},{2,6},{6,2},{3,7},{7,3},{8,12},{12,8},{9,1... | collective-permute-start | bytes 1769480 | tf_op jit(solution)/shard_map/ppermute | solution.py:82
  126.9 22.7 %all-to-all-start.4 = ((bf16[16,16,1152]{2,1,0:T(8,128)(2,1)}), bf16[16,16,1152]{2,1,0:T(8,128)(2,1)S(1)}, u32[]{:S(2)}, u32[]{:S(2)}) async-start(bf16[16,16,1152]{2,1,0:T(8,128)(2,1)} %bitcast.15), calls=%async_computation.4 | async-start | bytes 1179648 | tf_op jit(solution)/shard_map/all_to_all | solution.py:73
  132.2 34.2 %copy-start.5 = (f32[256,272]{0,1:T(8,128)S(1)}, f32[256,272]{0,1:T(8,128)}, u32[]{:S(2)}) copy-start(f32[256,272]{0,1:T(8,128)} %copy-done.4) | copy-start | bytes 835588
  132.2 10.1 %collective-permute-start.10 = (bf16[64,1152]{1,0:T(8,128)(2,1)S(1)}, bf16[64,1152]{1,0:T(8,128)(2,1)S(1)}, u32[]{:S(2)}, u32[]{:S(2)}) collective-permute-start(bf16[64,1152]{1,0:T(8,128)(2,1)S(1)} %get-tuple-element.78), channel_id=1, source_target_pairs={{0,64},{64,128},{128,192},{192,0},{1,65},{65,129},{129,193},{193,1... | collective-permute-start | bytes 442376 | tf_op jit(solution)/shard_map/ppermute | solution.py:82
  136.6 12.2 %collective-permute-start.8 = (bf16[64,1152]{1,0:T(8,128)(2,1)S(1)}, bf16[64,1152]{1,0:T(8,128)(2,1)S(1)}, u32[]{:S(2)}, u32[]{:S(2)}) collective-permute-start(bf16[64,1152]{1,0:T(8,128)(2,1)S(1)} %get-tuple-element.80), channel_id=1, source_target_pairs={{0,192},{64,0},{128,64},{192,128},{1,193},{65,1},{129,65},{193,129... | collective-permute-start | bytes 442376 | tf_op jit(solution)/shard_map/ppermute | solution.py:82
  138.5 10.3 %collective-permute-start.9 = (bf16[64,1152]{1,0:T(8,128)(2,1)S(1)}, bf16[64,1152]{1,0:T(8,128)(2,1)S(1)}, u32[]{:S(2)}, u32[]{:S(2)}) collective-permute-start(bf16[64,1152]{1,0:T(8,128)(2,1)S(1)} %get-tuple-element.79), channel_id=1, source_target_pairs={{0,128},{64,192},{128,0},{192,64},{1,129},{65,193},{129,1},{193,65... | collective-permute-start | bytes 442376 | tf_op jit(solution)/shard_map/ppermute | solution.py:82
  150.6 15.7 %all-to-all-start.5 = ((bf16[16,16,1152]{2,1,0:T(8,128)(2,1)}), bf16[16,16,1152]{2,1,0:T(8,128)(2,1)S(1)}, u32[]{:S(2)}, u32[]{:S(2)}) async-start(bf16[16,16,1152]{2,1,0:T(8,128)(2,1)} %get-tuple-element.61), calls=%async_computation.5 | async-start | bytes 1179648 | tf_op jit(solution)/shard_map/all_to_all | solution.py:302
  156.8 16.6 %collective-permute-start.11 = (bf16[64,1152]{1,0:T(8,128)(2,1)S(1)}, bf16[64,1152]{1,0:T(8,128)(2,1)S(1)}, u32[]{:S(2)}, u32[]{:S(2)}) collective-permute-start(bf16[64,1152]{1,0:T(8,128)(2,1)S(1)} %add_convert_fusion.1), channel_id=1, source_target_pairs={{0,2},{1,3},{2,0},{3,1},{4,6},{5,7},{6,4},{7,5},{8,10},{9,11},{10,... | collective-permute-start | bytes 442376 | tf_op jit(solution)/shard_map/ppermute | solution.py:86
  173.4 19.1 %all-to-all-start.6 = ((bf16[16,16,1152]{2,1,0:T(8,128)(2,1)}), bf16[16,16,1152]{2,1,0:T(8,128)(2,1)S(1)}, u32[]{:S(2)}, u32[]{:S(2)}) async-start(bf16[16,16,1152]{2,1,0:T(8,128)(2,1)} %bitcast.47), calls=%async_computation.6 | async-start | bytes 1179648 | tf_op jit(solution)/shard_map/all_to_all | solution.py:73
  180.9 13.6 %copy-start.2 = (bf16[1152,288]{0,1:T(8,128)(2,1)S(1)}, bf16[1152,288]{0,1:T(8,128)(2,1)}, u32[]{:S(2)}) copy-start(bf16[1152,288]{0,1:T(8,128)(2,1)} %copy-done.1) | copy-start | bytes 1990660
  180.9 12.1 %collective-permute-start.12 = (bf16[64,1152]{1,0:T(8,128)(2,1)S(1)}, bf16[64,1152]{1,0:T(8,128)(2,1)S(1)}, u32[]{:S(2)}, u32[]{:S(2)}) collective-permute-start(bf16[64,1152]{1,0:T(8,128)(2,1)S(1)} %add_convert_fusion), channel_id=1, source_target_pairs={{0,1},{1,0},{2,3},{3,2},{4,5},{5,4},{6,7},{7,6},{8,9},{9,8},{10,11... | collective-permute-start | bytes 442376 | tf_op jit(solution)/shard_map/ppermute | solution.py:86
  195.7 15.2 %all-to-all-start.7 = ((bf16[4,336,128]{2,1,0:T(8,128)(2,1)}), bf16[4,336,128]{2,1,0:T(8,128)(2,1)S(1)}, u32[]{:S(2)}, u32[]{:S(2)}) async-start(bf16[4,336,128]{2,1,0:T(8,128)(2,1)} %broadcast_in_dim.22), calls=%async_computation.7 | async-start | bytes 688128 | tf_op jit(solution)/shard_map/all_to_all | solution.py:67

commit v5 on v4

--- a/solution.py
+++ b/solution.py
@@ -229,9 +229,10 @@
         padded = jnp.pad(arr, ((0, 0), (0, chunk * group_count - hidden_local)))
         return padded.reshape(arr.shape[0], group_count, chunk)
 
-    bias_high = image_up_bias.astype(low)
-    bias_low = (image_up_bias - bias_high.astype(jnp.float32)).astype(low)
-    rows = jnp.concatenate([image_up, image_down.T, bias_high[None], bias_low[None]], axis=0)
+    bias_row = image_up_bias[None]
+    bias_high = bias_row.astype(low)
+    bias_low = (bias_row - bias_high.astype(jnp.float32)).astype(low)
+    rows = jnp.concatenate([image_up, image_down.T, bias_high, bias_low], axis=0)
     slots = cut(rows).transpose(1, 0, 2)
     slots = jnp.broadcast_to(slots[:, None], (group_count, tensor_count) + slots.shape[1:])
     slots = slots.reshape((group_count * tensor_count,) + slots.shape[2:])
@@ -271,11 +272,11 @@
     hidden_act, hidden_slope = gelu_parts(hidden_pre)
     image_part = mm_nt(hidden_act.astype(low), down_mine).astype(low)
     x_steps = range(1, lax.axis_size("x"))
-    image_part, text_emb, text_got = together(image_part, text_emb, passed(text_emb, "x", 2))
-    image_sum, text_near = together(
-        sum_slots(image_part, GROUP),
-        [text_emb, passed(text_emb, "x", 1), text_got, passed(text_emb, "x", 3)],
-    )
+    image_part, text_near = together(
+        image_part, [text_emb] + [passed(text_emb, "x", step) for step in (2, 1, 3)]
+    )
+    text_near = [text_near[0], text_near[2], text_near[1], text_near[3]]
+    image_sum = sum_slots(image_part, GROUP)
     text_near = jnp.concatenate(text_near, axis=0)
     image_sum = image_sum + image_own + turned(image_down_bias)
     image_unit, image_invnorm = unit_rows(image_sum)

time: 213 us -> 213 us (level)
    all_to_all x3, waiting for transfers between devices: 13.5 us -> 19.8 us  [swap_slots(): return lax.all_to_all(slots, axes, 0, 0, tiled=True)]
    all_to_all x3, waiting for transfers between devices: 31.2 us -> 25 us  [spread(): return lax.all_to_all(slots, axes, 0, 0, tiled=True)]
    all_to_all x1, waiting for transfers between devices: 3.05 us -> 8.92 us  [per_device(): back_all = lax.all_to_all(slots, GROUP, 0, 0, tiled=True).reshape(-1, width)]
    all_to_all x3, starting transfers between devices: 17.4 us -> 21.3 us  [spread(): return lax.all_to_all(slots, axes, 0, 0, tiled=True)]
    ppermute x2, waiting for transfers between devices: 3.69 us -> 0.01 us  [crossed(): lax.ppermute(block, axis, [(i, i ^ bits) for i in range(lax.axis_size(axi...]
    ppermute x2, starting transfers between devices: 8.45 us -> 5.94 us  [crossed(): lax.ppermute(block, axis, [(i, i ^ bits) for i in range(lax.axis_size(axi...]
  transfers between devices with their start and end apart: 21 -> 21, of which waited for: 11 -> 7; matrix products, arithmetic and copies ran while one was open for 8% -> 8% of each run, Pallas kernels for 0% -> 0%
where the time goes in v5:
time: 213 us; the launch traced here: 212 us
  starting transfers between devices  97.4 us (46%)
  waiting for transfers between devices  60.5 us (28%)
  blocking collectives  19.2 us (9%)
  matrix products  15 us (7%)
  local copies, waits for them, and re-layouts  8.32 us (4%)
  Pallas kernels  4.43 us (2%)
  other arithmetic  3.71 us (2%)
  between operations  3.26 us (2%)
    ppermute x11, starting transfers between devices, passed(): lax.ppermute(block, axis, [(i, (i + step) % count) for i in range(count)])  38.4 us
    all_to_all x3, waiting for transfers between devices, spread(): return lax.all_to_all(slots, axes, 0, 0, tiled=True)  25 us
    all_to_all x3, starting transfers between devices, spread(): return lax.all_to_all(slots, axes, 0, 0, tiled=True)  21.3 us
    all_to_all x3, waiting for transfers between devices, swap_slots(): return lax.all_to_all(slots, axes, 0, 0, tiled=True)  19.8 us
    all_to_all x3, starting transfers between devices, swap_slots(): return lax.all_to_all(slots, axes, 0, 0, tiled=True)  14.8 us
    all_gather x1, blocking collectives, per_device(): ready_all = lax.all_gather(ready_all, 'x', axis=0, tiled=True)  13.7 us
    all_to_all x1, starting transfers between devices, per_device(): got = lax.all_to_all(slots, GROUP + ('tensor',), 0, 0, tiled=True)  10.8 us
    all_to_all x1, waiting for transfers between devices, per_device(): back_all = lax.all_to_all(slots, GROUP, 0, 0, tiled=True).reshape(-1, width)  8.92 us
  transfers between devices with their start and end apart: 21, of which 7 were waited for; matrix products, arithmetic and copies ran while one was open for 8% of the time, Pallas kernels for 0%

profile of v5, /device:TPU:6, one launch (start us, length us, event | category | flops | bytes accessed | tf_op | source)
XLA Modules:
  0.0 211.8 jit_solution(1458766584926755785)
XLA Ops:
  0.6 0.8 subtract_convert_fusion
  1.4 0.8 fusion.52
  2.6 1.3 reshape.293
  3.9 10.8 %all-to-all-start = ((bf16[64,2,680]{2,1,0:T(2,128)(2,1)}), bf16[64,2,680]{2,1,0:T(2,128)(2,1)S(1)}, u32[]{:S(2)}, u32[]{:S(2)}) async-start(bf16[64,2,680]{2,1,0:T(2,128)(2,1)} %reshape.293), calls=%async_computation | async-start | bytes 393216 | tf_op jit(solution)/shard_map/all_to_all | solution.py:239
  14.8 1.9 fusion.78
  17.8 0.8 dynamic-slice.1
  18.8 5.5 %all_gather.6 = bf16[64,1152]{1,0:T(8,128)(2,1)S(1)} all-gather(bf16[16,1152]{1,0:T(8,128)(2,1)S(1)} %add_convert_fusion.3), channel_id=1, replica_groups=mesh['ylo'=2,'x'=4,'z'=8,'core'=2,'tensor'=4] {'ylo','core'}, dimensions={0}, use_global_device_ids=true | all-gather | bytes 184320 | tf_op jit(solution)/shard_map/all_gather | solution.py:245
  24.3 1.3 fusion.6
  25.6 0.5 reshape.294
  27.1 1.2 broadcast_in_dim.14
  28.4 10.3 %all-to-all-start.1 = ((bf16[8,144,544]{2,1,0:T(8,128)(2,1)}), bf16[8,144,544]{2,1,0:T(8,128)(2,1)}, u32[]{:S(2)}, u32[]{:S(2)}) async-start(bf16[8,144,544]{2,1,0:T(8,128)(2,1)} %broadcast_in_dim.14), calls=%async_computation.1 | async-start | bytes 2949120 | tf_op jit(solution)/shard_map/all_to_all | solution.py:67
  39.2 4.4 %collective-permute-start = (bf16[64,1152]{1,0:T(8,128)(2,1)S(1)}, bf16[64,1152]{1,0:T(8,128)(2,1)S(1)}, u32[]{:S(2)}, u32[]{:S(2)}) collective-permute-start(bf16[64,1152]{1,0:T(8,128)(2,1)S(1)} %convolution_convert_fusion.3), channel_id=1, source_target_pairs={{0,1},{1,2},{2,3},{3,0},{4,5},{5,6},{6,7},{7,4},{8,9},{9,10},{10,1... | collective-permute-start | bytes 442376 | tf_op jit(solution)/shard_map/ppermute | solution.py:82
  43.6 5.4 %collective-permute-start.1 = (bf16[64,1152]{1,0:T(8,128)(2,1)S(1)}, bf16[64,1152]{1,0:T(8,128)(2,1)S(1)}, u32[]{:S(2)}, u32[]{:S(2)}) collective-permute-start(bf16[64,1152]{1,0:T(8,128)(2,1)S(1)} %convolution_convert_fusion.3), channel_id=1, source_target_pairs={{0,2},{1,3},{2,0},{3,1},{4,6},{5,7},{6,4},{7,5},{8,10},{9,11},{10,... | collective-permute-start | bytes 442376 | tf_op jit(solution)/shard_map/ppermute | solution.py:82
  49.0 5.5 %collective-permute-start.2 = (bf16[64,1152]{1,0:T(8,128)(2,1)S(1)}, bf16[64,1152]{1,0:T(8,128)(2,1)S(1)}, u32[]{:S(2)}, u32[]{:S(2)}) collective-permute-start(bf16[64,1152]{1,0:T(8,128)(2,1)S(1)} %convolution_convert_fusion.3), channel_id=1, source_target_pairs={{0,3},{1,0},{2,1},{3,2},{4,7},{5,4},{6,5},{7,6},{8,11},{9,8},{10,9... | collective-permute-start | bytes 442376 | tf_op jit(solution)/shard_map/ppermute | solution.py:82
  54.5 13.7 %all_gather.7 = bf16[256,1152]{1,0:T(8,128)(2,1)S(1)} all-gather(bf16[64,1152]{1,0:T(8,128)(2,1)S(1)} %all_gather.6), channel_id=1, replica_groups=mesh['ylo'=2,'x'=4,'z'=8,'core'=2,'tensor'=4] {'x'}, dimensions={0}, use_global_device_ids=true | all-gather | bytes 737280 | tf_op jit(solution)/shard_map/all_gather | solution.py:247
  68.5 3.4 %collective-permute-start.3 = (bf16[64,1152]{1,0:T(8,128)(2,1)S(1)}, bf16[64,1152]{1,0:T(8,128)(2,1)S(1)}, u32[]{:S(2)}, u32[]{:S(2)}) collective-permute-start(bf16[64,1152]{1,0:T(8,128)(2,1)S(1)} %multiply_convert_fusion.2), channel_id=1, source_target_pairs={{0,128},{64,192},{128,0},{192,64},{1,129},{65,193},{129,1},{193,65... | collective-permute-start | bytes 442376 | tf_op jit(solution)/shard_map/ppermute | solution.py:82
  71.9 1.9 collective-permute-start.4
  73.9 3.9 %collective-permute-start.5 = (bf16[64,1152]{1,0:T(8,128)(2,1)S(1)}, bf16[64,1152]{1,0:T(8,128)(2,1)S(1)}, u32[]{:S(2)}, u32[]{:S(2)}) collective-permute-start(bf16[64,1152]{1,0:T(8,128)(2,1)S(1)} %multiply_convert_fusion.2), channel_id=1, source_target_pairs={{0,192},{64,0},{128,64},{192,128},{1,193},{65,1},{129,65},{193,129... | collective-permute-start | bytes 442376 | tf_op jit(solution)/shard_map/ppermute | solution.py:82
  77.8 1.6 convolution_add_fusion.1
  79.5 2.9 %convolution_convert_fusion.2 = bf16[256,1152]{1,0:T(8,128)(2,1)} fusion(bf16[1152,544]{1,0:T(8,128)(2,1)} %bitcast.11, f32[256,272]{0,1:T(8,128)S(1)} %convolution_add_fusion.1), kind=kOutput, calls=%fused_computation.12 | convolution fusion | flops 161353728 | bytes 1753088 | tf_op jit(solution)/shard_map/dot_general | solution.py:57
  82.4 5.1 %all-to-all-start.2 = ((bf16[16,16,1152]{2,1,0:T(8,128)(2,1)}), bf16[16,16,1152]{2,1,0:T(8,128)(2,1)S(1)}, u32[]{:S(2)}, u32[]{:S(2)}) async-start(bf16[16,16,1152]{2,1,0:T(8,128)(2,1)} %bitcast.12), calls=%async_computation.2 | async-start | bytes 1179648 | tf_op jit(solution)/shard_map/all_to_all | solution.py:73
  87.8 8.9 %all-to-all-done.2 = bf16[16,16,1152]{2,1,0:T(8,128)(2,1)S(1)} async-done(((bf16[16,16,1152]{2,1,0:T(8,128)(2,1)}), bf16[16,16,1152]{2,1,0:T(8,128)(2,1)S(1)}, u32[]{:S(2)}, u32[]{:S(2)}) %all-to-all-start.2) | async-done | bytes 589856 | tf_op jit(solution)/shard_map/all_to_all | solution.py:73
  97.1 0.9 broadcast_in_dim.15
  98.0 6.9 %all-to-all-start.3 = ((bf16[16,16,1152]{2,1,0:T(8,128)(2,1)}), bf16[16,16,1152]{2,1,0:T(8,128)(2,1)S(1)}, u32[]{:S(2)}, u32[]{:S(2)}) async-start(bf16[16,16,1152]{2,1,0:T(8,128)(2,1)} %broadcast_in_dim.15), calls=%async_computation.3 | async-start | bytes 1179648 | tf_op jit(solution)/shard_map/all_to_all | solution.py:67
  104.9 1.9 collective-permute-start.6
  109.0 14.3 %all-to-all-done.3 = bf16[16,16,1152]{2,1,0:T(8,128)(2,1)S(1)} async-done(((bf16[16,16,1152]{2,1,0:T(8,128)(2,1)}), bf16[16,16,1152]{2,1,0:T(8,128)(2,1)S(1)}, u32[]{:S(2)}, u32[]{:S(2)}) %all-to-all-start.3) | async-done | bytes 589856 | tf_op jit(solution)/shard_map/all_to_all | solution.py:67
  123.3 2.4 %shard_map.158 = (bf16[256,256]{1,0:T(8,128)(2,1)S(1)}, bf16[256,256]{1,0:T(8,128)(2,1)S(1)}, bf16[256,1152]{1,0:T(8,128)(2,1)}) custom-call(f32[3]{0:T(128)S(1)} %pad_maximum_fusion.1.number_ref, s32[3]{0:T(128)S(1)} %pad_add_fusion.place_ref, bf16[256,1152]{1,0:T(8,128)(2,1)S(1)} %bitcast.38, ...), custom_call_target="tpu_custom_call" | custom-call | tf_op jit(solution)/shard_map/pallas_call | solution.py:179
  126.1 1.9 collective-permute-start.7
  128.0 3.8 %all-to-all-start.4 = ((bf16[16,16,1152]{2,1,0:T(8,128)(2,1)}), bf16[16,16,1152]{2,1,0:T(8,128)(2,1)S(1)}, u32[]{:S(2)}, u32[]{:S(2)}) async-start(bf16[16,16,1152]{2,1,0:T(8,128)(2,1)} %bitcast.15), calls=%async_computation.4 | async-start | bytes 1179648 | tf_op jit(solution)/shard_map/all_to_all | solution.py:73
  131.8 1.4 fusion.7
  133.3 4.7 %collective-permute-start.10 = (bf16[64,1152]{1,0:T(8,128)(2,1)S(1)}, bf16[64,1152]{1,0:T(8,128)(2,1)S(1)}, u32[]{:S(2)}, u32[]{:S(2)}) collective-permute-start(bf16[64,1152]{1,0:T(8,128)(2,1)S(1)} %get-tuple-element.72), channel_id=1, source_target_pairs={{0,64},{64,128},{128,192},{192,0},{1,65},{65,129},{129,193},{193,1... | collective-permute-start | bytes 442376 | tf_op jit(solution)/shard_map/ppermute | solution.py:82
  138.0 1.9 collective-permute-start.8
  139.9 3.5 %collective-permute-start.9 = (bf16[64,1152]{1,0:T(8,128)(2,1)S(1)}, bf16[64,1152]{1,0:T(8,128)(2,1)S(1)}, u32[]{:S(2)}, u32[]{:S(2)}) collective-permute-start(bf16[64,1152]{1,0:T(8,128)(2,1)S(1)} %get-tuple-element.73), channel_id=1, source_target_pairs={{0,128},{64,192},{128,0},{192,64},{1,129},{65,193},{129,1},{193,65... | collective-permute-start | bytes 442376 | tf_op jit(solution)/shard_map/ppermute | solution.py:82
  143.6 6.7 %collective-permute-done.8 = bf16[64,1152]{1,0:T(8,128)(2,1)S(1)} collective-permute-done((bf16[64,1152]{1,0:T(8,128)(2,1)S(1)}, bf16[64,1152]{1,0:T(8,128)(2,1)S(1)}, u32[]{:S(2)}, u32[]{:S(2)}) %collective-permute-start.8) | collective-permute-done | bytes 147488 | tf_op jit(solution)/shard_map/ppermute | solution.py:82
  150.3 0.5 all-to-all-done.4.got_ref
  150.8 1.1 shard_map.159
  151.8 6.2 %all-to-all-start.5 = ((bf16[16,16,1152]{2,1,0:T(8,128)(2,1)}), bf16[16,16,1152]{2,1,0:T(8,128)(2,1)S(1)}, u32[]{:S(2)}, u32[]{:S(2)}) async-start(bf16[16,16,1152]{2,1,0:T(8,128)(2,1)} %get-tuple-element.55), calls=%async_computation.5 | async-start | bytes 1179648 | tf_op jit(solution)/shard_map/all_to_all | solution.py:303
  158.1 3.9 %collective-permute-start.11 = (bf16[64,1152]{1,0:T(8,128)(2,1)S(1)}, bf16[64,1152]{1,0:T(8,128)(2,1)S(1)}, u32[]{:S(2)}, u32[]{:S(2)}) collective-permute-start(bf16[64,1152]{1,0:T(8,128)(2,1)S(1)} %add_convert_fusion.1), channel_id=1, source_target_pairs={{0,2},{1,3},{2,0},{3,1},{4,6},{5,7},{6,4},{7,5},{8,10},{9,11},{10,... | collective-permute-start | bytes 442376 | tf_op jit(solution)/shard_map/ppermute | solution.py:86
  162.0 8.9 %all-to-all-done.5 = bf16[16,16,1152]{2,1,0:T(8,128)(2,1)S(1)} async-done(((bf16[16,16,1152]{2,1,0:T(8,128)(2,1)}), bf16[16,16,1152]{2,1,0:T(8,128)(2,1)S(1)}, u32[]{:S(2)}, u32[]{:S(2)}) %all-to-all-start.5) | async-done | bytes 589856 | tf_op jit(solution)/shard_map/all_to_all | solution.py:303
  170.9 3.9 %convolution_convert_fusion.1 = bf16[256,1152]{1,0:T(8,128)(2,1)} fusion(bf16[256,1152]{1,0:T(8,128)(2,1)S(1)} %bitcast.46, bf16[1152,544]{1,0:T(8,128)(2,1)} %bitcast.11, f32[256,272]{0,1:T(8,128)S(1)} %copy-done.5), kind=kOutput, calls=%fused_computation.11 | convolution fusion | flops 322482176 | bytes 3227648 | tf_op jit(solution)/shard_map/dot_general | solution.py:57
  174.8 5.9 %all-to-all-start.6 = ((bf16[16,16,1152]{2,1,0:T(8,128)(2,1)}), bf16[16,16,1152]{2,1,0:T(8,128)(2,1)S(1)}, u32[]{:S(2)}, u32[]{:S(2)}) async-start(bf16[16,16,1152]{2,1,0:T(8,128)(2,1)} %bitcast.47), calls=%async_computation.6 | async-start | bytes 1179648 | tf_op jit(solution)/shard_map/all_to_all | solution.py:73
  180.7 2.1 collective-permute-start.12
  182.8 10.3 %all-to-all-done.6 = bf16[16,16,1152]{2,1,0:T(8,128)(2,1)S(1)} async-done(((bf16[16,16,1152]{2,1,0:T(8,128)(2,1)}), bf16[16,16,1152]{2,1,0:T(8,128)(2,1)S(1)}, u32[]{:S(2)}, u32[]{:S(2)}) %all-to-all-start.6) | async-done | bytes 589856 | tf_op jit(solution)/shard_map/all_to_all | solution.py:73
  193.4 1.0 fusion.8
  195.1 0.8 broadcast_in_dim.16
  195.9 4.1 %all-to-all-start.7 = ((bf16[4,336,128]{2,1,0:T(8,128)(2,1)}), bf16[4,336,128]{2,1,0:T(8,128)(2,1)S(1)}, u32[]{:S(2)}, u32[]{:S(2)}) async-start(bf16[4,336,128]{2,1,0:T(8,128)(2,1)} %broadcast_in_dim.16), calls=%async_computation.7 | async-start | bytes 688128 | tf_op jit(solution)/shard_map/all_to_all | solution.py:67
  200.1 10.7 %all-to-all-done.7.last_ref = bf16[4,336,128]{2,1,0:T(8,128)(2,1)S(1)} async-done(((bf16[4,336,128]{2,1,0:T(8,128)(2,1)}), bf16[4,336,128]{2,1,0:T(8,128)(2,1)S(1)}, u32[]{:S(2)}, u32[]{:S(2)}) %all-to-all-start.7) | async-done | bytes 344096 | tf_op jit(solution)/shard_map/all_to_all | solution.py:67
  210.8 1.0 shard_map.160
  (103 shorter events, 6.0 us)
Async XLA Ops:
  0.6 23.7 %copy-start = (bf16[288,1152]{1,0:T(8,128)(2,1)S(1)}, bf16[288,1152]{1,0:T(8,128)(2,1)}, u32[]{:S(2)}) copy-start(bf16[288,1152]{1,0:T(8,128)(2,1)} %param.25) | copy-start | bytes 1990660
  2.5 14.4 %copy-start.7 = (f32[1152]{0:T(1024)S(1)}, f32[1152]{0:T(1024)}, u32[]{:S(2)}) copy-start(f32[1152]{0:T(1024)} %param.17) | copy-start | bytes 13828
  2.6 14.7 %copy-start.8 = (f32[1152]{0:T(1024)S(1)}, f32[1152]{0:T(1024)}, u32[]{:S(2)}) copy-start(f32[1152]{0:T(1024)} %param.18) | copy-start | bytes 13828
  2.6 15.1 %copy-start.6 = (f32[1152]{0:T(1024)S(1)}, f32[1152]{0:T(1024)}, u32[]{:S(2)}) copy-start(f32[1152]{0:T(1024)} %param.23) | copy-start | bytes 13828
  2.6 15.9 %copy-start.9 = (f32[1152]{0:T(1024)S(1)}, f32[1152]{0:T(1024)}, u32[]{:S(2)}) copy-start(f32[1152]{0:T(1024)} %param.26) | copy-start | bytes 13828
  3.9 21.7 %all-to-all-start = ((bf16[64,2,680]{2,1,0:T(2,128)(2,1)}), bf16[64,2,680]{2,1,0:T(2,128)(2,1)S(1)}, u32[]{:S(2)}, u32[]{:S(2)}) async-start(bf16[64,2,680]{2,1,0:T(2,128)(2,1)} %reshape.293), calls=%async_computation | async-start | bytes 393216 | tf_op jit(solution)/shard_map/all_to_all | solution.py:239
  24.3 1.8 copy-start.3
  25.6 13.2 %copy-start.1 = (bf16[1152,288]{0,1:T(8,128)(2,1)}, bf16[1152,288]{0,1:T(8,128)(2,1)S(1)}, u32[]{:S(2)}) copy-start(bf16[1152,288]{0,1:T(8,128)(2,1)S(1)} %fusion.6) | copy-start | bytes 1990660
  28.4 49.4 %all-to-all-start.1 = ((bf16[8,144,544]{2,1,0:T(8,128)(2,1)}), bf16[8,144,544]{2,1,0:T(8,128)(2,1)}, u32[]{:S(2)}, u32[]{:S(2)}) async-start(bf16[8,144,544]{2,1,0:T(8,128)(2,1)} %broadcast_in_dim.14), calls=%async_computation.1 | async-start | bytes 2949120 | tf_op jit(solution)/shard_map/all_to_all | solution.py:67
  39.2 29.1 %collective-permute-start = (bf16[64,1152]{1,0:T(8,128)(2,1)S(1)}, bf16[64,1152]{1,0:T(8,128)(2,1)S(1)}, u32[]{:S(2)}, u32[]{:S(2)}) collective-permute-start(bf16[64,1152]{1,0:T(8,128)(2,1)S(1)} %convolution_convert_fusion.3), channel_id=1, source_target_pairs={{0,1},{1,2},{2,3},{3,0},{4,5},{5,6},{6,7},{7,4},{8,9},{9,10},{10,1... | collective-permute-start | bytes 442376 | tf_op jit(solution)/shard_map/ppermute | solution.py:82
  43.6 24.6 %collective-permute-start.1 = (bf16[64,1152]{1,0:T(8,128)(2,1)S(1)}, bf16[64,1152]{1,0:T(8,128)(2,1)S(1)}, u32[]{:S(2)}, u32[]{:S(2)}) collective-permute-start(bf16[64,1152]{1,0:T(8,128)(2,1)S(1)} %convolution_convert_fusion.3), channel_id=1, source_target_pairs={{0,2},{1,3},{2,0},{3,1},{4,6},{5,7},{6,4},{7,5},{8,10},{9,11},{10,... | collective-permute-start | bytes 442376 | tf_op jit(solution)/shard_map/ppermute | solution.py:82
  49.0 19.3 %collective-permute-start.2 = (bf16[64,1152]{1,0:T(8,128)(2,1)S(1)}, bf16[64,1152]{1,0:T(8,128)(2,1)S(1)}, u32[]{:S(2)}, u32[]{:S(2)}) collective-permute-start(bf16[64,1152]{1,0:T(8,128)(2,1)S(1)} %convolution_convert_fusion.3), channel_id=1, source_target_pairs={{0,3},{1,0},{2,1},{3,2},{4,7},{5,4},{6,5},{7,6},{8,11},{9,8},{10,9... | collective-permute-start | bytes 442376 | tf_op jit(solution)/shard_map/ppermute | solution.py:82
  68.5 13.8 %collective-permute-start.3 = (bf16[64,1152]{1,0:T(8,128)(2,1)S(1)}, bf16[64,1152]{1,0:T(8,128)(2,1)S(1)}, u32[]{:S(2)}, u32[]{:S(2)}) collective-permute-start(bf16[64,1152]{1,0:T(8,128)(2,1)S(1)} %multiply_convert_fusion.2), channel_id=1, source_target_pairs={{0,128},{64,192},{128,0},{192,64},{1,129},{65,193},{129,1},{193,65... | collective-permute-start | bytes 442376 | tf_op jit(solution)/shard_map/ppermute | solution.py:82
  71.9 10.4 %collective-permute-start.4 = (bf16[64,1152]{1,0:T(8,128)(2,1)S(1)}, bf16[64,1152]{1,0:T(8,128)(2,1)S(1)}, u32[]{:S(2)}, u32[]{:S(2)}) collective-permute-start(bf16[64,1152]{1,0:T(8,128)(2,1)S(1)} %multiply_convert_fusion.2), channel_id=1, source_target_pairs={{0,64},{64,128},{128,192},{192,0},{1,65},{65,129},{129,193},{193,1... | collective-permute-start | bytes 442376 | tf_op jit(solution)/shard_map/ppermute | solution.py:82
  73.9 8.5 %collective-permute-start.5 = (bf16[64,1152]{1,0:T(8,128)(2,1)S(1)}, bf16[64,1152]{1,0:T(8,128)(2,1)S(1)}, u32[]{:S(2)}, u32[]{:S(2)}) collective-permute-start(bf16[64,1152]{1,0:T(8,128)(2,1)S(1)} %multiply_convert_fusion.2), channel_id=1, source_target_pairs={{0,192},{64,0},{128,64},{192,128},{1,193},{65,1},{129,65},{193,129... | collective-permute-start | bytes 442376 | tf_op jit(solution)/shard_map/ppermute | solution.py:82
  79.4 2.9 %copy-start.4 = (f32[256,272]{0,1:T(8,128)}, f32[256,272]{0,1:T(8,128)S(1)}, u32[]{:S(2)}) copy-start(f32[256,272]{0,1:T(8,128)S(1)} %convolution_add_fusion.1) | copy-start | bytes 835588
  79.4 8.0 %copy-start.10 = (f32[1152]{0:T(1024)S(1)}, f32[1152]{0:T(1024)}, u32[]{:S(2)}) copy-start(f32[1152]{0:T(1024)} %param.22) | copy-start | bytes 13828
  82.4 14.4 %all-to-all-start.2 = ((bf16[16,16,1152]{2,1,0:T(8,128)(2,1)}), bf16[16,16,1152]{2,1,0:T(8,128)(2,1)S(1)}, u32[]{:S(2)}, u32[]{:S(2)}) async-start(bf16[16,16,1152]{2,1,0:T(8,128)(2,1)} %bitcast.12), calls=%async_computation.2 | async-start | bytes 1179648 | tf_op jit(solution)/shard_map/all_to_all | solution.py:73
  98.0 25.3 %all-to-all-start.3 = ((bf16[16,16,1152]{2,1,0:T(8,128)(2,1)}), bf16[16,16,1152]{2,1,0:T(8,128)(2,1)S(1)}, u32[]{:S(2)}, u32[]{:S(2)}) async-start(bf16[16,16,1152]{2,1,0:T(8,128)(2,1)} %broadcast_in_dim.15), calls=%async_computation.3 | async-start | bytes 1179648 | tf_op jit(solution)/shard_map/all_to_all | solution.py:67
  104.9 4.1 %collective-permute-start.6 = (bf16[256,1152]{1,0:T(8,128)(2,1)S(1)}, bf16[256,1152]{1,0:T(8,128)(2,1)S(1)}, u32[]{:S(2)}, u32[]{:S(2)}) collective-permute-start(bf16[256,1152]{1,0:T(8,128)(2,1)S(1)} %constant_dynamic-update-slice_fusion.near_ref), channel_id=1, source_target_pairs={{0,4},{4,0},{1,5},{5,1},{2,6},{6,2},{3,7},{7,3},{8,12},{12,8},{9,1... | collective-permute-start | bytes 1769480 | tf_op jit(solution)/shard_map/ppermute | solution.py:82
  126.1 5.7 %collective-permute-start.7 = (bf16[256,1152]{1,0:T(8,128)(2,1)S(1)}, bf16[256,1152]{1,0:T(8,128)(2,1)}, u32[]{:S(2)}, u32[]{:S(2)}) collective-permute-start(bf16[256,1152]{1,0:T(8,128)(2,1)S(1)} %convolution_convert_fusion), channel_id=1, source_target_pairs={{0,4},{4,0},{1,5},{5,1},{2,6},{6,2},{3,7},{7,3},{8,12},{12,8},{9,1... | collective-permute-start | bytes 1769480 | tf_op jit(solution)/shard_map/ppermute | solution.py:82
  128.0 22.8 %all-to-all-start.4 = ((bf16[16,16,1152]{2,1,0:T(8,128)(2,1)}), bf16[16,16,1152]{2,1,0:T(8,128)(2,1)S(1)}, u32[]{:S(2)}, u32[]{:S(2)}) async-start(bf16[16,16,1152]{2,1,0:T(8,128)(2,1)} %bitcast.15), calls=%async_computation.4 | async-start | bytes 1179648 | tf_op jit(solution)/shard_map/all_to_all | solution.py:73
  133.3 37.6 %copy-start.5 = (f32[256,272]{0,1:T(8,128)S(1)}, f32[256,272]{0,1:T(8,128)}, u32[]{:S(2)}) copy-start(f32[256,272]{0,1:T(8,128)} %copy-done.4) | copy-start | bytes 835588
  133.3 10.2 %collective-permute-start.10 = (bf16[64,1152]{1,0:T(8,128)(2,1)S(1)}, bf16[64,1152]{1,0:T(8,128)(2,1)S(1)}, u32[]{:S(2)}, u32[]{:S(2)}) collective-permute-start(bf16[64,1152]{1,0:T(8,128)(2,1)S(1)} %get-tuple-element.72), channel_id=1, source_target_pairs={{0,64},{64,128},{128,192},{192,0},{1,65},{65,129},{129,193},{193,1... | collective-permute-start | bytes 442376 | tf_op jit(solution)/shard_map/ppermute | solution.py:82
  138.0 12.2 %collective-permute-start.8 = (bf16[64,1152]{1,0:T(8,128)(2,1)S(1)}, bf16[64,1152]{1,0:T(8,128)(2,1)S(1)}, u32[]{:S(2)}, u32[]{:S(2)}) collective-permute-start(bf16[64,1152]{1,0:T(8,128)(2,1)S(1)} %get-tuple-element.74), channel_id=1, source_target_pairs={{0,192},{64,0},{128,64},{192,128},{1,193},{65,1},{129,65},{193,129... | collective-permute-start | bytes 442376 | tf_op jit(solution)/shard_map/ppermute | solution.py:82
  139.9 10.3 %collective-permute-start.9 = (bf16[64,1152]{1,0:T(8,128)(2,1)S(1)}, bf16[64,1152]{1,0:T(8,128)(2,1)S(1)}, u32[]{:S(2)}, u32[]{:S(2)}) collective-permute-start(bf16[64,1152]{1,0:T(8,128)(2,1)S(1)} %get-tuple-element.73), channel_id=1, source_target_pairs={{0,128},{64,192},{128,0},{192,64},{1,129},{65,193},{129,1},{193,65... | collective-permute-start | bytes 442376 | tf_op jit(solution)/shard_map/ppermute | solution.py:82
  151.8 19.1 %all-to-all-start.5 = ((bf16[16,16,1152]{2,1,0:T(8,128)(2,1)}), bf16[16,16,1152]{2,1,0:T(8,128)(2,1)S(1)}, u32[]{:S(2)}, u32[]{:S(2)}) async-start(bf16[16,16,1152]{2,1,0:T(8,128)(2,1)} %get-tuple-element.55), calls=%async_computation.5 | async-start | bytes 1179648 | tf_op jit(solution)/shard_map/all_to_all | solution.py:303
  158.1 16.7 %collective-permute-start.11 = (bf16[64,1152]{1,0:T(8,128)(2,1)S(1)}, bf16[64,1152]{1,0:T(8,128)(2,1)S(1)}, u32[]{:S(2)}, u32[]{:S(2)}) collective-permute-start(bf16[64,1152]{1,0:T(8,128)(2,1)S(1)} %add_convert_fusion.1), channel_id=1, source_target_pairs={{0,2},{1,3},{2,0},{3,1},{4,6},{5,7},{6,4},{7,5},{8,10},{9,11},{10,... | collective-permute-start | bytes 442376 | tf_op jit(solution)/shard_map/ppermute | solution.py:86
  174.8 18.3 %all-to-all-start.6 = ((bf16[16,16,1152]{2,1,0:T(8,128)(2,1)}), bf16[16,16,1152]{2,1,0:T(8,128)(2,1)S(1)}, u32[]{:S(2)}, u32[]{:S(2)}) async-start(bf16[16,16,1152]{2,1,0:T(8,128)(2,1)} %bitcast.47), calls=%async_computation.6 | async-start | bytes 1179648 | tf_op jit(solution)/shard_map/all_to_all | solution.py:73
  180.7 14.0 %copy-start.2 = (bf16[1152,288]{0,1:T(8,128)(2,1)S(1)}, bf16[1152,288]{0,1:T(8,128)(2,1)}, u32[]{:S(2)}) copy-start(bf16[1152,288]{0,1:T(8,128)(2,1)} %copy-done.1) | copy-start | bytes 1990660
  180.7 12.5 %collective-permute-start.12 = (bf16[64,1152]{1,0:T(8,128)(2,1)S(1)}, bf16[64,1152]{1,0:T(8,128)(2,1)S(1)}, u32[]{:S(2)}, u32[]{:S(2)}) collective-permute-start(bf16[64,1152]{1,0:T(8,128)(2,1)S(1)} %add_convert_fusion), channel_id=1, source_target_pairs={{0,1},{1,0},{2,3},{3,2},{4,5},{5,4},{6,7},{7,6},{8,9},{9,8},{10,11... | collective-permute-start | bytes 442376 | tf_op jit(solution)/shard_map/ppermute | solution.py:86
  195.9 14.9 %all-to-all-start.7 = ((bf16[4,336,128]{2,1,0:T(8,128)(2,1)}), bf16[4,336,128]{2,1,0:T(8,128)(2,1)S(1)}, u32[]{:S(2)}, u32[]{:S(2)}) async-start(bf16[4,336,128]{2,1,0:T(8,128)(2,1)} %broadcast_in_dim.16), calls=%async_computation.7 | async-start | bytes 688128 | tf_op jit(solution)/shard_map/all_to_all | solution.py:67

commit v6 on v5

--- a/solution.py
+++ b/solution.py
@@ -269,19 +269,21 @@
     down_mine = weights[:, hidden_mine:]
 
     hidden_pre = mm(ready_all, up_mine) + up_bias
-    hidden_act, hidden_slope = gelu_parts(hidden_pre)
+    hidden_act = gelu_parts(hidden_pre)[0]
     image_part = mm_nt(hidden_act.astype(low), down_mine).astype(low)
     x_steps = range(1, lax.axis_size("x"))
     image_part, text_near = together(
         image_part, [text_emb] + [passed(text_emb, "x", step) for step in (2, 1, 3)]
     )
     text_near = [text_near[0], text_near[2], text_near[1], text_near[3]]
-    image_sum = sum_slots(image_part, GROUP)
+    image_sum, hidden_pre = together(sum_slots(image_part, GROUP), hidden_pre)
     text_near = jnp.concatenate(text_near, axis=0)
     image_sum = image_sum + image_own + turned(image_down_bias)
     image_unit, image_invnorm = unit_rows(image_sum)
-    image_all, text_far = together(
-        spread(image_unit.astype(low), IMAGES).reshape(-1, width), passed(text_near, "core", 1)
+    image_all, text_far, hidden_slope = together(
+        spread(image_unit.astype(low), IMAGES).reshape(-1, width),
+        passed(text_near, "core", 1),
+        gelu_parts(hidden_pre)[1],
     )
 
     scale_value = jnp.exp(log_scale[0])

time: 213 us -> 215 us (level)
  other arithmetic: 3.71 us -> 6.47 us
  waiting for transfers between devices: 60.5 us -> 58 us
  transfers between devices with their start and end apart: 21 -> 21, of which waited for: 7 -> 8; matrix products, arithmetic and copies ran while one was open for 8% -> 9% of each run, Pallas kernels for 0% -> 0%
where the time goes in v6:
time: 215 us; the launch traced here: 213 us
  starting transfers between devices  97.9 us (46%)
  waiting for transfers between devices  58 us (27%)
  blocking collectives  19.2 us (9%)
  matrix products  14.9 us (7%)
  local copies, waits for them, and re-layouts  9.01 us (4%)
  other arithmetic  6.47 us (3%)
  Pallas kernels  4.42 us (2%)
  between operations  3.23 us (2%)
    ppermute x11, starting transfers between devices, passed(): lax.ppermute(block, axis, [(i, (i + step) % count) for i in range(count)])  39 us
    all_to_all x3, waiting for transfers between devices, spread(): return lax.all_to_all(slots, axes, 0, 0, tiled=True)  23.8 us
    all_to_all x3, starting transfers between devices, spread(): return lax.all_to_all(slots, axes, 0, 0, tiled=True)  21.6 us
    all_to_all x3, waiting for transfers between devices, swap_slots(): return lax.all_to_all(slots, axes, 0, 0, tiled=True)  21.4 us
    all_to_all x3, starting transfers between devices, swap_slots(): return lax.all_to_all(slots, axes, 0, 0, tiled=True)  14.6 us
    all_gather x1, blocking collectives, per_device(): ready_all = lax.all_gather(ready_all, 'x', axis=0, tiled=True)  13.7 us
    all_to_all x1, starting transfers between devices, per_device(): got = lax.all_to_all(slots, GROUP + ('tensor',), 0, 0, tiled=True)  10.8 us
    dot_general x4, matrix products, mm_nt(): lax.dot_general(a, b, (((1,), (1,)), ((), ())), preferred_element_type=jn...  8.03 us
  transfers between devices with their start and end apart: 21, of which 8 were waited for; matrix products, arithmetic and copies ran while one was open for 9% of the time, Pallas kernels for 0%

profile of v6, /device:TPU:6, one launch (start us, length us, event | category | flops | bytes accessed | tf_op | source)
XLA Modules:
  0.0 213.2 jit_solution(16729893252182355521)
XLA Ops:
  1.5 0.8 fusion.47
  2.6 1.3 reshape.293
  3.9 10.8 %all-to-all-start = ((bf16[64,2,680]{2,1,0:T(2,128)(2,1)}), bf16[64,2,680]{2,1,0:T(2,128)(2,1)S(1)}, u32[]{:S(2)}, u32[]{:S(2)}) async-start(bf16[64,2,680]{2,1,0:T(2,128)(2,1)} %reshape.293), calls=%async_computation | async-start | bytes 393216 | tf_op jit(solution)/shard_map/all_to_all | solution.py:239
  15.5 1.9 fusion.68
  18.8 5.5 %all_gather.6 = bf16[64,1152]{1,0:T(8,128)(2,1)S(1)} all-gather(bf16[16,1152]{1,0:T(8,128)(2,1)S(1)} %add_convert_fusion.3), channel_id=1, replica_groups=mesh['ylo'=2,'x'=4,'z'=8,'core'=2,'tensor'=4] {'ylo','core'}, dimensions={0}, use_global_device_ids=true | all-gather | bytes 184320 | tf_op jit(solution)/shard_map/all_gather | solution.py:245
  24.3 1.3 fusion.6
  26.8 1.2 broadcast_in_dim.14
  28.0 10.4 %all-to-all-start.1 = ((bf16[8,144,544]{2,1,0:T(8,128)(2,1)}), bf16[8,144,544]{2,1,0:T(8,128)(2,1)}, u32[]{:S(2)}, u32[]{:S(2)}) async-start(bf16[8,144,544]{2,1,0:T(8,128)(2,1)} %broadcast_in_dim.14), calls=%async_computation.1 | async-start | bytes 2949120 | tf_op jit(solution)/shard_map/all_to_all | solution.py:67
  39.3 4.4 %collective-permute-start = (bf16[64,1152]{1,0:T(8,128)(2,1)S(1)}, bf16[64,1152]{1,0:T(8,128)(2,1)S(1)}, u32[]{:S(2)}, u32[]{:S(2)}) collective-permute-start(bf16[64,1152]{1,0:T(8,128)(2,1)S(1)} %convolution_convert_fusion.3), channel_id=1, source_target_pairs={{0,1},{1,2},{2,3},{3,0},{4,5},{5,6},{6,7},{7,4},{8,9},{9,10},{10,1... | collective-permute-start | bytes 442376 | tf_op jit(solution)/shard_map/ppermute | solution.py:82
  43.7 5.4 %collective-permute-start.1 = (bf16[64,1152]{1,0:T(8,128)(2,1)S(1)}, bf16[64,1152]{1,0:T(8,128)(2,1)S(1)}, u32[]{:S(2)}, u32[]{:S(2)}) collective-permute-start(bf16[64,1152]{1,0:T(8,128)(2,1)S(1)} %convolution_convert_fusion.3), channel_id=1, source_target_pairs={{0,2},{1,3},{2,0},{3,1},{4,6},{5,7},{6,4},{7,5},{8,10},{9,11},{10,... | collective-permute-start | bytes 442376 | tf_op jit(solution)/shard_map/ppermute | solution.py:82
  49.1 5.5 %collective-permute-start.2 = (bf16[64,1152]{1,0:T(8,128)(2,1)S(1)}, bf16[64,1152]{1,0:T(8,128)(2,1)S(1)}, u32[]{:S(2)}, u32[]{:S(2)}) collective-permute-start(bf16[64,1152]{1,0:T(8,128)(2,1)S(1)} %convolution_convert_fusion.3), channel_id=1, source_target_pairs={{0,3},{1,0},{2,1},{3,2},{4,7},{5,4},{6,5},{7,6},{8,11},{9,8},{10,9... | collective-permute-start | bytes 442376 | tf_op jit(solution)/shard_map/ppermute | solution.py:82
  54.7 13.7 %all_gather.7 = bf16[256,1152]{1,0:T(8,128)(2,1)S(1)} all-gather(bf16[64,1152]{1,0:T(8,128)(2,1)S(1)} %all_gather.6), channel_id=1, replica_groups=mesh['ylo'=2,'x'=4,'z'=8,'core'=2,'tensor'=4] {'x'}, dimensions={0}, use_global_device_ids=true | all-gather | bytes 737280 | tf_op jit(solution)/shard_map/all_gather | solution.py:247
  68.7 3.4 %collective-permute-start.3 = (bf16[64,1152]{1,0:T(8,128)(2,1)S(1)}, bf16[64,1152]{1,0:T(8,128)(2,1)S(1)}, u32[]{:S(2)}, u32[]{:S(2)}) collective-permute-start(bf16[64,1152]{1,0:T(8,128)(2,1)S(1)} %multiply_convert_fusion.2), channel_id=1, source_target_pairs={{0,128},{64,192},{128,0},{192,64},{1,129},{65,193},{129,1},{193,65... | collective-permute-start | bytes 442376 | tf_op jit(solution)/shard_map/ppermute | solution.py:82
  72.0 1.9 collective-permute-start.4
  74.0 3.9 %collective-permute-start.5 = (bf16[64,1152]{1,0:T(8,128)(2,1)S(1)}, bf16[64,1152]{1,0:T(8,128)(2,1)S(1)}, u32[]{:S(2)}, u32[]{:S(2)}) collective-permute-start(bf16[64,1152]{1,0:T(8,128)(2,1)S(1)} %multiply_convert_fusion.2), channel_id=1, source_target_pairs={{0,192},{64,0},{128,64},{192,128},{1,193},{65,1},{129,65},{193,129... | collective-permute-start | bytes 442376 | tf_op jit(solution)/shard_map/ppermute | solution.py:82
  77.9 1.6 convolution_add_fusion.1
  80.3 2.8 %convolution_convert_fusion.2 = bf16[256,1152]{1,0:T(8,128)(2,1)} fusion(bf16[1152,544]{1,0:T(8,128)(2,1)} %bitcast.11, f32[256,272]{0,1:T(8,128)S(1)} %convolution_add_fusion.1), kind=kOutput, calls=%fused_computation.12 | convolution fusion | flops 161353728 | bytes 1753088 | tf_op jit(solution)/shard_map/dot_general | solution.py:57
  83.1 4.8 %all-to-all-start.2 = ((bf16[16,16,1152]{2,1,0:T(8,128)(2,1)}), bf16[16,16,1152]{2,1,0:T(8,128)(2,1)S(1)}, u32[]{:S(2)}, u32[]{:S(2)}) async-start(bf16[16,16,1152]{2,1,0:T(8,128)(2,1)} %bitcast.12), calls=%async_computation.2 | async-start | bytes 1179648 | tf_op jit(solution)/shard_map/all_to_all | solution.py:73
  88.2 8.9 %all-to-all-done.2 = bf16[16,16,1152]{2,1,0:T(8,128)(2,1)S(1)} async-done(((bf16[16,16,1152]{2,1,0:T(8,128)(2,1)}), bf16[16,16,1152]{2,1,0:T(8,128)(2,1)S(1)}, u32[]{:S(2)}, u32[]{:S(2)}) %all-to-all-start.2) | async-done | bytes 589856 | tf_op jit(solution)/shard_map/all_to_all | solution.py:73
  97.4 0.9 broadcast_in_dim.15
  98.3 7.2 %all-to-all-start.3 = ((bf16[16,16,1152]{2,1,0:T(8,128)(2,1)}), bf16[16,16,1152]{2,1,0:T(8,128)(2,1)S(1)}, u32[]{:S(2)}, u32[]{:S(2)}) async-start(bf16[16,16,1152]{2,1,0:T(8,128)(2,1)} %broadcast_in_dim.15), calls=%async_computation.3 | async-start | bytes 1179648 | tf_op jit(solution)/shard_map/all_to_all | solution.py:67
  105.6 1.9 collective-permute-start.6
  109.7 1.8 fusion.27
  111.5 12.5 %all-to-all-done.3 = bf16[16,16,1152]{2,1,0:T(8,128)(2,1)S(1)} async-done(((bf16[16,16,1152]{2,1,0:T(8,128)(2,1)}), bf16[16,16,1152]{2,1,0:T(8,128)(2,1)S(1)}, u32[]{:S(2)}, u32[]{:S(2)}) %all-to-all-start.3) | async-done | bytes 589856 | tf_op jit(solution)/shard_map/all_to_all | solution.py:67
  124.0 2.4 %shard_map.158 = (bf16[256,256]{1,0:T(8,128)(2,1)S(1)}, bf16[256,256]{1,0:T(8,128)(2,1)S(1)}, bf16[256,1152]{1,0:T(8,128)(2,1)}) custom-call(f32[3]{0:T(128)S(1)} %pad_maximum_fusion.1.number_ref, s32[3]{0:T(128)S(1)} %pad_add_fusion.place_ref, bf16[256,1152]{1,0:T(8,128)(2,1)S(1)} %bitcast.38, ...), custom_call_target="tpu_custom_call" | custom-call | tf_op jit(solution)/shard_map/pallas_call | solution.py:179
  126.8 1.9 collective-permute-start.7
  128.7 3.8 %all-to-all-start.4 = ((bf16[16,16,1152]{2,1,0:T(8,128)(2,1)}), bf16[16,16,1152]{2,1,0:T(8,128)(2,1)S(1)}, u32[]{:S(2)}, u32[]{:S(2)}) async-start(bf16[16,16,1152]{2,1,0:T(8,128)(2,1)} %bitcast.15), calls=%async_computation.4 | async-start | bytes 1179648 | tf_op jit(solution)/shard_map/all_to_all | solution.py:73
  132.5 1.4 fusion.7
  134.0 2.8 %collective-permute-start.8 = (bf16[64,1152]{1,0:T(8,128)(2,1)S(1)}, bf16[64,1152]{1,0:T(8,128)(2,1)S(1)}, u32[]{:S(2)}, u32[]{:S(2)}) collective-permute-start(bf16[64,1152]{1,0:T(8,128)(2,1)S(1)} %get-tuple-element.80), channel_id=1, source_target_pairs={{0,192},{64,0},{128,64},{192,128},{1,193},{65,1},{129,65},{193,129... | collective-permute-start | bytes 442376 | tf_op jit(solution)/shard_map/ppermute | solution.py:82
  136.8 5.3 %collective-permute-start.9 = (bf16[64,1152]{1,0:T(8,128)(2,1)S(1)}, bf16[64,1152]{1,0:T(8,128)(2,1)S(1)}, u32[]{:S(2)}, u32[]{:S(2)}) collective-permute-start(bf16[64,1152]{1,0:T(8,128)(2,1)S(1)} %get-tuple-element.79), channel_id=1, source_target_pairs={{0,128},{64,192},{128,0},{192,64},{1,129},{65,193},{129,1},{193,65... | collective-permute-start | bytes 442376 | tf_op jit(solution)/shard_map/ppermute | solution.py:82
  142.1 2.7 %collective-permute-start.10 = (bf16[64,1152]{1,0:T(8,128)(2,1)S(1)}, bf16[64,1152]{1,0:T(8,128)(2,1)S(1)}, u32[]{:S(2)}, u32[]{:S(2)}) collective-permute-start(bf16[64,1152]{1,0:T(8,128)(2,1)S(1)} %get-tuple-element.78), channel_id=1, source_target_pairs={{0,64},{64,128},{128,192},{192,0},{1,65},{65,129},{129,193},{193,1... | collective-permute-start | bytes 442376 | tf_op jit(solution)/shard_map/ppermute | solution.py:82
  144.8 2.7 %collective-permute-done.9 = bf16[64,1152]{1,0:T(8,128)(2,1)S(1)} collective-permute-done((bf16[64,1152]{1,0:T(8,128)(2,1)S(1)}, bf16[64,1152]{1,0:T(8,128)(2,1)S(1)}, u32[]{:S(2)}, u32[]{:S(2)}) %collective-permute-start.9) | collective-permute-done | bytes 147488 | tf_op jit(solution)/shard_map/ppermute | solution.py:82
  147.5 2.1 %collective-permute-done.10 = bf16[64,1152]{1,0:T(8,128)(2,1)S(1)} collective-permute-done((bf16[64,1152]{1,0:T(8,128)(2,1)S(1)}, bf16[64,1152]{1,0:T(8,128)(2,1)S(1)}, u32[]{:S(2)}, u32[]{:S(2)}) %collective-permute-start.10) | collective-permute-done | bytes 147488 | tf_op jit(solution)/shard_map/ppermute | solution.py:82
  149.7 2.0 all-to-all-done.4.got_ref
  151.7 1.0 shard_map.159
  152.7 6.1 %all-to-all-start.5 = ((bf16[16,16,1152]{2,1,0:T(8,128)(2,1)}), bf16[16,16,1152]{2,1,0:T(8,128)(2,1)S(1)}, u32[]{:S(2)}, u32[]{:S(2)}) async-start(bf16[16,16,1152]{2,1,0:T(8,128)(2,1)} %get-tuple-element.60), calls=%async_computation.5 | async-start | bytes 1179648 | tf_op jit(solution)/shard_map/all_to_all | solution.py:305
  158.8 1.0 add_convert_fusion.1
  159.8 3.9 %collective-permute-start.11 = (bf16[64,1152]{1,0:T(8,128)(2,1)S(1)}, bf16[64,1152]{1,0:T(8,128)(2,1)S(1)}, u32[]{:S(2)}, u32[]{:S(2)}) collective-permute-start(bf16[64,1152]{1,0:T(8,128)(2,1)S(1)} %add_convert_fusion.1), channel_id=1, source_target_pairs={{0,2},{1,3},{2,0},{3,1},{4,6},{5,7},{6,4},{7,5},{8,10},{9,11},{10,... | collective-permute-start | bytes 442376 | tf_op jit(solution)/shard_map/ppermute | solution.py:86
  163.7 8.0 %all-to-all-done.5 = bf16[16,16,1152]{2,1,0:T(8,128)(2,1)S(1)} async-done(((bf16[16,16,1152]{2,1,0:T(8,128)(2,1)}), bf16[16,16,1152]{2,1,0:T(8,128)(2,1)S(1)}, u32[]{:S(2)}, u32[]{:S(2)}) %all-to-all-start.5) | async-done | bytes 589856 | tf_op jit(solution)/shard_map/all_to_all | solution.py:305
  171.7 3.9 %convolution_convert_fusion.1 = bf16[256,1152]{1,0:T(8,128)(2,1)} fusion(bf16[1152,544]{1,0:T(8,128)(2,1)} %bitcast.11, f32[256,272]{0,1:T(8,128)S(1)} %copy-done.5, bf16[256,1152]{1,0:T(8,128)(2,1)S(1)} %bitcast.46), kind=kOutput, calls=%fused_computation.11 | convolution fusion | flops 321298432 | bytes 3227648 | tf_op jit(solution)/shard_map/dot_general | solution.py:57
  175.6 6.0 %all-to-all-start.6 = ((bf16[16,16,1152]{2,1,0:T(8,128)(2,1)}), bf16[16,16,1152]{2,1,0:T(8,128)(2,1)S(1)}, u32[]{:S(2)}, u32[]{:S(2)}) async-start(bf16[16,16,1152]{2,1,0:T(8,128)(2,1)} %bitcast.18), calls=%async_computation.6 | async-start | bytes 1179648 | tf_op jit(solution)/shard_map/all_to_all | solution.py:73
  181.7 1.9 collective-permute-start.12
  183.6 10.5 %all-to-all-done.6 = bf16[16,16,1152]{2,1,0:T(8,128)(2,1)S(1)} async-done(((bf16[16,16,1152]{2,1,0:T(8,128)(2,1)}), bf16[16,16,1152]{2,1,0:T(8,128)(2,1)S(1)}, u32[]{:S(2)}, u32[]{:S(2)}) %all-to-all-start.6) | async-done | bytes 589856 | tf_op jit(solution)/shard_map/all_to_all | solution.py:73
  195.0 1.0 fusion.8
  196.1 0.8 broadcast_in_dim.16
  196.8 4.0 %all-to-all-start.7 = ((bf16[4,336,128]{2,1,0:T(8,128)(2,1)}), bf16[4,336,128]{2,1,0:T(8,128)(2,1)S(1)}, u32[]{:S(2)}, u32[]{:S(2)}) async-start(bf16[4,336,128]{2,1,0:T(8,128)(2,1)} %broadcast_in_dim.16), calls=%async_computation.7 | async-start | bytes 688128 | tf_op jit(solution)/shard_map/all_to_all | solution.py:67
  200.9 11.3 %all-to-all-done.7.last_ref = bf16[4,336,128]{2,1,0:T(8,128)(2,1)S(1)} async-done(((bf16[4,336,128]{2,1,0:T(8,128)(2,1)}), bf16[4,336,128]{2,1,0:T(8,128)(2,1)S(1)}, u32[]{:S(2)}, u32[]{:S(2)}) %all-to-all-start.7) | async-done | bytes 344096 | tf_op jit(solution)/shard_map/all_to_all | solution.py:67
  212.2 1.0 shard_map.160
  (106 shorter events, 8.7 us)
Async XLA Ops:
  0.6 23.7 %copy-start = (bf16[288,1152]{1,0:T(8,128)(2,1)S(1)}, bf16[288,1152]{1,0:T(8,128)(2,1)}, u32[]{:S(2)}) copy-start(bf16[288,1152]{1,0:T(8,128)(2,1)} %param.25) | copy-start | bytes 1990660
  0.6 14.2 %copy-start.8 = (f32[1152]{0:T(1024)S(1)}, f32[1152]{0:T(1024)}, u32[]{:S(2)}) copy-start(f32[1152]{0:T(1024)} %param.18) | copy-start | bytes 13828
  0.7 14.5 %copy-start.9 = (f32[1152]{0:T(1024)S(1)}, f32[1152]{0:T(1024)}, u32[]{:S(2)}) copy-start(f32[1152]{0:T(1024)} %param.17) | copy-start | bytes 13828
  2.6 15.9 %copy-start.7 = (f32[1152]{0:T(1024)S(1)}, f32[1152]{0:T(1024)}, u32[]{:S(2)}) copy-start(f32[1152]{0:T(1024)} %param.23) | copy-start | bytes 13828
  2.6 15.9 %copy-start.10 = (f32[1152]{0:T(1024)S(1)}, f32[1152]{0:T(1024)}, u32[]{:S(2)}) copy-start(f32[1152]{0:T(1024)} %param.26) | copy-start | bytes 13828
  3.9 21.7 %all-to-all-start = ((bf16[64,2,680]{2,1,0:T(2,128)(2,1)}), bf16[64,2,680]{2,1,0:T(2,128)(2,1)S(1)}, u32[]{:S(2)}, u32[]{:S(2)}) async-start(bf16[64,2,680]{2,1,0:T(2,128)(2,1)} %reshape.293), calls=%async_computation | async-start | bytes 393216 | tf_op jit(solution)/shard_map/all_to_all | solution.py:239
  25.6 13.4 %copy-start.1 = (bf16[1152,288]{0,1:T(8,128)(2,1)}, bf16[1152,288]{0,1:T(8,128)(2,1)S(1)}, u32[]{:S(2)}) copy-start(bf16[1152,288]{0,1:T(8,128)(2,1)S(1)} %fusion.6) | copy-start | bytes 1990660
  28.0 10.4 %copy-start.3 = (bf16[64,1152]{1,0:T(8,128)(2,1)S(1)}, bf16[64,1152]{1,0:T(8,128)(2,1)}, u32[]{:S(2)}) copy-start(bf16[64,1152]{1,0:T(8,128)(2,1)} %param.16) | copy-start | bytes 442372
  28.0 49.9 %all-to-all-start.1 = ((bf16[8,144,544]{2,1,0:T(8,128)(2,1)}), bf16[8,144,544]{2,1,0:T(8,128)(2,1)}, u32[]{:S(2)}, u32[]{:S(2)}) async-start(bf16[8,144,544]{2,1,0:T(8,128)(2,1)} %broadcast_in_dim.14), calls=%async_computation.1 | async-start | bytes 2949120 | tf_op jit(solution)/shard_map/all_to_all | solution.py:67
  39.3 29.1 %collective-permute-start = (bf16[64,1152]{1,0:T(8,128)(2,1)S(1)}, bf16[64,1152]{1,0:T(8,128)(2,1)S(1)}, u32[]{:S(2)}, u32[]{:S(2)}) collective-permute-start(bf16[64,1152]{1,0:T(8,128)(2,1)S(1)} %convolution_convert_fusion.3), channel_id=1, source_target_pairs={{0,1},{1,2},{2,3},{3,0},{4,5},{5,6},{6,7},{7,4},{8,9},{9,10},{10,1... | collective-permute-start | bytes 442376 | tf_op jit(solution)/shard_map/ppermute | solution.py:82
  43.7 24.6 %collective-permute-start.1 = (bf16[64,1152]{1,0:T(8,128)(2,1)S(1)}, bf16[64,1152]{1,0:T(8,128)(2,1)S(1)}, u32[]{:S(2)}, u32[]{:S(2)}) collective-permute-start(bf16[64,1152]{1,0:T(8,128)(2,1)S(1)} %convolution_convert_fusion.3), channel_id=1, source_target_pairs={{0,2},{1,3},{2,0},{3,1},{4,6},{5,7},{6,4},{7,5},{8,10},{9,11},{10,... | collective-permute-start | bytes 442376 | tf_op jit(solution)/shard_map/ppermute | solution.py:82
  49.1 19.3 %collective-permute-start.2 = (bf16[64,1152]{1,0:T(8,128)(2,1)S(1)}, bf16[64,1152]{1,0:T(8,128)(2,1)S(1)}, u32[]{:S(2)}, u32[]{:S(2)}) collective-permute-start(bf16[64,1152]{1,0:T(8,128)(2,1)S(1)} %convolution_convert_fusion.3), channel_id=1, source_target_pairs={{0,3},{1,0},{2,1},{3,2},{4,7},{5,4},{6,5},{7,6},{8,11},{9,8},{10,9... | collective-permute-start | bytes 442376 | tf_op jit(solution)/shard_map/ppermute | solution.py:82
  68.7 14.4 %collective-permute-start.3 = (bf16[64,1152]{1,0:T(8,128)(2,1)S(1)}, bf16[64,1152]{1,0:T(8,128)(2,1)S(1)}, u32[]{:S(2)}, u32[]{:S(2)}) collective-permute-start(bf16[64,1152]{1,0:T(8,128)(2,1)S(1)} %multiply_convert_fusion.2), channel_id=1, source_target_pairs={{0,128},{64,192},{128,0},{192,64},{1,129},{65,193},{129,1},{193,65... | collective-permute-start | bytes 442376 | tf_op jit(solution)/shard_map/ppermute | solution.py:82
  72.0 11.0 %collective-permute-start.4 = (bf16[64,1152]{1,0:T(8,128)(2,1)S(1)}, bf16[64,1152]{1,0:T(8,128)(2,1)S(1)}, u32[]{:S(2)}, u32[]{:S(2)}) collective-permute-start(bf16[64,1152]{1,0:T(8,128)(2,1)S(1)} %multiply_convert_fusion.2), channel_id=1, source_target_pairs={{0,64},{64,128},{128,192},{192,0},{1,65},{65,129},{129,193},{193,1... | collective-permute-start | bytes 442376 | tf_op jit(solution)/shard_map/ppermute | solution.py:82
  74.0 9.1 %collective-permute-start.5 = (bf16[64,1152]{1,0:T(8,128)(2,1)S(1)}, bf16[64,1152]{1,0:T(8,128)(2,1)S(1)}, u32[]{:S(2)}, u32[]{:S(2)}) collective-permute-start(bf16[64,1152]{1,0:T(8,128)(2,1)S(1)} %multiply_convert_fusion.2), channel_id=1, source_target_pairs={{0,192},{64,0},{128,64},{192,128},{1,193},{65,1},{129,65},{193,129... | collective-permute-start | bytes 442376 | tf_op jit(solution)/shard_map/ppermute | solution.py:82
  79.6 0.7 copy-start.4
  80.3 7.6 %copy-start.11 = (f32[1152]{0:T(1024)S(1)}, f32[1152]{0:T(1024)}, u32[]{:S(2)}) copy-start(f32[1152]{0:T(1024)} %param.22) | copy-start | bytes 13828
  83.1 14.0 %all-to-all-start.2 = ((bf16[16,16,1152]{2,1,0:T(8,128)(2,1)}), bf16[16,16,1152]{2,1,0:T(8,128)(2,1)S(1)}, u32[]{:S(2)}, u32[]{:S(2)}) async-start(bf16[16,16,1152]{2,1,0:T(8,128)(2,1)} %bitcast.12), calls=%async_computation.2 | async-start | bytes 1179648 | tf_op jit(solution)/shard_map/all_to_all | solution.py:73
  98.3 25.7 %all-to-all-start.3 = ((bf16[16,16,1152]{2,1,0:T(8,128)(2,1)}), bf16[16,16,1152]{2,1,0:T(8,128)(2,1)S(1)}, u32[]{:S(2)}, u32[]{:S(2)}) async-start(bf16[16,16,1152]{2,1,0:T(8,128)(2,1)} %broadcast_in_dim.15), calls=%async_computation.3 | async-start | bytes 1179648 | tf_op jit(solution)/shard_map/all_to_all | solution.py:67
  105.6 5.9 %collective-permute-start.6 = (bf16[256,1152]{1,0:T(8,128)(2,1)S(1)}, bf16[256,1152]{1,0:T(8,128)(2,1)S(1)}, u32[]{:S(2)}, u32[]{:S(2)}) collective-permute-start(bf16[256,1152]{1,0:T(8,128)(2,1)S(1)} %constant_dynamic-update-slice_fusion.near_ref), channel_id=1, source_target_pairs={{0,4},{4,0},{1,5},{5,1},{2,6},{6,2},{3,7},{7,3},{8,12},{12,8},{9,1... | collective-permute-start | bytes 1769480 | tf_op jit(solution)/shard_map/ppermute | solution.py:82
  126.8 5.7 %collective-permute-start.7 = (bf16[256,1152]{1,0:T(8,128)(2,1)S(1)}, bf16[256,1152]{1,0:T(8,128)(2,1)}, u32[]{:S(2)}, u32[]{:S(2)}) collective-permute-start(bf16[256,1152]{1,0:T(8,128)(2,1)S(1)} %convolution_convert_fusion), channel_id=1, source_target_pairs={{0,4},{4,0},{1,5},{5,1},{2,6},{6,2},{3,7},{7,3},{8,12},{12,8},{9,1... | collective-permute-start | bytes 1769480 | tf_op jit(solution)/shard_map/ppermute | solution.py:82
  128.7 23.0 %all-to-all-start.4 = ((bf16[16,16,1152]{2,1,0:T(8,128)(2,1)}), bf16[16,16,1152]{2,1,0:T(8,128)(2,1)S(1)}, u32[]{:S(2)}, u32[]{:S(2)}) async-start(bf16[16,16,1152]{2,1,0:T(8,128)(2,1)} %bitcast.15), calls=%async_computation.4 | async-start | bytes 1179648 | tf_op jit(solution)/shard_map/all_to_all | solution.py:73
  134.0 37.7 %copy-start.5 = (f32[256,272]{0,1:T(8,128)S(1)}, f32[256,272]{0,1:T(8,128)}, u32[]{:S(2)}) copy-start(f32[256,272]{0,1:T(8,128)} %fusion.27) | copy-start | bytes 835588
  134.0 10.8 %collective-permute-start.8 = (bf16[64,1152]{1,0:T(8,128)(2,1)S(1)}, bf16[64,1152]{1,0:T(8,128)(2,1)S(1)}, u32[]{:S(2)}, u32[]{:S(2)}) collective-permute-start(bf16[64,1152]{1,0:T(8,128)(2,1)S(1)} %get-tuple-element.80), channel_id=1, source_target_pairs={{0,192},{64,0},{128,64},{192,128},{1,193},{65,1},{129,65},{193,129... | collective-permute-start | bytes 442376 | tf_op jit(solution)/shard_map/ppermute | solution.py:82
  136.8 10.8 %collective-permute-start.9 = (bf16[64,1152]{1,0:T(8,128)(2,1)S(1)}, bf16[64,1152]{1,0:T(8,128)(2,1)S(1)}, u32[]{:S(2)}, u32[]{:S(2)}) collective-permute-start(bf16[64,1152]{1,0:T(8,128)(2,1)S(1)} %get-tuple-element.79), channel_id=1, source_target_pairs={{0,128},{64,192},{128,0},{192,64},{1,129},{65,193},{129,1},{193,65... | collective-permute-start | bytes 442376 | tf_op jit(solution)/shard_map/ppermute | solution.py:82
  142.1 7.6 %collective-permute-start.10 = (bf16[64,1152]{1,0:T(8,128)(2,1)S(1)}, bf16[64,1152]{1,0:T(8,128)(2,1)S(1)}, u32[]{:S(2)}, u32[]{:S(2)}) collective-permute-start(bf16[64,1152]{1,0:T(8,128)(2,1)S(1)} %get-tuple-element.78), channel_id=1, source_target_pairs={{0,64},{64,128},{128,192},{192,0},{1,65},{65,129},{129,193},{193,1... | collective-permute-start | bytes 442376 | tf_op jit(solution)/shard_map/ppermute | solution.py:82
  149.7 3.1 %copy-start.6 = (bf16[64,1152]{1,0:T(8,128)(2,1)}, bf16[64,1152]{1,0:T(8,128)(2,1)S(1)}, u32[]{:S(2)}) copy-start(bf16[64,1152]{1,0:T(8,128)(2,1)S(1)} %collective-permute-done.10) | copy-start | bytes 442372
  152.7 19.0 %all-to-all-start.5 = ((bf16[16,16,1152]{2,1,0:T(8,128)(2,1)}), bf16[16,16,1152]{2,1,0:T(8,128)(2,1)S(1)}, u32[]{:S(2)}, u32[]{:S(2)}) async-start(bf16[16,16,1152]{2,1,0:T(8,128)(2,1)} %get-tuple-element.60), calls=%async_computation.5 | async-start | bytes 1179648 | tf_op jit(solution)/shard_map/all_to_all | solution.py:305
  159.8 15.8 %collective-permute-start.11 = (bf16[64,1152]{1,0:T(8,128)(2,1)S(1)}, bf16[64,1152]{1,0:T(8,128)(2,1)S(1)}, u32[]{:S(2)}, u32[]{:S(2)}) collective-permute-start(bf16[64,1152]{1,0:T(8,128)(2,1)S(1)} %add_convert_fusion.1), channel_id=1, source_target_pairs={{0,2},{1,3},{2,0},{3,1},{4,6},{5,7},{6,4},{7,5},{8,10},{9,11},{10,... | collective-permute-start | bytes 442376 | tf_op jit(solution)/shard_map/ppermute | solution.py:86
  175.6 18.8 %copy-start.2 = (bf16[1152,288]{0,1:T(8,128)(2,1)S(1)}, bf16[1152,288]{0,1:T(8,128)(2,1)}, u32[]{:S(2)}) copy-start(bf16[1152,288]{0,1:T(8,128)(2,1)} %copy-done.1) | copy-start | bytes 1990660
  175.6 18.5 %all-to-all-start.6 = ((bf16[16,16,1152]{2,1,0:T(8,128)(2,1)}), bf16[16,16,1152]{2,1,0:T(8,128)(2,1)S(1)}, u32[]{:S(2)}, u32[]{:S(2)}) async-start(bf16[16,16,1152]{2,1,0:T(8,128)(2,1)} %bitcast.18), calls=%async_computation.6 | async-start | bytes 1179648 | tf_op jit(solution)/shard_map/all_to_all | solution.py:73
  181.7 12.5 %collective-permute-start.12 = (bf16[64,1152]{1,0:T(8,128)(2,1)S(1)}, bf16[64,1152]{1,0:T(8,128)(2,1)S(1)}, u32[]{:S(2)}, u32[]{:S(2)}) collective-permute-start(bf16[64,1152]{1,0:T(8,128)(2,1)S(1)} %add_convert_fusion), channel_id=1, source_target_pairs={{0,1},{1,0},{2,3},{3,2},{4,5},{5,4},{6,7},{7,6},{8,9},{9,8},{10,11... | collective-permute-start | bytes 442376 | tf_op jit(solution)/shard_map/ppermute | solution.py:86
  196.8 15.4 %all-to-all-start.7 = ((bf16[4,336,128]{2,1,0:T(8,128)(2,1)}), bf16[4,336,128]{2,1,0:T(8,128)(2,1)S(1)}, u32[]{:S(2)}, u32[]{:S(2)}) async-start(bf16[4,336,128]{2,1,0:T(8,128)(2,1)} %broadcast_in_dim.16), calls=%async_computation.7 | async-start | bytes 688128 | tf_op jit(solution)/shard_map/all_to_all | solution.py:67
